TPU v7x, 32 devices: a whole 2x2x4 slice. The times are simulated.
32 devices in a mesh: row: 4 (over y, x), col: 8 (over z, core).
Axes of the slice: x: 2, y: 2, z: 4, core: 2. Of those that a mesh axis runs over, the one named last changes fastest.
Arguments:
- queries: bfloat16 [4096, 2048], P(('row', 'col')), may hold values from -6 to 6
- keys: bfloat16 [4096, 2048], P(('row', 'col')), may hold values from -6 to 6
- values: bfloat16 [4096, 2048], P(('row', 'col')), may hold values from -6 to 6
- grad_out: bfloat16 [4096, 2048], P(('row', 'col')), may hold values from -6 to 6
- conv_weight: float32 [4, 2048], replicated, may hold values from -3 to 3
Outputs:
- grad_queries: bfloat16 [4096, 2048], P(('row', 'col'))
- grad_keys: bfloat16 [4096, 2048], P(('row', 'col'))
- grad_values: bfloat16 [4096, 2048], P(('row', 'col'))
- grad_weight: float32 [4, 2048], replicated
All inputs are finite; a program needn't handle non-finite values.
Results may differ from a plain program's by a relative error of at most 0.025.
Values may be sent and summed in bfloat16 or wider, within the bound.
No kernel may reach another device: no remote copies, remote signals or barrier semaphores. Data moves between devices by JAX's collectives and lax.ppermute only.
A program may use at most 192 MiB of HBM per device.

v0:
```python
import jax
import jax.numpy as jnp
from jax import lax
from jax.sharding import PartitionSpec as P

HEADS = 16
DH = 128
CW = 4


def shifted(value, axis, by):
    devices = lax.axis_size(axis)
    pairs = [(i, i + by) for i in range(devices) if 0 <= i + by < devices]
    return lax.ppermute(value, axis, pairs)


def entering(value, axis, join, neutral, backward):
    count = lax.axis_size(axis)
    place = lax.axis_index(axis)
    ahead = count - 1 - place if backward else place
    gathered = lax.all_gather(value.astype(jnp.bfloat16), axis)
    state = jnp.zeros_like(value) + jnp.asarray(neutral, value.dtype)

    def one(lap, state):
        source = count - 1 - lap if backward else lap
        return join(state, lax.dynamic_index_in_dim(gathered, source, 0, False).astype(value.dtype))

    return lax.fori_loop(0, ahead, one, state)


def add_states(earlier, later):
    return earlier + later


def local(queries, keys, values, grad_out, conv_weight):
    rows, width = queries.shape
    total = rows * lax.axis_size("row") * lax.axis_size("col")
    scale = (DH * total) ** (-0.5)
    before = shifted(values[rows - (CW - 1) :], ("row", "col"), 1)
    value_ext = jnp.concatenate([before, values], axis=0).astype(jnp.float32)
    conv_acc = jnp.zeros((rows, width), jnp.float32)
    for offset in range(CW):
        conv_acc = (
            conv_acc
            + conv_weight[offset][None, :] * value_ext[CW - 1 - offset : CW - 1 - offset + rows]
        )
    conved = conv_acc.astype(jnp.bfloat16)
    query_heads = queries.reshape(rows, HEADS, DH)
    key_heads = keys.reshape(rows, HEADS, DH)
    conv_heads = conved.reshape(rows, HEADS, DH)
    grad_heads = grad_out.reshape(rows, HEADS, DH)
    key_state = jnp.einsum(
        "thd,the->hde", key_heads, conv_heads, preferred_element_type=jnp.float32
    )
    query_state = jnp.einsum(
        "thd,the->hde", query_heads, grad_heads, preferred_element_type=jnp.float32
    )
    zero_state = jnp.zeros((HEADS, DH, DH), jnp.float32)
    key_total, query_total = (
        lax.psum(key_state.astype(jnp.bfloat16), "col").astype(jnp.float32),
        lax.psum(query_state.astype(jnp.bfloat16), "col").astype(jnp.float32),
    )
    zero_total = jnp.zeros_like(key_total)
    prefix_col = entering(key_state, "col", add_states, zero_state, False)
    suffix_col = entering(query_state, "col", add_states, zero_state, True)
    prefix_row = entering(key_total, "row", add_states, zero_total, False)
    suffix_row = entering(query_total, "row", add_states, zero_total, True)
    prefix = prefix_row + prefix_col
    suffix = suffix_row + suffix_col
    prefix_half = prefix.astype(jnp.bfloat16)
    suffix_half = suffix.astype(jnp.bfloat16)
    positions = jnp.arange(rows)
    causal = (positions[:, None] >= positions[None, :])[None, :, :]
    attn = jnp.where(
        causal,
        jnp.einsum("thd,uhd->htu", grad_heads, conv_heads, preferred_element_type=jnp.float32),
        0.0,
    ).astype(jnp.bfloat16)
    score = jnp.where(
        causal,
        jnp.einsum("thd,uhd->htu", query_heads, key_heads, preferred_element_type=jnp.float32),
        0.0,
    ).astype(jnp.bfloat16)
    grad_query = jnp.einsum("htu,uhd->thd", attn, key_heads, preferred_element_type=jnp.float32)
    grad_query = scale * (
        grad_query
        + jnp.einsum("the,hde->thd", grad_heads, prefix_half, preferred_element_type=jnp.float32)
    )
    grad_key = jnp.einsum("htu,thd->uhd", attn, query_heads, preferred_element_type=jnp.float32)
    grad_key = scale * (
        grad_key
        + jnp.einsum("the,hde->thd", conv_heads, suffix_half, preferred_element_type=jnp.float32)
    )
    grad_conv = jnp.einsum("htu,thd->uhd", score, grad_heads, preferred_element_type=jnp.float32)
    grad_conv = scale * (
        grad_conv
        + jnp.einsum("thd,hde->the", key_heads, suffix_half, preferred_element_type=jnp.float32)
    )
    grad_conv = grad_conv.reshape(rows, width)
    after = shifted(grad_conv[: CW - 1], ("row", "col"), -1)
    grad_ext = jnp.concatenate([grad_conv, after], axis=0)
    value_acc = jnp.zeros((rows, width), jnp.float32)
    weight_rows = []
    for offset in range(CW):
        value_acc = value_acc + conv_weight[offset][None, :] * grad_ext[offset : offset + rows]
        weight_rows.append(
            jnp.sum(grad_conv * value_ext[CW - 1 - offset : CW - 1 - offset + rows], axis=0)
        )
    grad_weight = lax.psum(jnp.stack(weight_rows, axis=0), ("row", "col"))
    return (
        grad_query.reshape(rows, width).astype(jnp.bfloat16),
        grad_key.reshape(rows, width).astype(jnp.bfloat16),
        value_acc.astype(jnp.bfloat16),
        grad_weight,
    )


def solution(mesh):
    placed = (
        P(("row", "col"), None),
        P(("row", "col"), None),
        P(("row", "col"), None),
        P(("row", "col"), None),
        P(),
    )
    return jax.shard_map(
        local,
        mesh=mesh,
        in_specs=placed,
        out_specs=(P(("row", "col"), None), P(("row", "col"), None), P(("row", "col"), None), P()),
        check_vma=False,
    )
```

profile of v0, /device:TPU:1, one launch (start us, length us, event | category | flops | bytes accessed | tf_op | source)
XLA Modules:
  0.0 302.5 jit_solution(16184635319729926033)
XLA Ops:
  8.2 2.2 convolution_convert_fusion
  10.5 4.6 %collective-permute-start = (bf16[3,2048]{1,0:T(4,128)(2,1)S(1)}, bf16[3,2048]{1,0:T(4,128)(2,1)S(1)}, u32[]{:S(2)}, u32[]{:S(2)}) collective-permute-start(bf16[3,2048]{1,0:T(4,128)(2,1)S(1)} %slice.51), channel_id=1, source_target_pairs={{0,1},{1,2},{2,3},{3,4},{4,5},{5,6},{6,7},{7,8},{8,9},{9,10},{10,1... | collective-permute-start | bytes 36872 | tf_op jit(solution)/shard_map/ppermute | solution.py:14
  18.5 41.7 %all-gather.13.cloned.1.call-done = bf16[128,128,128]{2,1,0:T(8,128)(2,1)} async-done(((bf16[16,128,128]{2,1,0:T(8,128)(2,1)}), bf16[128,128,128]{2,1,0:T(8,128)(2,1)}) %all-gather.13.cloned.1.call-update) | async-done | bytes 4194320 | tf_op jit(solution)/shard_map/all_gather | solution.py:21
  61.7 57.9 %all-reduce.3.cloned.1.call-done = (bf16[1,16,128,128]{2,3,1,0:T(8,128)(2,1)}, bf16[1,16,128,128]{3,2,1,0:T(8,128)(2,1)}) async-done(((bf16[1,16,128,128]{2,3,1,0:T(8,128)(2,1)}, bf16[1,16,128,128]{3,2,1,0:T(8,128)(2,1)}), (bf16[1,16,128,128]{2,3,1,0:T(8,128)(2,1)}, bf16[1,16,128,128]{3,2,1,0:T(8,128)(2,1)})) %all-reduce.3.cloned.1.call-update) | async-done | bytes 1048592 | tf_op jit(solution)/shard_map/psum | solution.py:60
  120.6 1.5 copy.43
  122.1 1.9 convolution_bitcast_fusion.2
  124.5 1.6 convolution_bitcast_fusion.4
  127.2 8.0 %while.47 = (s32[]{:T(128)}, f32[16,128,128]{2,1,0:T(8,128)S(1)}, s32[]{:T(128)}, bf16[8,16,128,128]{3,2,1,0:T(8,128)(2,1)}, s32[]{:T(128)}, /*index=5*/s32[]{:T(128)}, s32[]{:T(128)}, s32[]{:T(128)}) while((s32[]{:T(128)}, f32[16,128,128]{2,1,0:T(8,128)S(1)}, s32[]{:T(128)}, bf16[8,16,128,128]{3,2,1,0:T(8,128)(2,1)}, s32[]{:T(128)}, ...), condition=%wide.region_9.10_spmd, body=%wide.region_8.9_spmd.sunk | while | flops 524294 | bytes 2621575 | solution.py:28
  127.2 1.3 convert_add_fusion.11
  128.5 1.3 convert_add_fusion.11
  129.8 1.3 convert_add_fusion.11
  131.2 1.3 convert_add_fusion.11
  132.6 1.3 convert_add_fusion.11
  133.9 1.3 convert_add_fusion.11
  135.2 35.0 %all-gather.11.cloned.1.call-done = bf16[128,128,128]{2,1,0:T(8,128)(2,1)} async-done(((bf16[16,128,128]{2,1,0:T(8,128)(2,1)}), bf16[128,128,128]{2,1,0:T(8,128)(2,1)}) %all-gather.11.cloned.1.call-update) | async-done | bytes 4194320 | tf_op jit(solution)/shard_map/all_gather | solution.py:21
  170.2 1.1 broadcast_in_dim.22.clone2.1
  171.3 2.5 while.45
  171.3 2.5 convert_add_fusion.9
  173.8 31.8 %all-gather.9.cloned.1.call-done = bf16[4,16,128,128]{3,2,1,0:T(8,128)(2,1)} async-done(((bf16[1,16,128,128]{3,2,1,0:T(8,128)(2,1)}), bf16[4,16,128,128]{3,2,1,0:T(8,128)(2,1)}) %all-gather.9.cloned.1.call-update) | async-done | bytes 2097168 | tf_op jit(solution)/shard_map/all_gather | solution.py:21
  206.6 7.4 %while.46 = (s32[]{:T(128)}, f32[16,128,128]{2,1,0:T(8,128)}, s32[]{:T(128)}, bf16[4,16,128,128]{3,2,1,0:T(8,128)(2,1)}, s32[]{:T(128)}, /*index=5*/s32[]{:T(128)}, s32[]{:T(128)}, s32[]{:T(128)}) while((s32[]{:T(128)}, f32[16,128,128]{2,1,0:T(8,128)}, s32[]{:T(128)}, bf16[4,16,128,128]{3,2,1,0:T(8,128)(2,1)}, s32[]{:T(128)}, ...), condition=%wide.region_7.8_spmd, body=%wide.region_6.7_spmd.sunk | while | flops 524294 | bytes 2621575 | solution.py:28
  206.6 2.5 convert_add_fusion.10
  209.1 2.5 convert_add_fusion.10
  211.6 2.5 convert_add_fusion.10
  214.0 1.5 add_convert_fusion
  217.0 2.6 collective-permute-start.1
  219.6 2.7 fusion.7
  222.3 21.2 %all-gather.7.cloned.1.call-done = bf16[4,16,128,128]{3,2,1,0:T(8,128)(2,1)} async-done(((bf16[1,16,128,128]{3,2,1,0:T(8,128)(2,1)}), bf16[4,16,128,128]{3,2,1,0:T(8,128)(2,1)}) %all-gather.7.cloned.1.call-update) | async-done | bytes 2097168 | tf_op jit(solution)/shard_map/all_gather | solution.py:21
  243.6 1.8 convolution_bitcast_fusion.5
  246.7 1.3 copy.62
  249.0 2.0 copy.69
  251.1 1.7 multiply_reduce_fusion.3
  252.8 43.2 %psum.23 = f32[4,2048]{1,0:T(4,128)} all-reduce(f32[4,2048]{1,0:T(4,128)S(1)} %pad_maximum_fusion.1), channel_id=1, replica_groups=mesh['row'=4,'col'=8] {'row','col'}, use_global_device_ids=true, to_apply=%region_14.15 | all-reduce | flops 8192 | bytes 65536 | tf_op jit(solution)/shard_map/psum | solution.py:109
  (67 shorter events, 13.4 us)
Async XLA Ops:
  7.2 1.0 copy-start
  7.2 3.2 %copy-start.15 = (bf16[128,2048]{1,0:T(8,128)(2,1)S(1)}, bf16[128,2048]{1,0:T(8,128)(2,1)}, u32[]{:S(2)}) copy-start(bf16[128,2048]{1,0:T(8,128)(2,1)} %param.15) | copy-start | bytes 1572868
  7.2 7.9 %copy-start.17 = (f32[4,2048]{1,0:T(4,128)S(1)}, f32[4,2048]{1,0:T(4,128)}, u32[]{:S(2)}) copy-start(f32[4,2048]{1,0:T(4,128)} %param.17) | copy-start | bytes 98308
  7.2 53.0 %all-gather.13.cloned.1.call-start = ((), (), s32[]{:S(2)}) async-start(), calls=%async_computation.3 | async-start | bytes 4718592 | tf_op jit(solution)/shard_map/all_gather | solution.py:21
  10.5 5.5 %collective-permute-start = (bf16[3,2048]{1,0:T(4,128)(2,1)S(1)}, bf16[3,2048]{1,0:T(4,128)(2,1)S(1)}, u32[]{:S(2)}, u32[]{:S(2)}) collective-permute-start(bf16[3,2048]{1,0:T(4,128)(2,1)S(1)} %slice.51), channel_id=1, source_target_pairs={{0,1},{1,2},{2,3},{3,4},{4,5},{5,6},{6,7},{7,8},{8,9},{9,10},{10,1... | collective-permute-start | bytes 36872 | tf_op jit(solution)/shard_map/ppermute | solution.py:14
  16.1 1.0 copy-start.8
  17.5 42.7 %copy-start.6 = (bf16[16,128,128]{2,1,0:T(8,128)(2,1)}, bf16[16,128,128]{2,1,0:T(8,128)(2,1)S(1)}, u32[]{:S(2)}) copy-start(bf16[16,128,128]{2,1,0:T(8,128)(2,1)S(1)} %convolution_convert_fusion.1) | copy-start | bytes 1572868
  60.2 59.4 %all-reduce.3.cloned.1.call-start = ((), (), s32[]{:S(2)}) async-start(), calls=%async_computation.4 | async-start | bytes 2097152 | tf_op jit(solution)/shard_map/psum | solution.py:60
  60.9 109.2 %all-gather.11.cloned.1.call-start = ((), (), s32[]{:S(2)}) async-start(), calls=%async_computation.2 | async-start | bytes 4718592 | tf_op jit(solution)/shard_map/all_gather | solution.py:21
  61.7 143.8 %all-gather.9.cloned.1.call-start = ((), (), s32[]{:S(2)}) async-start(), calls=%async_computation.1 | async-start | bytes 2621440 | tf_op jit(solution)/shard_map/all_gather | solution.py:21
  119.6 2.5 copy-start.5
  119.6 123.9 %all-gather.7.cloned.1.call-start = ((), (), s32[]{:S(2)}) async-start(), calls=%async_computation | async-start | bytes 2621440 | tf_op jit(solution)/shard_map/all_gather | solution.py:21
  122.0 1.9 copy-start.3
  124.4 1.6 copy-start.13
  124.5 1.6 copy-start.16
  214.0 1.5 copy-start.9
  214.0 1.9 copy-start.10
  215.9 0.8 copy-start.7
  216.7 5.6 %copy-start.1 = (f32[128,16,128]{0,2,1:T(8,128)}, f32[128,16,128]{0,2,1:T(8,128)S(1)}, u32[]{:S(2)}) copy-start(f32[128,16,128]{0,2,1:T(8,128)S(1)} %fusion.3) | copy-start | bytes 3145732
  217.0 34.1 %collective-permute-start.1 = (f32[3,2048]{1,0:T(4,128)S(1)}, f32[3,2048]{1,0:T(4,128)S(1)}, u32[]{:S(2)}, u32[]{:S(2)}) collective-permute-start(f32[3,2048]{1,0:T(4,128)S(1)} %copy.63), channel_id=1, source_target_pairs={{1,0},{2,1},{3,2},{4,3},{5,4},{6,5},{7,6},{8,7},{9,8},{10,9},{11,1... | collective-permute-start | bytes 73736 | tf_op jit(solution)/shard_map/ppermute | solution.py:14
  243.6 1.8 copy-start.4
  243.6 1.8 copy-start.14
  245.4 1.2 copy-start.2
  246.5 1.5 copy-start.12
  248.0 3.1 %copy-start.11 = (f32[128,2048]{1,0:T(8,128)S(1)}, f32[128,2048]{1,0:T(8,128)}, u32[]{:S(2)}) copy-start(f32[128,2048]{1,0:T(8,128)} %copy.62) | copy-start | bytes 3145732
Sparse Core Ops, SparseCore 0:
  10.5 49.6 all-gather.12
  64.0 55.5 all-reduce.2
  121.8 48.3 all-gather.10
  171.9 33.6 all-gather.8
  207.8 35.6 all-gather.6
where the time goes:
time: 305 us; the launch traced here: 303 us
  waiting for transfers between devices  190 us (62%)
  blocking collectives  43.2 us (14%)
  other arithmetic  21.6 us (7%)
  between operations  14 us (5%)
  local copies, waits for them, and re-layouts  13.8 us (5%)
  matrix products  12.5 us (4%)
  starting transfers between devices  7.38 us (2%)
    all_gather x4, waiting for transfers between devices, entering(): gathered = lax.all_gather(value.astype(jnp.bfloat16), axis)  130 us
    psum x1, waiting for transfers between devices, local(): lax.psum(key_state.astype(jnp.bfloat16), 'col').astype(jnp.float32)  57.9 us
    psum x1, blocking collectives, local(): grad_weight = lax.psum(jnp.stack(weight_rows, axis=0), ('row', 'col'))  43.2 us
    add x10, other arithmetic, add_states(): return earlier + later  17.7 us
    ppermute x2, starting transfers between devices, shifted(): return lax.ppermute(value, axis, pairs)  7.22 us
    unnamed x39, local copies, waits for them, and re-layouts  6.26 us
  transfers between devices with their start and end apart: 7, of which 6 were waited for; matrix products, arithmetic and copies ran while one was open for 14% of the time, Pallas kernels for 0%

commit v1 on v0

v1 whole, which is shorter than its diff:
```python
import functools

import jax
import jax.numpy as jnp
from jax import lax
from jax.experimental import pallas as pl
from jax.experimental.pallas import tpu as pltpu
from jax.sharding import PartitionSpec as P

HEADS = 16
DH = 128
CW = 4
HALF = HEADS // 2
HALO = 8
AXES = ("row", "col")
F32 = jnp.float32
BF16 = jnp.bfloat16
VMEM = pl.BlockSpec(memory_space=pltpu.VMEM)
SMEM = pl.BlockSpec(memory_space=pltpu.SMEM)
PARAMS = pltpu.CompilerParams(vmem_limit_bytes=40 * 1024 * 1024)


def dot(a, b, over):
    return lax.dot_general(a, b, ((over[:1], over[1:]), ((), ())), preferred_element_type=F32)


def columns(head):
    return pl.ds(pl.multiple_of(head * DH, DH), DH)


def call(kernel, outs, scalars, arrays, scratch=()):
    return pl.pallas_call(
        kernel,
        out_shape=outs,
        in_specs=[SMEM] * len(scalars) + [VMEM] * len(arrays),
        out_specs=jax.tree.map(lambda _: VMEM, outs),
        scratch_shapes=scratch,
        compiler_params=PARAMS,
    )(*scalars, *arrays)


def shape(dims, dtype=BF16):
    return jax.ShapeDtypeStruct(dims, dtype)


def query_state_kernel(core_ref, q_ref, g_ref, keep_ref, send_ref):
    core = core_ref[0]
    for side, out in enumerate((keep_ref, send_ref)):
        first = HALF * lax.rem(core + side, 2)
        for i in range(HALF):
            at = columns(first + i)
            out[i] = dot(q_ref[:, at], g_ref[:, at], (0, 0)).astype(BF16)


def key_state_kernel(core_ref, k_ref, v_ref, halo_ref, w_ref, conv_ref, keep_ref, send_ref):
    core = core_ref[0]
    rows = v_ref.shape[0]
    for side, out in enumerate((keep_ref, send_ref)):
        first = HALF * lax.rem(core + side, 2)
        for i in range(HALF):
            at = columns(first + i)
            ext = jnp.concatenate([halo_ref[:, at].astype(F32), v_ref[:, at].astype(F32)], axis=0)
            acc = w_ref[pl.ds(0, 1), at] * ext[HALO:]
            for j in range(1, CW):
                acc = acc + w_ref[pl.ds(j, 1), at] * ext[HALO - j : HALO - j + rows]
            conved = acc.astype(BF16)
            conv_ref[:, at] = conved
            out[i] = dot(k_ref[:, at], conved, (0, 0)).astype(BF16)


def turn_kernel(q_ref, keep_ref, recv_ref, out_ref):
    chips = q_ref.shape[0]
    total = jnp.zeros(q_ref.shape[1:], F32)
    for p in reversed(range(chips)):
        out_ref[p, 0] = total.astype(BF16)
        total = total + q_ref[p].astype(F32)
        out_ref[p, 1] = (keep_ref[p].astype(F32) + recv_ref[p].astype(F32)).astype(BF16)


def share_kernel(core_ref, chip_ref, keep_ref, recv_ref, own_ref, send_ref, *, first_gets):
    core = core_ref[0]
    mine = (core == (0 if first_gets else 1)).astype(F32)
    for p in range(chip_ref.shape[0]):
        state = chip_ref[p, 0].astype(F32)
        own_ref[p] = (state + mine * recv_ref[p].astype(F32)).astype(BF16)
        send_ref[p] = (state + (1.0 - mine) * keep_ref[p].astype(F32)).astype(BF16)


def query_side_kernel(
    core_ref,
    q_ref,
    k_ref,
    c_ref,
    g_ref,
    v_ref,
    halo_ref,
    own_ref,
    recv_ref,
    chip_ref,
    gk_ref,
    gc_ref,
    edge_ref,
    out_ref,
    taps_ref,
    *,
    scale,
):
    core = core_ref[0]
    rows = q_ref.shape[0]
    early = lax.broadcasted_iota(jnp.int32, (rows, rows), 0) <= lax.broadcasted_iota(
        jnp.int32, (rows, rows), 1
    )
    for side, states in enumerate((own_ref, recv_ref)):
        first = HALF * lax.rem(core + side, 2)
        for i in range(HALF):
            head = first + i
            at = columns(head)
            q, k, c, g, suffix = q_ref[:, at], k_ref[:, at], c_ref[:, at], g_ref[:, at], states[i]
            score = jnp.where(early, dot(k, q, (1, 1)), 0.0).astype(BF16)
            attn = jnp.where(early, dot(c, g, (1, 1)), 0.0).astype(BF16)
            gk = dot(attn, q, (1, 0)) + dot(c, suffix, (1, 1))
            gk_ref[:, at] = (scale * gk).astype(BF16)
            gc = scale * (dot(score, g, (1, 0)) + dot(k, suffix, (1, 0)))
            gc_ref[:, at] = gc
            edge_ref[:, at] = gc[:HALO]
            ext = jnp.concatenate([halo_ref[:, at].astype(F32), v_ref[:, at].astype(F32)], axis=0)
            for j in range(CW):
                part = jnp.sum(gc * ext[HALO - j : HALO - j + rows], axis=0, keepdims=True)
                taps_ref[pl.ds(j * HEADS + head, 1), :] = part
    chips, pieces, depth, _ = out_ref.shape
    total = jnp.zeros(out_ref.shape[2:], F32)
    taps = [taps_ref[n * depth : (n + 1) * depth].astype(BF16) for n in range(pieces - 1)]
    for p in range(chips):
        out_ref[p, 0] = total.astype(BF16)
        total = total + chip_ref[p, 1].astype(F32)
        for n in range(pieces - 1):
            out_ref[p, 1 + n] = taps[n]


def taps_kernel(chip_ref, out_ref):
    chips, pieces, depth, _ = chip_ref.shape
    for n in range(pieces - 1):
        total = chip_ref[0, 1 + n].astype(F32)
        for p in range(1, chips):
            total = total + chip_ref[p, 1 + n].astype(F32)
        out_ref[n * depth : (n + 1) * depth] = total


def key_side_kernel(
    core_ref,
    k_ref,
    c_ref,
    g_ref,
    own_ref,
    recv_ref,
    gc_ref,
    edge_ref,
    w_ref,
    taps_ref,
    far_ref,
    gq_ref,
    gv_ref,
    gw_ref,
    *,
    scale,
):
    core = core_ref[0]
    rows = k_ref.shape[0]
    causal = lax.broadcasted_iota(jnp.int32, (rows, rows), 0) >= lax.broadcasted_iota(
        jnp.int32, (rows, rows), 1
    )
    for side, states in enumerate((own_ref, recv_ref)):
        first = HALF * lax.rem(core + side, 2)
        for i in range(HALF):
            at = columns(first + i)
            k, c, g, prefix = k_ref[:, at], c_ref[:, at], g_ref[:, at], states[i]
            attn = jnp.where(causal, dot(g, c, (1, 1)), 0.0).astype(BF16)
            gq = dot(attn, k, (1, 0)) + dot(g, prefix, (1, 1))
            gq_ref[:, at] = (scale * gq).astype(BF16)
            ext = jnp.concatenate([gc_ref[:, at], edge_ref[:, at]], axis=0)
            acc = w_ref[pl.ds(0, 1), at] * ext[:rows]
            for j in range(1, CW):
                acc = acc + w_ref[pl.ds(j, 1), at] * ext[j : j + rows]
            gv_ref[:, at] = acc.astype(BF16)
    for head in range(HEADS):
        for j in range(CW):
            row = pl.ds(j * HEADS + head, 1)
            gw_ref[pl.ds(j, 1), pl.ds(head * DH, DH)] = taps_ref[row, :] + far_ref[row, :]


def local(queries, keys, values, grad_out, conv_weight):
    rows, width = queries.shape
    count = lax.axis_size("row") * lax.axis_size("col")
    chips = count // 2
    depth = HALF * DH // chips
    pieces = 1 + CW * HEADS // depth
    scale = (DH * rows * count) ** (-0.5)
    core = lax.rem(lax.axis_index("col"), 2).astype(jnp.int32).reshape(1)
    groups = [[2 * p + c for p in range(chips)] for c in range(2)]

    def swap(value):
        return lax.ppermute(value, AXES, [(d, d ^ 1) for d in range(count)])

    def shifted(value, by):
        pairs = [(d, d + by) for d in range(count) if 0 <= d + by < count]
        return lax.ppermute(value, AXES, pairs)

    def turn(value):
        return lax.all_to_all(value, AXES, 0, 0, axis_index_groups=groups, tiled=True)

    def sliced(value):
        return value.reshape(chips, depth, DH)

    def headed(value):
        return value.reshape(HALF, DH, DH)

    half = shape((HALF, DH, DH))
    slices = shape((chips, depth, DH))
    halo = shifted(values[rows - HALO :], 1)
    q_keep, q_send = call(query_state_kernel, (half, half), [core], [queries, grad_out])
    q_recv = swap(q_send)
    conved, k_keep, k_send = call(
        key_state_kernel,
        (shape((rows, width)), half, half),
        [core],
        [keys, values, halo, conv_weight],
    )
    k_recv = swap(k_send)
    q_chip = (q_keep.astype(F32) + q_recv.astype(F32)).astype(BF16)
    q_turned = turn(sliced(q_chip))
    both = call(
        turn_kernel,
        shape((chips, 2, depth, DH)),
        [],
        [q_turned, sliced(k_keep), sliced(k_recv)],
    )
    both = turn(both)
    q_own, q_give = call(
        functools.partial(share_kernel, first_gets=True),
        (slices, slices),
        [core],
        [both, sliced(q_keep), sliced(q_recv)],
    )
    q_got = swap(q_give)
    grad_keys, grad_conv, edge, last = call(
        functools.partial(query_side_kernel, scale=scale),
        (
            shape((rows, width)),
            shape((rows, width), F32),
            shape((HALO, width), F32),
            shape((chips, pieces, depth, DH)),
        ),
        [core],
        [
            queries,
            keys,
            conved,
            grad_out,
            values,
            halo,
            headed(q_own),
            headed(q_got),
            both,
        ],
        [pltpu.VMEM((CW * HEADS, DH), F32)],
    )
    edge = shifted(edge, -1)
    last = turn(last)
    k_own, k_give = call(
        functools.partial(share_kernel, first_gets=False),
        (slices, slices),
        [core],
        [last, sliced(k_keep), sliced(k_recv)],
    )
    k_got = swap(k_give)
    taps = call(taps_kernel, shape((CW * HEADS, DH), F32), [], [last])
    far = swap(taps)
    grad_queries, grad_values, grad_weight = call(
        functools.partial(key_side_kernel, scale=scale),
        (shape((rows, width)), shape((rows, width)), shape((CW, width), F32)),
        [core],
        [
            keys,
            conved,
            grad_out,
            headed(k_own),
            headed(k_got),
            grad_conv,
            edge,
            conv_weight,
            taps,
            far,
        ],
    )
    return grad_queries, grad_keys, grad_values, grad_weight


def solution(mesh):
    placed = (
        P(("row", "col"), None),
        P(("row", "col"), None),
        P(("row", "col"), None),
        P(("row", "col"), None),
        P(),
    )
    return jax.shard_map(
        local,
        mesh=mesh,
        in_specs=placed,
        out_specs=(P(("row", "col"), None), P(("row", "col"), None), P(("row", "col"), None), P()),
        check_vma=False,
    )
```

time: 305 us -> 79.4 us (0.26)
  waiting for transfers between devices: 190 us -> 10.4 us
  other arithmetic: 21.6 us -> 0.77 us
  between operations: 14 us -> 0.75 us
  matrix products: 12.5 us -> 0 us
  local copies, waits for them, and re-layouts: 13.8 us -> 2.1 us
  starting transfers between devices: 7.38 us -> 17.4 us
  Pallas kernels: 0 us -> 7.77 us
  blocking collectives: 43.2 us -> 39.7 us
    all_gather x4 -> x0, waiting for transfers between devices: 130 us -> none  [entering(): gathered = lax.all_gather(value.astype(jnp.bfloat16), axis)]
    psum x1 -> x0, waiting for transfers between devices: 57.9 us -> none  [local(): lax.psum(key_state.astype(jnp.bfloat16), 'col').astype(jnp.float32)]
    psum x1 -> x0, blocking collectives: 43.2 us -> none  [local(): grad_weight = lax.psum(jnp.stack(weight_rows, axis=0), ('row', 'col'))]
    all_to_all x0 -> x2, blocking collectives: none -> 39.7 us  [turn(): lax.all_to_all(value, AXES, 0, 0, axis_index_groups=groups, tiled=True)]
    add x10 -> x0, other arithmetic: 17.7 us -> none  [add_states(): return earlier + later]
    dot_general x9 -> x0, matrix products: 12.5 us -> none  [the longest x1 2.67 us: local(): jnp.einsum('the,hde->thd', conv_heads, suffix_half, preferred_element_typ...]
    ppermute x2 -> x7, waiting for transfers between devices: 0.81 us -> 8.74 us  [the longest x2 4.57 us: shifted(): return lax.ppermute(value, AXES, pairs)]
    pallas_call x0 -> x8, Pallas kernels: none -> 7.77 us  [call(): pl.pallas_call(kernel, out_shape=outs, in_specs=[SMEM] * len(scalars) + [...]
  transfers between devices with their start and end apart: 7 -> 8, of which waited for: 6 -> 6; matrix products, arithmetic and copies ran while one was open for 14% -> 0% of each run, Pallas kernels for 0% -> 1%
where the time goes in v1:
time: 79.4 us; the launch traced here: 78.9 us
  blocking collectives  39.7 us (50%)
  starting transfers between devices  17.4 us (22%)
  waiting for transfers between devices  10.4 us (13%)
  Pallas kernels  7.77 us (10%)
  local copies, waits for them, and re-layouts  2.1 us (3%)
    all_to_all x2, blocking collectives, turn(): lax.all_to_all(value, AXES, 0, 0, axis_index_groups=groups, tiled=True)  39.7 us
    pallas_call x8, Pallas kernels, call(): pl.pallas_call(kernel, out_shape=outs, in_specs=[SMEM] * len(scalars) + [...  7.77 us
    all_to_all x1, starting transfers between devices, turn(): lax.all_to_all(value, AXES, 0, 0, axis_index_groups=groups, tiled=True)  7.72 us
    ppermute x2, starting transfers between devices, shifted(): return lax.ppermute(value, AXES, pairs)  6.01 us
    ppermute x2, waiting for transfers between devices, shifted(): return lax.ppermute(value, AXES, pairs)  4.57 us
    ppermute x5, waiting for transfers between devices, swap(): return lax.ppermute(value, AXES, [(d, d ^ 1) for d in range(count)])  4.17 us
    ppermute x5, starting transfers between devices, swap(): return lax.ppermute(value, AXES, [(d, d ^ 1) for d in range(count)])  3.67 us
    unnamed x14, local copies, waits for them, and re-layouts  2.1 us
  transfers between devices with their start and end apart: 8, of which 6 were waited for; matrix products, arithmetic and copies ran while one was open for 0% of the time, Pallas kernels for 1%

profile of v1, /device:TPU:1, one launch (start us, length us, event | category | flops | bytes accessed | tf_op | source)
XLA Modules:
  0.0 78.9 jit_solution(7701703655433598816)
XLA Ops:
  0.6 0.0 copy-start.1
  0.6 1.0 %copy-done.1 = bf16[128,2048]{1,0:T(8,128)(2,1)S(1)} copy-done((bf16[128,2048]{1,0:T(8,128)(2,1)S(1)}, bf16[128,2048]{1,0:T(8,128)(2,1)}, u32[]{:S(2)}) %copy-start.1) | copy-done | bytes 524312
  1.7 1.0 %copy-done.4 = bf16[128,2048]{1,0:T(8,128)(2,1)S(1)} copy-done((bf16[128,2048]{1,0:T(8,128)(2,1)S(1)}, bf16[128,2048]{1,0:T(8,128)(2,1)}, u32[]{:S(2)}) %copy-start.4) | copy-done | bytes 524312
  2.7 0.5 shard_map.85
  3.2 0.1 collective-permute-start.1
  3.3 1.5 %collective-permute-done.1 = bf16[8,128,128]{2,1,0:T(8,128)(2,1)S(1)} collective-permute-done((bf16[8,128,128]{2,1,0:T(8,128)(2,1)S(1)}, bf16[8,128,128]{2,1,0:T(8,128)(2,1)S(1)}, u32[]{:S(2)}, u32[]{:S(2)}) %collective-permute-start.1) | collective-permute-done | bytes 262176 | tf_op jit(solution)/shard_map/ppermute | solution.py:202
  4.8 0.8 add_convert_fusion
  5.6 7.7 %all-to-all-start = ((bf16[16,64,128]{2,1,0:T(8,128)(2,1)}), bf16[16,64,128]{2,1,0:T(8,128)(2,1)S(1)}, u32[]{:S(2)}, u32[]{:S(2)}) async-start(bf16[16,64,128]{2,1,0:T(8,128)(2,1)} %bitcast.1), calls=%async_computation | async-start | bytes 524288 | tf_op jit(solution)/shard_map/all_to_all | solution.py:209
  13.3 0.0 copy-done.3
  13.3 0.0 copy-start.6
  13.3 4.1 %collective-permute-start = (bf16[8,2048]{1,0:T(8,128)(2,1)S(1)}, bf16[8,2048]{1,0:T(8,128)(2,1)S(1)}, u32[]{:S(2)}, u32[]{:S(2)}) collective-permute-start(bf16[8,2048]{1,0:T(8,128)(2,1)S(1)} %slice.3), channel_id=1, source_target_pairs={{0,1},{1,2},{2,3},{3,4},{4,5},{5,6},{6,7},{7,8},{8,9},{9,10},{10,1... | collective-permute-start | bytes 98312 | tf_op jit(solution)/shard_map/ppermute | solution.py:206
  17.4 1.1 %collective-permute-done.halo_ref = bf16[8,2048]{1,0:T(8,128)(2,1)S(1)} collective-permute-done((bf16[8,2048]{1,0:T(8,128)(2,1)S(1)}, bf16[8,2048]{1,0:T(8,128)(2,1)S(1)}, u32[]{:S(2)}, u32[]{:S(2)}) %collective-permute-start) | collective-permute-done | bytes 32800 | tf_op jit(solution)/shard_map/ppermute | solution.py:206
  18.5 0.0 copy-done.6
  18.5 0.8 %shard_map.84 = (bf16[128,2048]{1,0:T(8,128)(2,1)S(1)}, bf16[8,128,128]{2,1,0:T(8,128)(2,1)S(1)}, bf16[8,128,128]{2,1,0:T(8,128)(2,1)S(1)}) custom-call(s32[1]{0:T(128)} %bitcast.core_ref, bf16[128,2048]{1,0:T(8,128)(2,1)S(1)} %copy-done, bf16[128,2048]{1,0:T(8,128)(2,1)S(1)} %copy-done.3, bf16[8,2048]{1,0:T(8,128)(2,1)S(1)} %collective-permute-done.halo_ref, ...), custom_call_target="tpu_custom_call" | custom-call | tf_op jit(solution)/shard_map/pallas_call | solution.py:32
  19.3 0.1 collective-permute-start.2
  19.4 1.5 %collective-permute-done.2 = bf16[8,128,128]{2,1,0:T(8,128)(2,1)S(1)} collective-permute-done((bf16[8,128,128]{2,1,0:T(8,128)(2,1)S(1)}, bf16[8,128,128]{2,1,0:T(8,128)(2,1)S(1)}, u32[]{:S(2)}, u32[]{:S(2)}) %collective-permute-start.2) | collective-permute-done | bytes 262176 | tf_op jit(solution)/shard_map/ppermute | solution.py:202
  20.9 1.7 %all-to-all-done.q_ref = bf16[16,64,128]{2,1,0:T(8,128)(2,1)S(1)} async-done(((bf16[16,64,128]{2,1,0:T(8,128)(2,1)}), bf16[16,64,128]{2,1,0:T(8,128)(2,1)S(1)}, u32[]{:S(2)}, u32[]{:S(2)}) %all-to-all-start) | async-done | bytes 262176 | tf_op jit(solution)/shard_map/all_to_all | solution.py:209
  22.6 0.1 shard_map.86
  22.7 21.6 %all_to_all.15.chip_ref = bf16[16,2,64,128]{3,2,1,0:T(8,128)(2,1)S(1)} all-to-all(bf16[16,2,64,128]{3,2,1,0:T(8,128)(2,1)S(1)} %shard_map.86), channel_id=1, replica_groups={{0,2,4,6,8,10,12,14,16,18,20,22,24,26,28,30},{1,3,5,7,9,11,13,15,17,19,..., dimensions={0} | all-to-all | bytes 1048576 | tf_op jit(solution)/shard_map/all_to_all | solution.py:209
  44.3 0.1 shard_map.87
  44.4 1.8 %collective-permute-start.3 = (bf16[16,64,128]{2,1,0:T(8,128)(2,1)S(1)}, bf16[16,64,128]{2,1,0:T(8,128)(2,1)S(1)}, u32[]{:S(2)}, u32[]{:S(2)}) collective-permute-start(bf16[16,64,128]{2,1,0:T(8,128)(2,1)S(1)} %get-tuple-element.26), channel_id=1, source_target_pairs={{0,1},{1,0},{2,3},{3,2},{4,5},{5,4},{6,7},{7,6},{8,9},{9,8},{10,11... | collective-permute-start | bytes 786440 | tf_op jit(solution)/shard_map/ppermute | solution.py:202
  46.2 1.2 %collective-permute-done.3 = bf16[16,64,128]{2,1,0:T(8,128)(2,1)S(1)} collective-permute-done((bf16[16,64,128]{2,1,0:T(8,128)(2,1)S(1)}, bf16[16,64,128]{2,1,0:T(8,128)(2,1)S(1)}, u32[]{:S(2)}, u32[]{:S(2)}) %collective-permute-start.3) | collective-permute-done | bytes 262176 | tf_op jit(solution)/shard_map/ppermute | solution.py:202
  47.3 3.5 %shard_map.88 = (bf16[128,2048]{1,0:T(8,128)(2,1)}, f32[128,2048]{1,0:T(8,128)S(1)}, f32[8,2048]{1,0:T(8,128)S(1)}, bf16[16,2,64,128]{3,2,1,0:T(8,128)(2,1)S(1)}) custom-call(s32[1]{0:T(128)} %bitcast.core_ref, bf16[128,2048]{1,0:T(8,128)(2,1)S(1)} %copy-done.5, bf16[128,2048]{1,0:T(8,128)(2,1)S(1)} %copy-done, ...), custom_call_target="tpu_custom_call" | custom-call | tf_op jit(solution)/shard_map/pallas_call | solution.py:32
  50.9 18.2 %all_to_all.16.chip_ref = bf16[16,2,64,128]{3,2,1,0:T(8,128)(2,1)S(1)} all-to-all(bf16[16,2,64,128]{3,2,1,0:T(8,128)(2,1)S(1)} %get-tuple-element.27), channel_id=1, replica_groups={{0,2,4,6,8,10,12,14,16,18,20,22,24,26,28,30},{1,3,5,7,9,11,13,15,17,19,..., dimensions={0} | all-to-all | bytes 1048576 | tf_op jit(solution)/shard_map/all_to_all | solution.py:209
  69.1 0.1 shard_map.89
  69.2 1.6 %collective-permute-start.4 = (bf16[16,64,128]{2,1,0:T(8,128)(2,1)S(1)}, bf16[16,64,128]{2,1,0:T(8,128)(2,1)S(1)}, u32[]{:S(2)}, u32[]{:S(2)}) collective-permute-start(bf16[16,64,128]{2,1,0:T(8,128)(2,1)S(1)} %get-tuple-element.29), channel_id=1, source_target_pairs={{0,1},{1,0},{2,3},{3,2},{4,5},{5,4},{6,7},{7,6},{8,9},{9,8},{10,11... | collective-permute-start | bytes 786440 | tf_op jit(solution)/shard_map/ppermute | solution.py:202
  70.8 1.9 %collective-permute-start.5 = (f32[8,2048]{1,0:T(8,128)S(1)}, f32[8,2048]{1,0:T(8,128)S(1)}, u32[]{:S(2)}, u32[]{:S(2)}) collective-permute-start(f32[8,2048]{1,0:T(8,128)S(1)} %get-tuple-element.31), channel_id=1, source_target_pairs={{1,0},{2,1},{3,2},{4,3},{5,4},{6,5},{7,6},{8,7},{9,8},{10,9},{11,1... | collective-permute-start | bytes 196616 | tf_op jit(solution)/shard_map/ppermute | solution.py:206
  72.8 0.1 collective-permute-start.6
  72.9 3.5 %collective-permute-done.5.edge_ref = f32[8,2048]{1,0:T(8,128)S(1)} collective-permute-done((f32[8,2048]{1,0:T(8,128)S(1)}, f32[8,2048]{1,0:T(8,128)S(1)}, u32[]{:S(2)}, u32[]{:S(2)}) %collective-permute-start.5) | collective-permute-done | bytes 65568 | tf_op jit(solution)/shard_map/ppermute | solution.py:206
  76.4 0.0 collective-permute-done.6.far_ref
  76.4 0.0 collective-permute-done.4
  76.4 2.5 %shard_map.91 = (bf16[128,2048]{1,0:T(8,128)(2,1)}, bf16[128,2048]{1,0:T(8,128)(2,1)}, f32[4,2048]{1,0:T(4,128)}) custom-call(s32[1]{0:T(128)} %bitcast.core_ref, bf16[128,2048]{1,0:T(8,128)(2,1)S(1)} %copy-done, bf16[128,2048]{1,0:T(8,128)(2,1)S(1)} %get-tuple-element.20.c_ref, bf16[128,2048]{1,0:T(8,128)(2,1)S(1)} %copy-done.2, ...), custom_call_target="tpu_custom_call" | custom-call | tf_op jit(solution)/shard_map/pallas_call | solution.py:32
  (10 shorter events, 0.1 us)
Async XLA Ops:
  0.6 1.0 %copy-start.1 = (bf16[128,2048]{1,0:T(8,128)(2,1)S(1)}, bf16[128,2048]{1,0:T(8,128)(2,1)}, u32[]{:S(2)}) copy-start(bf16[128,2048]{1,0:T(8,128)(2,1)} %g_ref.5) | copy-start | bytes 1572868
  1.7 1.0 %copy-start.4 = (bf16[128,2048]{1,0:T(8,128)(2,1)S(1)}, bf16[128,2048]{1,0:T(8,128)(2,1)}, u32[]{:S(2)}) copy-start(bf16[128,2048]{1,0:T(8,128)(2,1)} %q_ref.3) | copy-start | bytes 1572868
  3.2 1.6 %collective-permute-start.1 = (bf16[8,128,128]{2,1,0:T(8,128)(2,1)S(1)}, bf16[8,128,128]{2,1,0:T(8,128)(2,1)S(1)}, u32[]{:S(2)}, u32[]{:S(2)}) collective-permute-start(bf16[8,128,128]{2,1,0:T(8,128)(2,1)S(1)} %get-tuple-element.22), channel_id=1, source_target_pairs={{0,1},{1,0},{2,3},{3,2},{4,5},{5,4},{6,7},{7,6},{8,9},{9,8},{10,11... | collective-permute-start | bytes 786440 | tf_op jit(solution)/shard_map/ppermute | solution.py:202
  4.8 8.5 %copy-start.3 = (bf16[128,2048]{1,0:T(8,128)(2,1)S(1)}, bf16[128,2048]{1,0:T(8,128)(2,1)}, u32[]{:S(2)}) copy-start(bf16[128,2048]{1,0:T(8,128)(2,1)} %v_ref.3) | copy-start | bytes 1572868
  4.8 13.7 %copy-start = (bf16[128,2048]{1,0:T(8,128)(2,1)S(1)}, bf16[128,2048]{1,0:T(8,128)(2,1)}, u32[]{:S(2)}) copy-start(bf16[128,2048]{1,0:T(8,128)(2,1)} %k_ref.5) | copy-start | bytes 1572868
  5.6 17.0 %all-to-all-start = ((bf16[16,64,128]{2,1,0:T(8,128)(2,1)}), bf16[16,64,128]{2,1,0:T(8,128)(2,1)S(1)}, u32[]{:S(2)}, u32[]{:S(2)}) async-start(bf16[16,64,128]{2,1,0:T(8,128)(2,1)} %bitcast.1), calls=%async_computation | async-start | bytes 524288 | tf_op jit(solution)/shard_map/all_to_all | solution.py:209
  13.3 5.2 %copy-start.6 = (f32[4,2048]{1,0:T(4,128)S(1)}, f32[4,2048]{1,0:T(4,128)}, u32[]{:S(2)}) copy-start(f32[4,2048]{1,0:T(4,128)} %w_ref.3) | copy-start | bytes 98308
  13.3 5.2 %collective-permute-start = (bf16[8,2048]{1,0:T(8,128)(2,1)S(1)}, bf16[8,2048]{1,0:T(8,128)(2,1)S(1)}, u32[]{:S(2)}, u32[]{:S(2)}) collective-permute-start(bf16[8,2048]{1,0:T(8,128)(2,1)S(1)} %slice.3), channel_id=1, source_target_pairs={{0,1},{1,2},{2,3},{3,4},{4,5},{5,6},{6,7},{7,8},{8,9},{9,10},{10,1... | collective-permute-start | bytes 98312 | tf_op jit(solution)/shard_map/ppermute | solution.py:206
  19.3 1.6 %collective-permute-start.2 = (bf16[8,128,128]{2,1,0:T(8,128)(2,1)S(1)}, bf16[8,128,128]{2,1,0:T(8,128)(2,1)S(1)}, u32[]{:S(2)}, u32[]{:S(2)}) collective-permute-start(bf16[8,128,128]{2,1,0:T(8,128)(2,1)S(1)} %get-tuple-element.24), channel_id=1, source_target_pairs={{0,1},{1,0},{2,3},{3,2},{4,5},{5,4},{6,7},{7,6},{8,9},{9,8},{10,11... | collective-permute-start | bytes 786440 | tf_op jit(solution)/shard_map/ppermute | solution.py:202
  44.3 3.1 %copy-start.2 = (bf16[128,2048]{1,0:T(8,128)(2,1)S(1)}, bf16[128,2048]{1,0:T(8,128)(2,1)}, u32[]{:S(2)}) copy-start(bf16[128,2048]{1,0:T(8,128)(2,1)} %g_ref.5) | copy-start | bytes 1572868
  44.3 3.1 %copy-start.5 = (bf16[128,2048]{1,0:T(8,128)(2,1)S(1)}, bf16[128,2048]{1,0:T(8,128)(2,1)}, u32[]{:S(2)}) copy-start(bf16[128,2048]{1,0:T(8,128)(2,1)} %q_ref.3) | copy-start | bytes 1572868
  44.4 2.9 %collective-permute-start.3 = (bf16[16,64,128]{2,1,0:T(8,128)(2,1)S(1)}, bf16[16,64,128]{2,1,0:T(8,128)(2,1)S(1)}, u32[]{:S(2)}, u32[]{:S(2)}) collective-permute-start(bf16[16,64,128]{2,1,0:T(8,128)(2,1)S(1)} %get-tuple-element.26), channel_id=1, source_target_pairs={{0,1},{1,0},{2,3},{3,2},{4,5},{5,4},{6,7},{7,6},{8,9},{9,8},{10,11... | collective-permute-start | bytes 786440 | tf_op jit(solution)/shard_map/ppermute | solution.py:202
  69.2 7.2 %collective-permute-start.4 = (bf16[16,64,128]{2,1,0:T(8,128)(2,1)S(1)}, bf16[16,64,128]{2,1,0:T(8,128)(2,1)S(1)}, u32[]{:S(2)}, u32[]{:S(2)}) collective-permute-start(bf16[16,64,128]{2,1,0:T(8,128)(2,1)S(1)} %get-tuple-element.29), channel_id=1, source_target_pairs={{0,1},{1,0},{2,3},{3,2},{4,5},{5,4},{6,7},{7,6},{8,9},{9,8},{10,11... | collective-permute-start | bytes 786440 | tf_op jit(solution)/shard_map/ppermute | solution.py:202
  70.8 5.6 %collective-permute-start.5 = (f32[8,2048]{1,0:T(8,128)S(1)}, f32[8,2048]{1,0:T(8,128)S(1)}, u32[]{:S(2)}, u32[]{:S(2)}) collective-permute-start(f32[8,2048]{1,0:T(8,128)S(1)} %get-tuple-element.31), channel_id=1, source_target_pairs={{1,0},{2,1},{3,2},{4,3},{5,4},{6,5},{7,6},{8,7},{9,8},{10,9},{11,1... | collective-permute-start | bytes 196616 | tf_op jit(solution)/shard_map/ppermute | solution.py:206
  72.8 3.6 %collective-permute-start.6 = (f32[64,128]{1,0:T(8,128)S(1)}, f32[64,128]{1,0:T(8,128)S(1)}, u32[]{:S(2)}, u32[]{:S(2)}) collective-permute-start(f32[64,128]{1,0:T(8,128)S(1)} %shard_map.90.taps_ref), channel_id=1, source_target_pairs={{0,1},{1,0},{2,3},{3,2},{4,5},{5,4},{6,7},{7,6},{8,9},{9,8},{10,11... | collective-permute-start | bytes 98312 | tf_op jit(solution)/shard_map/ppermute | solution.py:202

commit v2 on v0

v2 whole, which is shorter than its diff:
```python
import functools

import jax
import jax.numpy as jnp
from jax import lax
from jax.experimental import pallas as pl
from jax.experimental.pallas import tpu as pltpu
from jax.sharding import PartitionSpec as P

HEADS = 16
DH = 128
CW = 4
HALF = HEADS // 2
WIDE = HALF * DH
EDGE = 8
HALO = 16
AXES = ("row", "col")
F32 = jnp.float32
BF16 = jnp.bfloat16
VMEM = pl.BlockSpec(memory_space=pltpu.VMEM)
SMEM = pl.BlockSpec(memory_space=pltpu.SMEM)
ANY = pl.BlockSpec(memory_space=pl.ANY)
PARAMS = pltpu.CompilerParams(vmem_limit_bytes=48 * 1024 * 1024)


def dot(a, b, over):
    return lax.dot_general(a, b, ((over[:1], over[1:]), ((), ())), preferred_element_type=F32)


def columns(head):
    return pl.ds(head * DH, DH)


def half_of(core, size):
    return pl.ds(pl.multiple_of(core * size, size), size)


def call(kernel, outs, core, arrays, scratch=(), space=VMEM):
    return pl.pallas_call(
        kernel,
        out_shape=outs,
        in_specs=[SMEM] + [space] * len(arrays),
        out_specs=jax.tree.map(lambda _: VMEM, outs),
        scratch_shapes=scratch,
        compiler_params=PARAMS,
    )(core, *arrays)


def shape(dims, dtype=BF16):
    return jax.ShapeDtypeStruct(dims, dtype)


def split_kernel(core_ref, a_ref, b_ref, own_ref, send_ref, sems):
    core = core_ref[0]
    copies = []
    for n, ref in enumerate((a_ref, b_ref)):
        for m, (out, side) in enumerate(((send_ref, 1 - core), (own_ref, core))):
            copies.append(
                pltpu.make_async_copy(ref.at[:, half_of(side, WIDE)], out.at[n], sems.at[n, m])
            )
    for copy in copies:
        copy.start()
    for copy in copies:
        copy.wait()


def query_state_kernel(core_ref, own_ref, recv_ref, q_ref, g_ref, state_ref):
    core = core_ref[0]
    rows = own_ref.shape[1]
    for n, ref in enumerate((q_ref, g_ref)):
        ref[half_of(core, rows), :] = own_ref[n]
        ref[half_of(1 - core, rows), :] = recv_ref[n]
    for i in range(HALF):
        at = columns(i)
        state_ref[i] = dot(q_ref[:, at], g_ref[:, at], (0, 0)).astype(BF16)


def gather_kernel(core_ref, own_ref, recv_ref, k_ref, v_ref, tail_ref):
    core = core_ref[0]
    rows = own_ref.shape[1]
    for n, ref in enumerate((k_ref, v_ref)):
        ref[half_of(core, rows), :] = own_ref[n]
        ref[half_of(1 - core, rows), :] = recv_ref[n]
    tail_ref[...] = v_ref[2 * rows - HALO :, :]


def lagged(v_ref, halo_ref, at):
    ext = jnp.concatenate([halo_ref[:, at].astype(F32), v_ref[:, at].astype(F32)], axis=0)
    rows = v_ref.shape[0]
    return [ext[HALO - j : HALO - j + rows] for j in range(CW)]


def inner_kernel(
    core_ref,
    q_ref,
    g_ref,
    k_ref,
    v_ref,
    halo_ref,
    w_ref,
    qs_ref,
    c_ref,
    state_ref,
    gq_ref,
    gk_ref,
    gc_ref,
    edge_ref,
):
    core = core_ref[0]
    rows = q_ref.shape[0]
    first = lax.broadcasted_iota(jnp.int32, (rows, rows), 0)
    second = lax.broadcasted_iota(jnp.int32, (rows, rows), 1)
    for i in range(HALF):
        at = columns(i)
        taps = w_ref[:, pl.ds(pl.multiple_of(core * WIDE + i * DH, DH), DH)]
        parts = lagged(v_ref, halo_ref, at)
        acc = taps[0:1] * parts[0]
        for j in range(1, CW):
            acc = acc + taps[j : j + 1] * parts[j]
        c = acc.astype(BF16)
        c_ref[:, at] = c
        q, g, k = q_ref[:, at], g_ref[:, at], k_ref[:, at]
        state_ref[i] = dot(k, c, (0, 0)).astype(BF16)
        score = jnp.where(first <= second, dot(k, q, (1, 1)), 0.0).astype(BF16)
        turned = jnp.where(first <= second, dot(c, g, (1, 1)), 0.0).astype(BF16)
        attn = jnp.where(first >= second, dot(g, c, (1, 1)), 0.0).astype(BF16)
        gq_ref[:, at] = dot(attn, k, (1, 0))
        gk_ref[:, at] = dot(turned, q, (1, 0))
        gc = dot(score, g, (1, 0))
        gc_ref[:, at] = gc
        edge_ref[:EDGE, at] = (gc[:HALO] - dot(k[:HALO], qs_ref[i], (1, 0)))[:EDGE]
        edge_ref[EDGE:, at] = k[:HALO].astype(F32)[:EDGE]


def turn_kernel(core_ref, q_ref, state_ref, out_ref):
    total = jnp.zeros(q_ref.shape[1:], F32)
    for p in reversed(range(q_ref.shape[0])):
        out_ref[p, 0] = total.astype(BF16)
        total = total + q_ref[p].astype(F32)
        out_ref[p, 1] = state_ref[p]


def head_state(read, head, depth):
    parts = DH // depth
    if depth % HALO == 0:
        return jnp.concatenate([read(head * parts + n) for n in range(parts)], axis=0)
    found = [read(head * parts + n).astype(F32) for n in range(parts)]
    return jnp.concatenate(found, axis=0).astype(BF16)


def query_side_kernel(
    core_ref,
    chip_ref,
    k_ref,
    c_ref,
    v_ref,
    halo_ref,
    gk_ref,
    gc_ref,
    edge_ref,
    w_ref,
    own_ref,
    send_ref,
    out_ref,
    taps_ref,
    *,
    scale,
):
    core = core_ref[0]
    rows = k_ref.shape[0]
    chips, _, depth, _ = chip_ref.shape
    for i in range(HALF):
        at = columns(i)
        suffix = head_state(lambda p: chip_ref[p, 0], i, depth)
        gk = scale * (gk_ref[:, at] + dot(c_ref[:, at], suffix, (1, 1)))
        gc = scale * (gc_ref[:, at] + dot(k_ref[:, at], suffix, (1, 0)))
        after = dot(edge_ref[EDGE:, at].astype(BF16), suffix, (1, 0))
        ext = jnp.concatenate([gc, scale * (edge_ref[:EDGE, at] + after)], axis=0)
        taps = w_ref[:, pl.ds(pl.multiple_of(core * WIDE + i * DH, DH), DH)]
        gv = taps[0:1] * gc
        for j in range(1, CW):
            gv = gv + taps[j : j + 1] * ext[j : j + rows]
        for n, value in enumerate((gk, gv)):
            low, high = value[: rows // 2].astype(BF16), value[rows // 2 :].astype(BF16)
            own_ref[n, :, at] = jnp.where(core == 0, low, high)
            send_ref[n, :, at] = jnp.where(core == 0, high, low)
        for j, part in enumerate(lagged(v_ref, halo_ref, at)):
            taps_ref[j * HALF + i : j * HALF + i + 1, :] = jnp.sum(gc * part, axis=0, keepdims=True)
    total = jnp.zeros((depth, DH), F32)
    weights = taps_ref[...].astype(BF16)
    start = out_ref.shape[1] - CW * HALF
    for p in range(chips):
        out_ref[p, :depth] = total.astype(BF16)
        total = total + chip_ref[p, 1].astype(F32)
        out_ref[p, start:] = weights


def key_side_kernel(
    core_ref, chip_ref, g_ref, gq_ref, own_ref, send_ref, taps_ref, *, scale, depth
):
    core = core_ref[0]
    rows = g_ref.shape[0]
    chips, size, _ = chip_ref.shape
    for i in range(HALF):
        at = columns(i)
        prefix = head_state(lambda p: chip_ref[p, :depth], i, depth)
        gq = scale * (gq_ref[:, at] + dot(g_ref[:, at], prefix, (1, 1)))
        low, high = gq[: rows // 2].astype(BF16), gq[rows // 2 :].astype(BF16)
        own_ref[:, at] = jnp.where(core == 0, low, high)
        send_ref[:, at] = jnp.where(core == 0, high, low)
    total = chip_ref[0, size - CW * HALF :].astype(F32)
    for p in range(1, chips):
        total = total + chip_ref[p, size - CW * HALF :].astype(F32)
    taps_ref[...] = total


def join_kernel(core_ref, own_ref, recv_ref, a_ref, b_ref):
    core = core_ref[0]
    for n, ref in enumerate((a_ref, b_ref)):
        ref[:, half_of(core, WIDE)] = own_ref[n]
        ref[:, half_of(1 - core, WIDE)] = recv_ref[n]


def finish_kernel(core_ref, own_ref, recv_ref, taps_ref, far_ref, gq_ref, gw_ref):
    core = core_ref[0]
    gq_ref[:, half_of(core, WIDE)] = own_ref[...]
    gq_ref[:, half_of(1 - core, WIDE)] = recv_ref[...]
    for side, ref in ((core, taps_ref), (1 - core, far_ref)):
        for i in range(HALF):
            at = pl.ds(pl.multiple_of(side * WIDE + i * DH, DH), DH)
            for j in range(CW):
                row = j * HALF + i
                gw_ref[j : j + 1, at] = ref[row : row + 1, :]


def local(queries, keys, values, grad_out, conv_weight):
    rows, width = queries.shape
    count = lax.axis_size("row") * lax.axis_size("col")
    chips = count // 2
    depth = WIDE // chips
    scale = (DH * rows * count) ** (-0.5)
    core = lax.rem(lax.axis_index("col"), 2).astype(jnp.int32).reshape(1)
    groups = [[2 * p + c for p in range(chips)] for c in range(2)]

    def swap(value):
        return lax.ppermute(value, AXES, [(d, d ^ 1) for d in range(count)])

    def shifted(value, by):
        pairs = [(d, d + by) for d in range(count) if 0 <= d + by < count]
        return lax.ppermute(value, AXES, pairs)

    def turn(value):
        return lax.all_to_all(value, AXES, 0, 0, axis_index_groups=groups, tiled=True)

    pair = shape((2, rows, WIDE))
    block = shape((2 * rows, WIDE))
    block32 = shape((2 * rows, WIDE), F32)
    states = shape((HALF, DH, DH))
    sems = [pltpu.SemaphoreType.DMA((2, 2))]
    qg_own, qg_send = call(split_kernel, (pair, pair), core, [queries, grad_out], sems, ANY)
    qg_recv = swap(qg_send)
    kv_own, kv_send = call(split_kernel, (pair, pair), core, [keys, values], sems, ANY)
    kv_recv = swap(kv_send)
    q, g, q_state = call(query_state_kernel, (block, block, states), core, [qg_own, qg_recv])
    q_turned = turn(q_state.reshape(chips, depth, DH))
    k, v, tail = call(
        gather_kernel, (block, block, shape((HALO, WIDE))), core, [kv_own, kv_recv]
    )
    halo = shifted(tail, 2)
    c, k_state, gq, gk, gc, edge = call(
        inner_kernel,
        (block, states, block32, block32, block32, shape((2 * EDGE, WIDE), F32)),
        core,
        [q, g, k, v, halo, conv_weight, q_state],
    )
    edge = shifted(edge, -2)
    both = call(
        turn_kernel,
        shape((chips, 2, depth, DH)),
        core,
        [q_turned, k_state.reshape(chips, depth, DH)],
    )
    both = turn(both)
    kv_grad, kv_give, last = call(
        functools.partial(query_side_kernel, scale=scale),
        (pair, pair, shape((chips, max(depth, HALO) + CW * HALF, DH))),
        core,
        [both, k, c, v, halo, gk, gc, edge, conv_weight],
        [pltpu.VMEM((CW * HALF, DH), F32)],
    )
    kv_got = swap(kv_give)
    last = turn(last)
    q_grad, q_give, taps = call(
        functools.partial(key_side_kernel, scale=scale, depth=depth),
        (shape((rows, WIDE)), shape((rows, WIDE)), shape((CW * HALF, DH), F32)),
        core,
        [last, g, gq],
    )
    q_got = swap(q_give)
    far = swap(taps)
    full = shape((rows, width))
    grad_keys, grad_values = call(join_kernel, (full, full), core, [kv_grad, kv_got])
    grad_queries, grad_weight = call(
        finish_kernel, (full, shape((CW, width), F32)), core, [q_grad, q_got, taps, far]
    )
    return grad_queries, grad_keys, grad_values, grad_weight


def solution(mesh):
    placed = (
        P(("row", "col"), None),
        P(("row", "col"), None),
        P(("row", "col"), None),
        P(("row", "col"), None),
        P(),
    )
    return jax.shard_map(
        local,
        mesh=mesh,
        in_specs=placed,
        out_specs=(P(("row", "col"), None), P(("row", "col"), None), P(("row", "col"), None), P()),
        check_vma=False,
    )
```

time: 305 us -> 80.9 us (0.27)
  waiting for transfers between devices: 190 us -> 27.4 us
  blocking collectives: 43.2 us -> 0 us
  starting transfers between devices: 7.38 us -> 29.2 us
  other arithmetic: 21.6 us -> 0 us
  between operations: 14 us -> 0.78 us
  matrix products: 12.5 us -> 0 us
  Pallas kernels: 0 us -> 12.5 us
  local copies, waits for them, and re-layouts: 13.8 us -> 9.89 us
    all_gather x4 -> x0, waiting for transfers between devices: 130 us -> none  [entering(): gathered = lax.all_gather(value.astype(jnp.bfloat16), axis)]
    psum x1 -> x0, waiting for transfers between devices: 57.9 us -> none  [local(): lax.psum(key_state.astype(jnp.bfloat16), 'col').astype(jnp.float32)]
    psum x1 -> x0, blocking collectives: 43.2 us -> none  [local(): grad_weight = lax.psum(jnp.stack(weight_rows, axis=0), ('row', 'col'))]
    all_to_all x0 -> x3, starting transfers between devices: none -> 21.4 us  [turn(): lax.all_to_all(value, AXES, 0, 0, axis_index_groups=groups, tiled=True)]
    all_to_all x0 -> x3, waiting for transfers between devices: none -> 19 us  [turn(): lax.all_to_all(value, AXES, 0, 0, axis_index_groups=groups, tiled=True)]
    add x10 -> x0, other arithmetic: 17.7 us -> none  [add_states(): return earlier + later]
    dot_general x9 -> x0, matrix products: 12.5 us -> none  [the longest x1 2.67 us: local(): jnp.einsum('the,hde->thd', conv_heads, suffix_half, preferred_element_typ...]
    pallas_call x0 -> x10, Pallas kernels: none -> 12.5 us  [call(): pl.pallas_call(kernel, out_shape=outs, in_specs=[SMEM] + [space] * len(ar...]
  transfers between devices with their start and end apart: 7 -> 10, of which waited for: 6 -> 5; matrix products, arithmetic and copies ran while one was open for 14% -> 0% of each run, Pallas kernels for 0% -> 10%
where the time goes in v2:
time: 80.9 us; the launch traced here: 79.7 us
  starting transfers between devices  29.2 us (36%)
  waiting for transfers between devices  27.4 us (34%)
  Pallas kernels  12.5 us (15%)
  local copies, waits for them, and re-layouts  9.89 us (12%)
    all_to_all x3, starting transfers between devices, turn(): lax.all_to_all(value, AXES, 0, 0, axis_index_groups=groups, tiled=True)  21.4 us
    all_to_all x3, waiting for transfers between devices, turn(): lax.all_to_all(value, AXES, 0, 0, axis_index_groups=groups, tiled=True)  19 us
    pallas_call x10, Pallas kernels, call(): pl.pallas_call(kernel, out_shape=outs, in_specs=[SMEM] + [space] * len(ar...  12.5 us
    unnamed x32, local copies, waits for them, and re-layouts  9.89 us
    ppermute x2, waiting for transfers between devices, shifted(): return lax.ppermute(value, AXES, pairs)  8.27 us
    ppermute x2, starting transfers between devices, shifted(): return lax.ppermute(value, AXES, pairs)  4.69 us
    ppermute x5, starting transfers between devices, swap(): return lax.ppermute(value, AXES, [(d, d ^ 1) for d in range(count)])  3.13 us
  transfers between devices with their start and end apart: 10, of which 5 were waited for; matrix products, arithmetic and copies ran while one was open for 0% of the time, Pallas kernels for 10%

profile of v2, /device:TPU:1, one launch (start us, length us, event | category | flops | bytes accessed | tf_op | source)
XLA Modules:
  0.0 79.7 jit_solution(12698861550365275181)
XLA Ops:
  0.6 1.0 %copy-done.5 = bf16[128,2048]{1,0:T(8,128)(2,1)S(1)} copy-done((bf16[128,2048]{1,0:T(8,128)(2,1)S(1)}, bf16[128,2048]{1,0:T(8,128)(2,1)}, u32[]{:S(2)}) %copy-start.5) | copy-done | bytes 524312
  1.7 1.0 %copy-done.6 = bf16[128,2048]{1,0:T(8,128)(2,1)S(1)} copy-done((bf16[128,2048]{1,0:T(8,128)(2,1)S(1)}, bf16[128,2048]{1,0:T(8,128)(2,1)}, u32[]{:S(2)}) %copy-start.6) | copy-done | bytes 524312
  2.8 0.1 collective-permute-start
  3.0 0.8 copy-done.7
  3.8 0.2 copy-done.8
  3.9 0.9 %shard_map.86 = (bf16[2,128,1024]{2,1,0:T(8,128)(2,1)S(1)}, bf16[2,128,1024]{2,1,0:T(8,128)(2,1)}) custom-call(s32[1]{0:T(128)} %bitcast.core_ref, bf16[128,2048]{1,0:T(8,128)(2,1)S(1)} %copy-done.7, bf16[128,2048]{1,0:T(8,128)(2,1)S(1)} %copy-done.8), custom_call_target="tpu_custom_call" | custom-call | tf_op jit(solution)/shard_map/pallas_call | solution.py:39
  4.8 0.1 collective-permute-start.1
  5.0 1.1 %shard_map.85 = (bf16[256,1024]{1,0:T(8,128)(2,1)S(1)}, bf16[256,1024]{1,0:T(8,128)(2,1)S(1)}, bf16[8,128,128]{2,1,0:T(8,128)(2,1)}) custom-call(s32[1]{0:T(128)} %bitcast.core_ref, bf16[2,128,1024]{2,1,0:T(8,128)(2,1)S(1)} %get-tuple-element.30.own_ref, bf16[2,128,1024]{2,1,0:T(8,128)(2,1)S(1)} %collective-permute-done.recv_ref), custom_call_target="tpu_custom_call" | custom-call | tf_op jit(solution)/shard_map/pallas_call | solution.py:39
  6.1 8.0 %all-to-all-start = ((bf16[16,64,128]{2,1,0:T(8,128)(2,1)}), bf16[16,64,128]{2,1,0:T(8,128)(2,1)S(1)}, u32[]{:S(2)}, u32[]{:S(2)}) async-start(bf16[16,64,128]{2,1,0:T(8,128)(2,1)} %bitcast.1), calls=%async_computation | async-start | bytes 524288 | tf_op jit(solution)/shard_map/all_to_all | solution.py:253
  14.2 3.4 %collective-permute-start.2 = (bf16[16,1024]{1,0:T(8,128)(2,1)S(1)}, bf16[16,1024]{1,0:T(8,128)(2,1)S(1)}, u32[]{:S(2)}, u32[]{:S(2)}) collective-permute-start(bf16[16,1024]{1,0:T(8,128)(2,1)S(1)} %get-tuple-element.39), channel_id=1, source_target_pairs={{0,2},{1,3},{2,4},{3,5},{4,6},{5,7},{6,8},{7,9},{8,10},{9,11},{10,... | collective-permute-start | bytes 98312 | tf_op jit(solution)/shard_map/ppermute | solution.py:250
  17.6 1.6 %collective-permute-done.2.halo_ref = bf16[16,1024]{1,0:T(8,128)(2,1)S(1)} collective-permute-done((bf16[16,1024]{1,0:T(8,128)(2,1)S(1)}, bf16[16,1024]{1,0:T(8,128)(2,1)S(1)}, u32[]{:S(2)}, u32[]{:S(2)}) %collective-permute-start.2) | collective-permute-done | bytes 32800 | tf_op jit(solution)/shard_map/ppermute | solution.py:250
  19.2 4.7 %shard_map.88 = (bf16[256,1024]{1,0:T(8,128)(2,1)S(1)}, bf16[8,128,128]{2,1,0:T(8,128)(2,1)S(1)}, f32[256,1024]{1,0:T(8,128)S(1)}, f32[256,1024]{1,0:T(8,128)S(1...) custom-call(s32[1]{0:T(128)} %bitcast.core_ref, bf16[256,1024]{1,0:T(8,128)(2,1)S(1)} %copy-done.12, ...), custom_call_target="tpu_custom_call" | custom-call | tf_op jit(solution)/shard_map/pallas_call | solution.py:39
  24.0 1.0 %copy-done.1 = f32[256,1024]{1,0:T(8,128)} copy-done((f32[256,1024]{1,0:T(8,128)}, f32[256,1024]{1,0:T(8,128)S(1)}, u32[]{:S(2)}) %copy-start.1) | copy-done | bytes 1048600
  24.9 0.8 copy-done.3
  25.7 0.8 %shard_map.89 = bf16[16,2,64,128]{3,2,1,0:T(8,128)(2,1)} custom-call(s32[1]{0:T(128)} %bitcast.core_ref, bf16[16,64,128]{2,1,0:T(8,128)(2,1)S(1)} %all-to-all-done.q_ref, bf16[16,64,128]{2,1,0:T(8,128)(2,1)S(1)} %bitcast.3), custom_call_target="tpu_custom_call" | custom-call | tf_op jit(solution)/shard_map/pallas_call | solution.py:39
  26.6 8.2 %all-to-all-start.1 = ((bf16[16,2,64,128]{3,2,1,0:T(8,128)(2,1)}), bf16[16,2,64,128]{3,2,1,0:T(8,128)(2,1)S(1)}, u32[]{:S(2)}, u32[]{:S(2)}) async-start(bf16[16,2,64,128]{3,2,1,0:T(8,128)(2,1)} %shard_map.89), calls=%async_computation.1 | async-start | bytes 1048576 | tf_op jit(solution)/shard_map/all_to_all | solution.py:253
  34.8 1.3 %collective-permute-start.3 = (f32[16,1024]{1,0:T(8,128)S(1)}, f32[16,1024]{1,0:T(8,128)S(1)}, u32[]{:S(2)}, u32[]{:S(2)}) collective-permute-start(f32[16,1024]{1,0:T(8,128)S(1)} %get-tuple-element.44), channel_id=1, source_target_pairs={{2,0},{3,1},{4,2},{5,3},{6,4},{7,5},{8,6},{9,7},{10,8},{11,9},{12,... | collective-permute-start | bytes 196616 | tf_op jit(solution)/shard_map/ppermute | solution.py:250
  36.1 6.7 %collective-permute-done.3.edge_ref = f32[16,1024]{1,0:T(8,128)S(1)} collective-permute-done((f32[16,1024]{1,0:T(8,128)S(1)}, f32[16,1024]{1,0:T(8,128)S(1)}, u32[]{:S(2)}, u32[]{:S(2)}) %collective-permute-start.3) | collective-permute-done | bytes 65568 | tf_op jit(solution)/shard_map/ppermute | solution.py:250
  42.8 7.4 %all-to-all-done.1.chip_ref = bf16[16,2,64,128]{3,2,1,0:T(8,128)(2,1)S(1)} async-done(((bf16[16,2,64,128]{3,2,1,0:T(8,128)(2,1)}), bf16[16,2,64,128]{3,2,1,0:T(8,128)(2,1)S(1)}, u32[]{:S(2)}, u32[]{:S(2)}) %all-to-all-start.1) | async-done | bytes 524320 | tf_op jit(solution)/shard_map/all_to_all | solution.py:253
  50.2 1.2 %copy-done = f32[256,1024]{1,0:T(8,128)S(1)} copy-done((f32[256,1024]{1,0:T(8,128)S(1)}, f32[256,1024]{1,0:T(8,128)}, u32[]{:S(2)}) %copy-start) | copy-done | bytes 1048600
  51.4 1.0 %copy-done.4 = bf16[256,1024]{1,0:T(8,128)(2,1)S(1)} copy-done((bf16[256,1024]{1,0:T(8,128)(2,1)S(1)}, bf16[256,1024]{1,0:T(8,128)(2,1)}, u32[]{:S(2)}) %copy-start.4) | copy-done | bytes 524312
  52.5 2.5 %shard_map.90 = (bf16[2,128,1024]{2,1,0:T(8,128)(2,1)S(1)}, bf16[2,128,1024]{2,1,0:T(8,128)(2,1)S(1)}, bf16[16,96,128]{2,1,0:T(8,128)(2,1)}) custom-call(s32[1]{0:T(128)} %bitcast.core_ref, bf16[16,2,64,128]{3,2,1,0:T(8,128)(2,1)S(1)} %all-to-all-done.1.chip_ref, bf16[256,1024]{1,0:T(8,128)(2,1)S(1)} %get-tuple-element.37.k_ref, ...), custom_call_target="tpu_custom_call" | custom-call | tf_op jit(solution)/shard_map/pallas_call | solution.py:39
  54.9 0.8 copy-done.9
  55.7 0.8 copy-done.14
  56.5 5.2 %all-to-all-start.2 = ((bf16[16,96,128]{2,1,0:T(8,128)(2,1)}), bf16[16,96,128]{2,1,0:T(8,128)(2,1)S(1)}, u32[]{:S(2)}, u32[]{:S(2)}) async-start(bf16[16,96,128]{2,1,0:T(8,128)(2,1)} %get-tuple-element.45), calls=%async_computation.2 | async-start | bytes 786432 | tf_op jit(solution)/shard_map/all_to_all | solution.py:253
  61.7 1.0 %collective-permute-start.6 = (bf16[2,128,1024]{2,1,0:T(8,128)(2,1)S(1)}, bf16[2,128,1024]{2,1,0:T(8,128)(2,1)S(1)}, u32[]{:S(2)}, u32[]{:S(2)}) collective-permute-start(bf16[2,128,1024]{2,1,0:T(8,128)(2,1)S(1)} %copy-done.15), channel_id=1, source_target_pairs={{0,1},{1,0},{2,3},{3,2},{4,5},{5,4},{6,7},{7,6},{8,9},{9,8},{10,11... | collective-permute-start | bytes 1572872 | tf_op jit(solution)/shard_map/ppermute | solution.py:246
  62.7 11.6 %all-to-all-done.2.chip_ref = bf16[16,96,128]{2,1,0:T(8,128)(2,1)S(1)} async-done(((bf16[16,96,128]{2,1,0:T(8,128)(2,1)}), bf16[16,96,128]{2,1,0:T(8,128)(2,1)S(1)}, u32[]{:S(2)}, u32[]{:S(2)}) %all-to-all-start.2) | async-done | bytes 393248 | tf_op jit(solution)/shard_map/all_to_all | solution.py:253
  74.3 1.2 %copy-done.2 = f32[256,1024]{1,0:T(8,128)S(1)} copy-done((f32[256,1024]{1,0:T(8,128)S(1)}, f32[256,1024]{1,0:T(8,128)}, u32[]{:S(2)}) %copy-start.2) | copy-done | bytes 1048600
  75.5 0.3 shard_map.91
  75.9 1.8 %collective-permute-start.4 = (bf16[128,1024]{1,0:T(8,128)(2,1)S(1)}, bf16[128,1024]{1,0:T(8,128)(2,1)S(1)}, u32[]{:S(2)}, u32[]{:S(2)}) collective-permute-start(bf16[128,1024]{1,0:T(8,128)(2,1)S(1)} %get-tuple-element.48), channel_id=1, source_target_pairs={{0,1},{1,0},{2,3},{3,2},{4,5},{5,4},{6,7},{7,6},{8,9},{9,8},{10,11... | collective-permute-start | bytes 786440 | tf_op jit(solution)/shard_map/ppermute | solution.py:246
  77.8 1.0 %shard_map.93 = (bf16[128,2048]{1,0:T(8,128)(2,1)}, bf16[128,2048]{1,0:T(8,128)(2,1)}) custom-call(s32[1]{0:T(128)} %bitcast.core_ref, bf16[2,128,1024]{2,1,0:T(8,128)(2,1)S(1)} %copy-done.10, bf16[2,128,1024]{2,1,0:T(8,128)(2,1)S(1)} %collective-permute-done.6.recv_ref), custom_call_target="tpu_custom_call" | custom-call | tf_op jit(solution)/shard_map/pallas_call | solution.py:39
  78.9 0.9 %shard_map.92 = (bf16[128,2048]{1,0:T(8,128)(2,1)}, f32[4,2048]{1,0:T(4,128)}) custom-call(s32[1]{0:T(128)} %bitcast.core_ref, bf16[128,1024]{1,0:T(8,128)(2,1)S(1)} %get-tuple-element.47.own_ref, bf16[128,1024]{1,0:T(8,128)(2,1)S(1)} %collective-permute-done.4.recv_ref, f32[32,128]{1,0:T(8,128)S(1)} %get-tuple-element.49.taps_ref, ...), custom_call_target="tpu_custom_call" | custom-call | tf_op jit(solution)/shard_map/pallas_call | solution.py:39
  (30 shorter events, 0.4 us)
Async XLA Ops:
  0.6 1.0 %copy-start.5 = (bf16[128,2048]{1,0:T(8,128)(2,1)S(1)}, bf16[128,2048]{1,0:T(8,128)(2,1)}, u32[]{:S(2)}) copy-start(bf16[128,2048]{1,0:T(8,128)(2,1)} %a_ref.2) | copy-start | bytes 1572868
  1.7 1.0 %copy-start.6 = (bf16[128,2048]{1,0:T(8,128)(2,1)S(1)}, bf16[128,2048]{1,0:T(8,128)(2,1)}, u32[]{:S(2)}) copy-start(bf16[128,2048]{1,0:T(8,128)(2,1)} %b_ref.2) | copy-start | bytes 1572868
  2.7 1.0 %copy-start.7 = (bf16[128,2048]{1,0:T(8,128)(2,1)S(1)}, bf16[128,2048]{1,0:T(8,128)(2,1)}, u32[]{:S(2)}) copy-start(bf16[128,2048]{1,0:T(8,128)(2,1)} %a_ref.3) | copy-start | bytes 1572868
  2.7 1.2 %copy-start.8 = (bf16[128,2048]{1,0:T(8,128)(2,1)S(1)}, bf16[128,2048]{1,0:T(8,128)(2,1)}, u32[]{:S(2)}) copy-start(bf16[128,2048]{1,0:T(8,128)(2,1)} %b_ref.3) | copy-start | bytes 1572868
  2.8 2.1 %collective-permute-start = (bf16[2,128,1024]{2,1,0:T(8,128)(2,1)S(1)}, bf16[2,128,1024]{2,1,0:T(8,128)(2,1)S(1)}, u32[]{:S(2)}, u32[]{:S(2)}) collective-permute-start(bf16[2,128,1024]{2,1,0:T(8,128)(2,1)S(1)} %get-tuple-element.31), channel_id=1, source_target_pairs={{0,1},{1,0},{2,3},{3,2},{4,5},{5,4},{6,7},{7,6},{8,9},{9,8},{10,11... | collective-permute-start | bytes 1572872 | tf_op jit(solution)/shard_map/ppermute | solution.py:246
  4.8 9.3 %collective-permute-start.1 = (bf16[2,128,1024]{2,1,0:T(8,128)(2,1)}, bf16[2,128,1024]{2,1,0:T(8,128)(2,1)S(1)}, u32[]{:S(2)}, u32[]{:S(2)}) collective-permute-start(bf16[2,128,1024]{2,1,0:T(8,128)(2,1)} %get-tuple-element.36), channel_id=1, source_target_pairs={{0,1},{1,0},{2,3},{3,2},{4,5},{5,4},{6,7},{7,6},{8,9},{9,8},{10,11... | collective-permute-start | bytes 1572872 | tf_op jit(solution)/shard_map/ppermute | solution.py:246
  6.1 8.1 %copy-start.11 = (bf16[256,1024]{1,0:T(8,128)(2,1)}, bf16[256,1024]{1,0:T(8,128)(2,1)S(1)}, u32[]{:S(2)}) copy-start(bf16[256,1024]{1,0:T(8,128)(2,1)S(1)} %get-tuple-element.33.q_ref) | copy-start | bytes 1572868
  6.1 19.7 %all-to-all-start = ((bf16[16,64,128]{2,1,0:T(8,128)(2,1)}), bf16[16,64,128]{2,1,0:T(8,128)(2,1)S(1)}, u32[]{:S(2)}, u32[]{:S(2)}) async-start(bf16[16,64,128]{2,1,0:T(8,128)(2,1)} %bitcast.1), calls=%async_computation | async-start | bytes 524288 | tf_op jit(solution)/shard_map/all_to_all | solution.py:253
  14.1 5.1 %copy-start.12 = (bf16[256,1024]{1,0:T(8,128)(2,1)S(1)}, bf16[256,1024]{1,0:T(8,128)(2,1)}, u32[]{:S(2)}) copy-start(bf16[256,1024]{1,0:T(8,128)(2,1)} %copy-done.11) | copy-start | bytes 1572868
  14.1 5.1 %copy-start.13 = (f32[4,2048]{1,0:T(4,128)S(1)}, f32[4,2048]{1,0:T(4,128)}, u32[]{:S(2)}) copy-start(f32[4,2048]{1,0:T(4,128)} %w_ref.3) | copy-start | bytes 98308
  14.2 5.0 %collective-permute-start.2 = (bf16[16,1024]{1,0:T(8,128)(2,1)S(1)}, bf16[16,1024]{1,0:T(8,128)(2,1)S(1)}, u32[]{:S(2)}, u32[]{:S(2)}) collective-permute-start(bf16[16,1024]{1,0:T(8,128)(2,1)S(1)} %get-tuple-element.39), channel_id=1, source_target_pairs={{0,2},{1,3},{2,4},{3,5},{4,6},{5,7},{6,8},{7,9},{8,10},{9,11},{10,... | collective-permute-start | bytes 98312 | tf_op jit(solution)/shard_map/ppermute | solution.py:250
  24.0 1.0 %copy-start.1 = (f32[256,1024]{1,0:T(8,128)}, f32[256,1024]{1,0:T(8,128)S(1)}, u32[]{:S(2)}) copy-start(f32[256,1024]{1,0:T(8,128)S(1)} %get-tuple-element.46.gq_ref) | copy-start | bytes 3145732
  24.9 0.8 copy-start.3
  26.6 23.6 %all-to-all-start.1 = ((bf16[16,2,64,128]{3,2,1,0:T(8,128)(2,1)}), bf16[16,2,64,128]{3,2,1,0:T(8,128)(2,1)S(1)}, u32[]{:S(2)}, u32[]{:S(2)}) async-start(bf16[16,2,64,128]{3,2,1,0:T(8,128)(2,1)} %shard_map.89), calls=%async_computation.1 | async-start | bytes 1048576 | tf_op jit(solution)/shard_map/all_to_all | solution.py:253
  34.8 8.0 %collective-permute-start.3 = (f32[16,1024]{1,0:T(8,128)S(1)}, f32[16,1024]{1,0:T(8,128)S(1)}, u32[]{:S(2)}, u32[]{:S(2)}) collective-permute-start(f32[16,1024]{1,0:T(8,128)S(1)} %get-tuple-element.44), channel_id=1, source_target_pairs={{2,0},{3,1},{4,2},{5,3},{6,4},{7,5},{8,6},{9,7},{10,8},{11,9},{12,... | collective-permute-start | bytes 196616 | tf_op jit(solution)/shard_map/ppermute | solution.py:250
  50.2 1.2 %copy-start = (f32[256,1024]{1,0:T(8,128)S(1)}, f32[256,1024]{1,0:T(8,128)}, u32[]{:S(2)}) copy-start(f32[256,1024]{1,0:T(8,128)} %get-tuple-element.43.gc_ref) | copy-start | bytes 3145732
  51.4 1.0 %copy-start.4 = (bf16[256,1024]{1,0:T(8,128)(2,1)S(1)}, bf16[256,1024]{1,0:T(8,128)(2,1)}, u32[]{:S(2)}) copy-start(bf16[256,1024]{1,0:T(8,128)(2,1)} %copy-done.3) | copy-start | bytes 1572868
  54.9 0.8 copy-start.9
  55.7 0.8 copy-start.14
  56.5 5.2 %copy-start.15 = (bf16[2,128,1024]{2,1,0:T(8,128)(2,1)S(1)}, bf16[2,128,1024]{2,1,0:T(8,128)(2,1)}, u32[]{:S(2)}) copy-start(bf16[2,128,1024]{2,1,0:T(8,128)(2,1)} %copy-done.14) | copy-start | bytes 1572868
  56.5 17.8 %all-to-all-start.2 = ((bf16[16,96,128]{2,1,0:T(8,128)(2,1)}), bf16[16,96,128]{2,1,0:T(8,128)(2,1)S(1)}, u32[]{:S(2)}, u32[]{:S(2)}) async-start(bf16[16,96,128]{2,1,0:T(8,128)(2,1)} %get-tuple-element.45), calls=%async_computation.2 | async-start | bytes 786432 | tf_op jit(solution)/shard_map/all_to_all | solution.py:253
  61.7 16.0 %collective-permute-start.6 = (bf16[2,128,1024]{2,1,0:T(8,128)(2,1)S(1)}, bf16[2,128,1024]{2,1,0:T(8,128)(2,1)S(1)}, u32[]{:S(2)}, u32[]{:S(2)}) collective-permute-start(bf16[2,128,1024]{2,1,0:T(8,128)(2,1)S(1)} %copy-done.15), channel_id=1, source_target_pairs={{0,1},{1,0},{2,3},{3,2},{4,5},{5,4},{6,7},{7,6},{8,9},{9,8},{10,11... | collective-permute-start | bytes 1572872 | tf_op jit(solution)/shard_map/ppermute | solution.py:246
  74.3 1.2 %copy-start.2 = (f32[256,1024]{1,0:T(8,128)S(1)}, f32[256,1024]{1,0:T(8,128)}, u32[]{:S(2)}) copy-start(f32[256,1024]{1,0:T(8,128)} %copy-done.1) | copy-start | bytes 3145732
  75.5 2.2 %copy-start.10 = (bf16[2,128,1024]{2,1,0:T(8,128)(2,1)S(1)}, bf16[2,128,1024]{2,1,0:T(8,128)(2,1)}, u32[]{:S(2)}) copy-start(bf16[2,128,1024]{2,1,0:T(8,128)(2,1)} %copy-done.9) | copy-start | bytes 1572868
  75.9 3.0 %collective-permute-start.4 = (bf16[128,1024]{1,0:T(8,128)(2,1)S(1)}, bf16[128,1024]{1,0:T(8,128)(2,1)S(1)}, u32[]{:S(2)}, u32[]{:S(2)}) collective-permute-start(bf16[128,1024]{1,0:T(8,128)(2,1)S(1)} %get-tuple-element.48), channel_id=1, source_target_pairs={{0,1},{1,0},{2,3},{3,2},{4,5},{5,4},{6,7},{7,6},{8,9},{9,8},{10,11... | collective-permute-start | bytes 786440 | tf_op jit(solution)/shard_map/ppermute | solution.py:246
  77.7 1.2 %collective-permute-start.5 = (f32[32,128]{1,0:T(8,128)S(1)}, f32[32,128]{1,0:T(8,128)S(1)}, u32[]{:S(2)}, u32[]{:S(2)}) collective-permute-start(f32[32,128]{1,0:T(8,128)S(1)} %get-tuple-element.49.taps_ref), channel_id=1, source_target_pairs={{0,1},{1,0},{2,3},{3,2},{4,5},{5,4},{6,7},{7,6},{8,9},{9,8},{10,11... | collective-permute-start | bytes 49160 | tf_op jit(solution)/shard_map/ppermute | solution.py:246

commit v3 on v2

v3 whole, which is shorter than its diff:
```python
import functools

import jax
import jax.numpy as jnp
from jax import lax
from jax.experimental import pallas as pl
from jax.experimental.pallas import tpu as pltpu
from jax.sharding import PartitionSpec as P

HEADS = 16
DH = 128
CW = 4
HALF = HEADS // 2
WIDE = HALF * DH
EDGE = 8
HALO = 16
AXES = ("row", "col")
F32 = jnp.float32
BF16 = jnp.bfloat16
VMEM = pl.BlockSpec(memory_space=pltpu.VMEM)
SMEM = pl.BlockSpec(memory_space=pltpu.SMEM)
HBM = pl.BlockSpec(memory_space=pl.ANY)
PARAMS = pltpu.CompilerParams(vmem_limit_bytes=16 * 1024 * 1024)


def dot(a, b, over):
    return lax.dot_general(a, b, ((over[:1], over[1:]), ((), ())), preferred_element_type=F32)


def columns(head):
    return pl.ds(head * DH, DH)


def half_of(core, size):
    return pl.ds(pl.multiple_of(core * size, size), size)


def call(kernel, outs, core, arrays, scratch=(), space=VMEM):
    return pl.pallas_call(
        kernel,
        out_shape=outs,
        in_specs=[SMEM] + [space] * len(arrays),
        out_specs=jax.tree.map(lambda _: VMEM, outs),
        scratch_shapes=scratch,
        compiler_params=PARAMS,
    )(core, *arrays)


def shape(dims, dtype=BF16):
    return jax.ShapeDtypeStruct(dims, dtype)


def split_kernel(core_ref, a_ref, b_ref, own_ref, send_ref, sems):
    core = core_ref[0]
    copies = []
    for n, ref in enumerate((a_ref, b_ref)):
        for m, (out, side) in enumerate(((send_ref, 1 - core), (own_ref, core))):
            copies.append(
                pltpu.make_async_copy(ref.at[:, half_of(side, WIDE)], out.at[n], sems.at[n, m])
            )
    for copy in copies:
        copy.start()
    for copy in copies:
        copy.wait()


def gather(core, own_ref, recv_ref, refs):
    rows = own_ref.shape[1]
    for n, ref in enumerate(refs):
        ref[half_of(core, rows), :] = own_ref[n]
        ref[half_of(1 - core, rows), :] = recv_ref[n]


def query_state_kernel(core_ref, own_ref, recv_ref, q_ref, g_ref, state_ref):
    gather(core_ref[0], own_ref, recv_ref, (q_ref, g_ref))
    for i in range(HALF):
        at = columns(i)
        state_ref[i] = dot(q_ref[:, at], g_ref[:, at], (0, 0)).astype(BF16)


def gather_kernel(core_ref, own_ref, recv_ref, k_ref, v_ref, tail_ref):
    gather(core_ref[0], own_ref, recv_ref, (k_ref, v_ref))
    tail_ref[...] = v_ref[v_ref.shape[0] - HALO :, :]


def lagged(v_ref, halo_ref, at):
    ext = jnp.concatenate([halo_ref[:, at].astype(F32), v_ref[:, at].astype(F32)], axis=0)
    rows = v_ref.shape[0]
    return [ext[HALO - j : HALO - j + rows] for j in range(CW)]


def tap_rows(w_ref, core, head):
    return w_ref[:, pl.ds(pl.multiple_of(core * WIDE + head * DH, DH), DH)]


def later(rows):
    first = lax.broadcasted_iota(jnp.int32, (rows, rows), 0)
    return first <= lax.broadcasted_iota(jnp.int32, (rows, rows), 1)


def score_kernel(core_ref, q_ref, g_ref, k_ref, state_ref, gc_ref, edge_ref):
    seen = later(q_ref.shape[0])
    for i in range(HALF):
        at = columns(i)
        k = k_ref[:, at]
        score = jnp.where(seen, dot(k, q_ref[:, at], (1, 1)), 0.0).astype(BF16)
        gc = dot(score, g_ref[:, at], (1, 0))
        gc_ref[:, at] = gc.astype(BF16)
        edge = gc[:HALO] - dot(k[:HALO], state_ref[i], (1, 0))
        both = jnp.concatenate([edge[:EDGE], k[:HALO].astype(F32)[:EDGE]], axis=0)
        edge_ref[:, at] = both.astype(BF16)


def conv_kernel(core_ref, k_ref, v_ref, halo_ref, w_ref, c_ref, state_ref):
    for i in range(HALF):
        at = columns(i)
        taps = tap_rows(w_ref, core_ref[0], i)
        parts = lagged(v_ref, halo_ref, at)
        acc = taps[0:1] * parts[0]
        for j in range(1, CW):
            acc = acc + taps[j : j + 1] * parts[j]
        c = acc.astype(BF16)
        c_ref[:, at] = c
        state_ref[i] = dot(k_ref[:, at], c, (0, 0)).astype(BF16)


def turn_kernel(core_ref, q_ref, state_ref, out_ref, done_ref, *, order):
    total = jnp.zeros(q_ref.shape[1:], F32)
    for n in reversed(order):
        out_ref[n, 0] = total.astype(BF16)
        total = total + q_ref[n].astype(F32)
        out_ref[n, 1] = state_ref[n]
    done_ref[...] = jnp.zeros(done_ref.shape, F32)


def attn_kernel(core_ref, q_ref, g_ref, k_ref, c_ref, done_ref, gq_ref, gk_ref):
    seen = later(q_ref.shape[0])
    for i in range(HALF):
        at = columns(i)
        c, g = c_ref[:, at], g_ref[:, at]
        turned = jnp.where(seen, dot(c, g, (1, 1)), 0.0)
        gk_ref[:, at] = dot(turned.astype(BF16), q_ref[:, at], (1, 0)).astype(BF16)
        attn = jnp.where(seen.T, dot(g, c, (1, 1)), 0.0)
        gq_ref[:, at] = dot(attn.astype(BF16), k_ref[:, at], (1, 0)).astype(BF16)


def head_state(read, head, depth):
    parts = DH // depth
    if depth % HALO == 0:
        return jnp.concatenate([read(head * parts + n) for n in range(parts)], axis=0)
    found = [read(head * parts + n).astype(F32) for n in range(parts)]
    return jnp.concatenate(found, axis=0).astype(BF16)


def tap_kernel(
    core_ref, chip_ref, k_ref, gc_ref, v_ref, halo_ref, out_ref, done_ref, taps_ref, *, scale, order
):
    depth = chip_ref.shape[2]
    for i in range(HALF):
        at = columns(i)
        suffix = head_state(lambda n: chip_ref[n, 0], i, depth)
        gc = scale * (gc_ref[:, at].astype(F32) + dot(k_ref[:, at], suffix, (1, 0)))
        for j, part in enumerate(lagged(v_ref, halo_ref, at)):
            row = j * HALF + i
            taps_ref[row : row + 1, :] = jnp.sum(gc * part, axis=0, keepdims=True)
    total = jnp.zeros((depth, DH), F32)
    weights = taps_ref[...].astype(BF16)
    start = out_ref.shape[1] - CW * HALF
    for n in order:
        out_ref[n, :depth] = total.astype(BF16)
        total = total + chip_ref[n, 1].astype(F32)
        out_ref[n, start:] = weights
    done_ref[...] = jnp.zeros(done_ref.shape, F32)


def query_side_kernel(
    core_ref,
    chip_ref,
    k_ref,
    c_ref,
    gk_ref,
    gc_ref,
    edge_ref,
    w_ref,
    done_ref,
    own_ref,
    send_ref,
    *,
    scale,
):
    core = core_ref[0]
    rows = k_ref.shape[0]
    depth = chip_ref.shape[2]
    for i in range(HALF):
        at = columns(i)
        suffix = head_state(lambda n: chip_ref[n, 0], i, depth)
        gk = scale * (gk_ref[:, at].astype(F32) + dot(c_ref[:, at], suffix, (1, 1)))
        gc = scale * (gc_ref[:, at].astype(F32) + dot(k_ref[:, at], suffix, (1, 0)))
        edge = edge_ref[:, at]
        after = dot(edge, suffix, (1, 0))[EDGE:] + edge.astype(F32)[:EDGE]
        ext = jnp.concatenate([gc, scale * after], axis=0)
        taps = tap_rows(w_ref, core, i)
        gv = taps[0:1] * gc
        for j in range(1, CW):
            gv = gv + taps[j : j + 1] * ext[j : j + rows]
        for n, value in enumerate((gk, gv)):
            low, high = value[: rows // 2].astype(BF16), value[rows // 2 :].astype(BF16)
            own_ref[n, :, at] = jnp.where(core == 0, low, high)
            send_ref[n, :, at] = jnp.where(core == 0, high, low)


def key_side_kernel(
    core_ref, chip_ref, g_ref, gq_ref, own_ref, send_ref, taps_ref, *, scale, depth
):
    core = core_ref[0]
    rows = g_ref.shape[0]
    chips, size, _ = chip_ref.shape
    for i in range(HALF):
        at = columns(i)
        prefix = head_state(lambda n: chip_ref[n, :depth], i, depth)
        gq = scale * (gq_ref[:, at].astype(F32) + dot(g_ref[:, at], prefix, (1, 1)))
        low, high = gq[: rows // 2].astype(BF16), gq[rows // 2 :].astype(BF16)
        own_ref[:, at] = jnp.where(core == 0, low, high)
        send_ref[:, at] = jnp.where(core == 0, high, low)
    total = chip_ref[0, size - CW * HALF :].astype(F32)
    for n in range(1, chips):
        total = total + chip_ref[n, size - CW * HALF :].astype(F32)
    taps_ref[...] = total


def join_kernel(core_ref, own_ref, recv_ref, a_ref, b_ref):
    core = core_ref[0]
    for n, ref in enumerate((a_ref, b_ref)):
        ref[:, half_of(core, WIDE)] = own_ref[n]
        ref[:, half_of(1 - core, WIDE)] = recv_ref[n]


def finish_kernel(core_ref, own_ref, recv_ref, taps_ref, far_ref, gq_ref, gw_ref):
    core = core_ref[0]
    gq_ref[:, half_of(core, WIDE)] = own_ref[...]
    gq_ref[:, half_of(1 - core, WIDE)] = recv_ref[...]
    for side, ref in ((core, taps_ref), (1 - core, far_ref)):
        for i in range(HALF):
            at = pl.ds(pl.multiple_of(side * WIDE + i * DH, DH), DH)
            for j in range(CW):
                row = j * HALF + i
                gw_ref[j : j + 1, at] = ref[row : row + 1, :]


def local(queries, keys, values, grad_out, conv_weight):
    rows, width = queries.shape
    lines, line = lax.axis_size("row"), lax.axis_size("col") // 2
    count = 2 * lines * line
    chips = lines * line
    depth = WIDE // chips
    scale = (DH * rows * count) ** (-0.5)
    core = lax.rem(lax.axis_index("col"), 2).astype(jnp.int32).reshape(1)
    listed = [r * line + (z + line // 2) % line for z in range(line) for r in range(lines)]
    groups = [[2 * p + c for p in listed] for c in range(2)]
    order = tuple(listed.index(p) for p in range(chips))

    def swap(value):
        return lax.ppermute(value, AXES, [(d, d ^ 1) for d in range(count)])

    def shifted(value, by):
        pairs = [(d, d + by) for d in range(count) if 0 <= d + by < count]
        return lax.ppermute(value, AXES, pairs)

    def turn(value):
        return lax.all_to_all(value, AXES, 0, 0, axis_index_groups=groups, tiled=True)

    def split(*arrays):
        arrays = [pltpu.with_memory_space_constraint(a, pltpu.HBM) for a in arrays]
        sems = [pltpu.SemaphoreType.DMA((2, 2))]
        return call(split_kernel, (pair, pair), core, arrays, sems, HBM)

    pair = shape((2, rows, WIDE))
    block = shape((2 * rows, WIDE))
    states = shape((HALF, DH, DH))
    edges = shape((HALO, WIDE))
    flag = shape((8, DH), F32)
    qg_own, qg_send = split(queries, grad_out)
    qg_recv = swap(qg_send)
    kv_own, kv_send = split(keys, values)
    kv_recv = swap(kv_send)
    q, g, q_state = call(query_state_kernel, (block, block, states), core, [qg_own, qg_recv])
    q_turned = turn(q_state.reshape(chips, depth, DH))
    k, v, tail = call(gather_kernel, (block, block, edges), core, [kv_own, kv_recv])
    halo = shifted(tail, 2)
    gc, edge = call(score_kernel, (block, edges), core, [q, g, k, q_state])
    c, k_state = call(conv_kernel, (block, states), core, [k, v, halo, conv_weight])
    both, turned = call(
        functools.partial(turn_kernel, order=order),
        (shape((chips, 2, depth, DH)), flag),
        core,
        [q_turned, k_state.reshape(chips, depth, DH)],
    )
    both = turn(both)
    edge = shifted(edge, -2)
    gq, gk = call(attn_kernel, (block, block), core, [q, g, k, c, turned])
    last, tapped = call(
        functools.partial(tap_kernel, scale=scale, order=order),
        (shape((chips, max(depth, HALO) + CW * HALF, DH)), flag),
        core,
        [both, k, gc, v, halo],
        [pltpu.VMEM((CW * HALF, DH), F32)],
    )
    last = turn(last)
    kv_grad, kv_give = call(
        functools.partial(query_side_kernel, scale=scale),
        (pair, pair),
        core,
        [both, k, c, gk, gc, edge, conv_weight, tapped],
    )
    kv_got = swap(kv_give)
    q_grad, q_give, taps = call(
        functools.partial(key_side_kernel, scale=scale, depth=depth),
        (shape((rows, WIDE)), shape((rows, WIDE)), shape((CW * HALF, DH), F32)),
        core,
        [last, g, gq],
    )
    q_got = swap(q_give)
    far = swap(taps)
    full = shape((rows, width))
    grad_keys, grad_values = call(join_kernel, (full, full), core, [kv_grad, kv_got])
    grad_queries, grad_weight = call(
        finish_kernel, (full, shape((CW, width), F32)), core, [q_grad, q_got, taps, far]
    )
    return grad_queries, grad_keys, grad_values, grad_weight


def solution(mesh):
    placed = (
        P(("row", "col"), None),
        P(("row", "col"), None),
        P(("row", "col"), None),
        P(("row", "col"), None),
        P(),
    )
    return jax.shard_map(
        local,
        mesh=mesh,
        in_specs=placed,
        out_specs=(P(("row", "col"), None), P(("row", "col"), None), P(("row", "col"), None), P()),
        check_vma=False,
    )
```

time: 80.9 us -> 63.6 us (0.79)
  waiting for transfers between devices: 27.4 us -> 11.5 us
  local copies, waits for them, and re-layouts: 9.89 us -> 4.22 us
  Pallas kernels: 12.5 us -> 15 us
  starting transfers between devices: 29.2 us -> 31.2 us
    all_to_all x3, waiting for transfers between devices: 19 us -> 6.53 us  [turn(): lax.all_to_all(value, AXES, 0, 0, axis_index_groups=groups, tiled=True)]
    unnamed x32 -> x18, local copies, waits for them, and re-layouts: 9.89 us -> 4.22 us
    ppermute x2, waiting for transfers between devices: 8.27 us -> 4.18 us  [shifted(): return lax.ppermute(value, AXES, pairs)]
    pallas_call x10 -> x13, Pallas kernels: 12.5 us -> 15 us  [call(): pl.pallas_call(kernel, out_shape=outs, in_specs=[SMEM] + [space] * len(ar...]
    all_to_all x3, starting transfers between devices: 21.4 us -> 23.1 us  [turn(): lax.all_to_all(value, AXES, 0, 0, axis_index_groups=groups, tiled=True)]
    ppermute x5, starting transfers between devices: 3.13 us -> 4.66 us  [swap(): return lax.ppermute(value, AXES, [(d, d ^ 1) for d in range(count)])]
    ppermute x2, starting transfers between devices: 4.69 us -> 3.47 us  [shifted(): return lax.ppermute(value, AXES, pairs)]
  transfers between devices with their start and end apart: 10 -> 10, of which waited for: 5 -> 5; matrix products, arithmetic and copies ran while one was open for 0% -> 0% of each run, Pallas kernels for 10% -> 18%
where the time goes in v3:
time: 63.6 us; the launch traced here: 62.7 us
  starting transfers between devices  31.2 us (49%)
  Pallas kernels  15 us (24%)
  waiting for transfers between devices  11.5 us (18%)
  local copies, waits for them, and re-layouts  4.22 us (7%)
  between operations  0.76 us (1%)
    all_to_all x3, starting transfers between devices, turn(): lax.all_to_all(value, AXES, 0, 0, axis_index_groups=groups, tiled=True)  23.1 us
    pallas_call x13, Pallas kernels, call(): pl.pallas_call(kernel, out_shape=outs, in_specs=[SMEM] + [space] * len(ar...  15 us
    all_to_all x3, waiting for transfers between devices, turn(): lax.all_to_all(value, AXES, 0, 0, axis_index_groups=groups, tiled=True)  6.53 us
    ppermute x5, starting transfers between devices, swap(): return lax.ppermute(value, AXES, [(d, d ^ 1) for d in range(count)])  4.66 us
    unnamed x18, local copies, waits for them, and re-layouts  4.22 us
    ppermute x2, waiting for transfers between devices, shifted(): return lax.ppermute(value, AXES, pairs)  4.18 us
    ppermute x2, starting transfers between devices, shifted(): return lax.ppermute(value, AXES, pairs)  3.47 us
  transfers between devices with their start and end apart: 10, of which 5 were waited for; matrix products, arithmetic and copies ran while one was open for 0% of the time, Pallas kernels for 18%

profile of v3, /device:TPU:1, one launch (start us, length us, event | category | flops | bytes accessed | tf_op | source)
XLA Modules:
  0.0 62.7 jit_solution(426210601109274003)
XLA Ops:
  0.6 1.2 %shard_map.84 = (bf16[2,128,1024]{2,1,0:T(8,128)(2,1)S(1)}, bf16[2,128,1024]{2,1,0:T(8,128)(2,1)S(1)}) custom-call(s32[1]{0:T(128)} %bitcast.core_ref, bf16[128,2048]{1,0:T(8,128)(2,1)} %a_ref.2, bf16[128,2048]{1,0:T(8,128)(2,1)} %b_ref.2), custom_call_target="tpu_custom_call" | custom-call | tf_op jit(solution)/shard_map/pallas_call | solution.py:39
  1.9 0.1 collective-permute-start
  2.0 2.0 %shard_map.86 = (bf16[2,128,1024]{2,1,0:T(8,128)(2,1)S(1)}, bf16[2,128,1024]{2,1,0:T(8,128)(2,1)}) custom-call(s32[1]{0:T(128)} %bitcast.core_ref, bf16[128,2048]{1,0:T(8,128)(2,1)} %a_ref.3, bf16[128,2048]{1,0:T(8,128)(2,1)} %b_ref.3), custom_call_target="tpu_custom_call" | custom-call | tf_op jit(solution)/shard_map/pallas_call | solution.py:39
  4.0 0.5 collective-permute-start.1
  4.5 1.1 %shard_map.85 = (bf16[256,1024]{1,0:T(8,128)(2,1)S(1)}, bf16[256,1024]{1,0:T(8,128)(2,1)S(1)}, bf16[8,128,128]{2,1,0:T(8,128)(2,1)}) custom-call(s32[1]{0:T(128)} %bitcast.core_ref, bf16[2,128,1024]{2,1,0:T(8,128)(2,1)S(1)} %get-tuple-element.33.own_ref, bf16[2,128,1024]{2,1,0:T(8,128)(2,1)S(1)} %collective-permute-done.recv_ref), custom_call_target="tpu_custom_call" | custom-call | tf_op jit(solution)/shard_map/pallas_call | solution.py:39
  5.6 7.8 %all-to-all-start = ((bf16[16,64,128]{2,1,0:T(8,128)(2,1)}), bf16[16,64,128]{2,1,0:T(8,128)(2,1)S(1)}, u32[]{:S(2)}, u32[]{:S(2)}) async-start(bf16[16,64,128]{2,1,0:T(8,128)(2,1)} %bitcast.1), calls=%async_computation | async-start | bytes 524288 | tf_op jit(solution)/shard_map/all_to_all | solution.py:270
  13.4 0.1 shard_map.87
  13.5 2.2 %collective-permute-start.2 = (bf16[16,1024]{1,0:T(8,128)(2,1)S(1)}, bf16[16,1024]{1,0:T(8,128)(2,1)S(1)}, u32[]{:S(2)}, u32[]{:S(2)}) collective-permute-start(bf16[16,1024]{1,0:T(8,128)(2,1)S(1)} %get-tuple-element.40), channel_id=1, source_target_pairs={{0,2},{1,3},{2,4},{3,5},{4,6},{5,7},{6,8},{7,9},{8,10},{9,11},{10,... | collective-permute-start | bytes 98312 | tf_op jit(solution)/shard_map/ppermute | solution.py:267
  15.7 2.1 %collective-permute-done.2.halo_ref = bf16[16,1024]{1,0:T(8,128)(2,1)S(1)} collective-permute-done((bf16[16,1024]{1,0:T(8,128)(2,1)S(1)}, bf16[16,1024]{1,0:T(8,128)(2,1)S(1)}, u32[]{:S(2)}, u32[]{:S(2)}) %collective-permute-start.2) | collective-permute-done | bytes 32800 | tf_op jit(solution)/shard_map/ppermute | solution.py:267
  17.8 0.8 %shard_map.88 = (bf16[256,1024]{1,0:T(8,128)(2,1)S(1)}, bf16[8,128,128]{2,1,0:T(8,128)(2,1)S(1)}) custom-call(s32[1]{0:T(128)} %bitcast.core_ref, bf16[256,1024]{1,0:T(8,128)(2,1)S(1)} %get-tuple-element.38.k_ref, bf16[256,1024]{1,0:T(8,128)(2,1)S(1)} %get-tuple-element.39.v_ref, bf16[16,1024]{1,0:T(8,128)(2,1)S(1)} %collective-permute-done.2.halo_ref, ...), custom_call_target="tpu_custom_call" | custom-call | tf_op jit(solution)/shard_map/pallas_call | solution.py:39
  18.6 1.0 %all-to-all-done.q_ref = bf16[16,64,128]{2,1,0:T(8,128)(2,1)S(1)} async-done(((bf16[16,64,128]{2,1,0:T(8,128)(2,1)}), bf16[16,64,128]{2,1,0:T(8,128)(2,1)S(1)}, u32[]{:S(2)}, u32[]{:S(2)}) %all-to-all-start) | async-done | bytes 262176 | tf_op jit(solution)/shard_map/all_to_all | solution.py:270
  19.7 0.8 %copy-done.5 = bf16[16,2,64,128]{3,2,1,0:T(8,128)(2,1)} copy-done((bf16[16,2,64,128]{3,2,1,0:T(8,128)(2,1)}, bf16[16,2,64,128]{3,2,1,0:T(8,128)(2,1)S(1)}, u32[]{:S(2)}) %copy-start.5) | copy-done | bytes 524312
  20.5 7.6 %all-to-all-start.1 = ((bf16[16,2,64,128]{3,2,1,0:T(8,128)(2,1)}), bf16[16,2,64,128]{3,2,1,0:T(8,128)(2,1)S(1)}, u32[]{:S(2)}, u32[]{:S(2)}) async-start(bf16[16,2,64,128]{3,2,1,0:T(8,128)(2,1)} %copy-done.5), calls=%async_computation.1 | async-start | bytes 1048576 | tf_op jit(solution)/shard_map/all_to_all | solution.py:270
  28.0 2.5 %shard_map.90 = (bf16[256,1024]{1,0:T(8,128)(2,1)S(1)}, bf16[16,1024]{1,0:T(8,128)(2,1)S(1)}) custom-call(s32[1]{0:T(128)} %bitcast.core_ref, bf16[256,1024]{1,0:T(8,128)(2,1)S(1)} %get-tuple-element.43.q_ref, bf16[256,1024]{1,0:T(8,128)(2,1)S(1)} %get-tuple-element.44.g_ref, bf16[256,1024]{1,0:T(8,128)(2,1)S(1)} %get-tuple-element.38.k_ref, ...), custom_call_target="tpu_custom_call" | custom-call | tf_op jit(solution)/shard_map/pallas_call | solution.py:39
  30.5 0.8 %copy-done = bf16[256,1024]{1,0:T(8,128)(2,1)} copy-done((bf16[256,1024]{1,0:T(8,128)(2,1)}, bf16[256,1024]{1,0:T(8,128)(2,1)S(1)}, u32[]{:S(2)}) %copy-start) | copy-done | bytes 524312
  31.3 5.5 %all-to-all-done.1.chip_ref = bf16[16,2,64,128]{3,2,1,0:T(8,128)(2,1)S(1)} async-done(((bf16[16,2,64,128]{3,2,1,0:T(8,128)(2,1)}), bf16[16,2,64,128]{3,2,1,0:T(8,128)(2,1)S(1)}, u32[]{:S(2)}, u32[]{:S(2)}) %all-to-all-start.1) | async-done | bytes 524320 | tf_op jit(solution)/shard_map/all_to_all | solution.py:270
  36.9 1.0 %copy-done.1 = bf16[256,1024]{1,0:T(8,128)(2,1)S(1)} copy-done((bf16[256,1024]{1,0:T(8,128)(2,1)S(1)}, bf16[256,1024]{1,0:T(8,128)(2,1)}, u32[]{:S(2)}) %copy-start.1) | copy-done | bytes 524312
  37.9 1.6 %shard_map.91 = (bf16[16,96,128]{2,1,0:T(8,128)(2,1)}, f32[8,128]{1,0:T(8,128)S(1)}) custom-call(s32[1]{0:T(128)} %bitcast.core_ref, bf16[16,2,64,128]{3,2,1,0:T(8,128)(2,1)S(1)} %all-to-all-done.1.chip_ref, bf16[256,1024]{1,0:T(8,128)(2,1)S(1)} %get-tuple-element.38.k_ref, bf16[256,1024]{1,0:T(8,128)(2,1)S(1)} %copy-done.1, ...), custom_call_target="tpu_custom_call" | custom-call | tf_op jit(solution)/shard_map/pallas_call | solution.py:39
  39.5 7.7 %all-to-all-start.2 = ((bf16[16,96,128]{2,1,0:T(8,128)(2,1)}), bf16[16,96,128]{2,1,0:T(8,128)(2,1)S(1)}, u32[]{:S(2)}, u32[]{:S(2)}) async-start(bf16[16,96,128]{2,1,0:T(8,128)(2,1)} %get-tuple-element.46), calls=%async_computation.2 | async-start | bytes 786432 | tf_op jit(solution)/shard_map/all_to_all | solution.py:270
  47.2 1.3 %collective-permute-start.5 = (bf16[16,1024]{1,0:T(8,128)(2,1)S(1)}, bf16[16,1024]{1,0:T(8,128)(2,1)S(1)}, u32[]{:S(2)}, u32[]{:S(2)}) collective-permute-start(bf16[16,1024]{1,0:T(8,128)(2,1)S(1)} %get-tuple-element.55), channel_id=1, source_target_pairs={{2,0},{3,1},{4,2},{5,3},{6,4},{7,5},{8,6},{9,7},{10,8},{11,9},{12,... | collective-permute-start | bytes 98312 | tf_op jit(solution)/shard_map/ppermute | solution.py:267
  48.5 1.5 %shard_map.92 = (bf16[256,1024]{1,0:T(8,128)(2,1)S(1)}, bf16[256,1024]{1,0:T(8,128)(2,1)S(1)}) custom-call(s32[1]{0:T(128)} %bitcast.core_ref, bf16[256,1024]{1,0:T(8,128)(2,1)S(1)} %get-tuple-element.43.q_ref, bf16[256,1024]{1,0:T(8,128)(2,1)S(1)} %get-tuple-element.44.g_ref, bf16[256,1024]{1,0:T(8,128)(2,1)S(1)} %get-tuple-element.38.k_ref, ...), custom_call_target="tpu_custom_call" | custom-call | tf_op jit(solution)/shard_map/pallas_call | solution.py:39
  50.0 0.8 %copy-done.3 = bf16[256,1024]{1,0:T(8,128)(2,1)} copy-done((bf16[256,1024]{1,0:T(8,128)(2,1)}, bf16[256,1024]{1,0:T(8,128)(2,1)S(1)}, u32[]{:S(2)}) %copy-start.3) | copy-done | bytes 524312
  50.8 2.1 %collective-permute-done.5.edge_ref = bf16[16,1024]{1,0:T(8,128)(2,1)S(1)} collective-permute-done((bf16[16,1024]{1,0:T(8,128)(2,1)S(1)}, bf16[16,1024]{1,0:T(8,128)(2,1)S(1)}, u32[]{:S(2)}, u32[]{:S(2)}) %collective-permute-start.5) | collective-permute-done | bytes 32800 | tf_op jit(solution)/shard_map/ppermute | solution.py:267
  52.9 1.9 %shard_map.95 = (bf16[2,128,1024]{2,1,0:T(8,128)(2,1)S(1)}, bf16[2,128,1024]{2,1,0:T(8,128)(2,1)}) custom-call(s32[1]{0:T(128)} %bitcast.core_ref, bf16[16,2,64,128]{3,2,1,0:T(8,128)(2,1)S(1)} %all-to-all-done.1.chip_ref, bf16[256,1024]{1,0:T(8,128)(2,1)S(1)} %get-tuple-element.38.k_ref, bf16[256,1024]{1,0:T(8,128)(2,1)S(1)} %get-tuple-element.47.c_ref, ...), custom_call_target="tpu_custom_call" | custom-call | tf_op jit(solution)/shard_map/pallas_call | solution.py:39
  54.8 0.8 %copy-done.6 = bf16[2,128,1024]{2,1,0:T(8,128)(2,1)} copy-done((bf16[2,128,1024]{2,1,0:T(8,128)(2,1)}, bf16[2,128,1024]{2,1,0:T(8,128)(2,1)S(1)}, u32[]{:S(2)}) %copy-start.6) | copy-done | bytes 524312
  55.6 3.4 %collective-permute-start.6 = (bf16[2,128,1024]{2,1,0:T(8,128)(2,1)}, bf16[2,128,1024]{2,1,0:T(8,128)(2,1)S(1)}, u32[]{:S(2)}, u32[]{:S(2)}) collective-permute-start(bf16[2,128,1024]{2,1,0:T(8,128)(2,1)} %get-tuple-element.58), channel_id=1, source_target_pairs={{0,1},{1,0},{2,3},{3,2},{4,5},{5,4},{6,7},{7,6},{8,9},{9,8},{10,11... | collective-permute-start | bytes 1572872 | tf_op jit(solution)/shard_map/ppermute | solution.py:263
  59.0 0.4 shard_map.93
  59.4 0.1 collective-permute-start.3
  59.5 0.5 collective-permute-start.4
  60.0 0.8 %collective-permute-done.6.recv_ref = bf16[2,128,1024]{2,1,0:T(8,128)(2,1)S(1)} collective-permute-done((bf16[2,128,1024]{2,1,0:T(8,128)(2,1)}, bf16[2,128,1024]{2,1,0:T(8,128)(2,1)S(1)}, u32[]{:S(2)}, u32[]{:S(2)}) %collective-permute-start.6) | collective-permute-done | bytes 524320 | tf_op jit(solution)/shard_map/ppermute | solution.py:263
  60.8 1.0 %shard_map.96 = (bf16[128,2048]{1,0:T(8,128)(2,1)}, bf16[128,2048]{1,0:T(8,128)(2,1)}) custom-call(s32[1]{0:T(128)} %bitcast.core_ref, bf16[2,128,1024]{2,1,0:T(8,128)(2,1)S(1)} %copy-done.7, bf16[2,128,1024]{2,1,0:T(8,128)(2,1)S(1)} %collective-permute-done.6.recv_ref), custom_call_target="tpu_custom_call" | custom-call | tf_op jit(solution)/shard_map/pallas_call | solution.py:39
  61.8 0.9 %shard_map.94 = (bf16[128,2048]{1,0:T(8,128)(2,1)}, f32[4,2048]{1,0:T(4,128)}) custom-call(s32[1]{0:T(128)} %bitcast.core_ref, bf16[128,1024]{1,0:T(8,128)(2,1)S(1)} %get-tuple-element.50.own_ref, bf16[128,1024]{1,0:T(8,128)(2,1)S(1)} %collective-permute-done.3.recv_ref, f32[32,128]{1,0:T(8,128)S(1)} %get-tuple-element.52.taps_ref, ...), custom_call_target="tpu_custom_call" | custom-call | tf_op jit(solution)/shard_map/pallas_call | solution.py:39
  (19 shorter events, 0.1 us)
Async XLA Ops:
  1.9 2.7 %collective-permute-start = (bf16[2,128,1024]{2,1,0:T(8,128)(2,1)S(1)}, bf16[2,128,1024]{2,1,0:T(8,128)(2,1)S(1)}, u32[]{:S(2)}, u32[]{:S(2)}) collective-permute-start(bf16[2,128,1024]{2,1,0:T(8,128)(2,1)S(1)} %get-tuple-element.34), channel_id=1, source_target_pairs={{0,1},{1,0},{2,3},{3,2},{4,5},{5,4},{6,7},{7,6},{8,9},{9,8},{10,11... | collective-permute-start | bytes 1572872 | tf_op jit(solution)/shard_map/ppermute | solution.py:263
  4.0 9.4 %collective-permute-start.1 = (bf16[2,128,1024]{2,1,0:T(8,128)(2,1)}, bf16[2,128,1024]{2,1,0:T(8,128)(2,1)S(1)}, u32[]{:S(2)}, u32[]{:S(2)}) collective-permute-start(bf16[2,128,1024]{2,1,0:T(8,128)(2,1)} %get-tuple-element.37), channel_id=1, source_target_pairs={{0,1},{1,0},{2,3},{3,2},{4,5},{5,4},{6,7},{7,6},{8,9},{9,8},{10,11... | collective-permute-start | bytes 1572872 | tf_op jit(solution)/shard_map/ppermute | solution.py:263
  5.6 14.0 %all-to-all-start = ((bf16[16,64,128]{2,1,0:T(8,128)(2,1)}), bf16[16,64,128]{2,1,0:T(8,128)(2,1)S(1)}, u32[]{:S(2)}, u32[]{:S(2)}) async-start(bf16[16,64,128]{2,1,0:T(8,128)(2,1)} %bitcast.1), calls=%async_computation | async-start | bytes 524288 | tf_op jit(solution)/shard_map/all_to_all | solution.py:270
  13.4 4.4 %copy-start.8 = (f32[4,2048]{1,0:T(4,128)S(1)}, f32[4,2048]{1,0:T(4,128)}, u32[]{:S(2)}) copy-start(f32[4,2048]{1,0:T(4,128)} %w_ref.3) | copy-start | bytes 98308
  13.5 4.3 %collective-permute-start.2 = (bf16[16,1024]{1,0:T(8,128)(2,1)S(1)}, bf16[16,1024]{1,0:T(8,128)(2,1)S(1)}, u32[]{:S(2)}, u32[]{:S(2)}) collective-permute-start(bf16[16,1024]{1,0:T(8,128)(2,1)S(1)} %get-tuple-element.40), channel_id=1, source_target_pairs={{0,2},{1,3},{2,4},{3,5},{4,6},{5,7},{6,8},{7,9},{8,10},{9,11},{10,... | collective-permute-start | bytes 98312 | tf_op jit(solution)/shard_map/ppermute | solution.py:267
  19.7 0.8 %copy-start.5 = (bf16[16,2,64,128]{3,2,1,0:T(8,128)(2,1)}, bf16[16,2,64,128]{3,2,1,0:T(8,128)(2,1)S(1)}, u32[]{:S(2)}) copy-start(bf16[16,2,64,128]{3,2,1,0:T(8,128)(2,1)S(1)} %get-tuple-element.42) | copy-start | bytes 1572868
  20.5 16.4 %all-to-all-start.1 = ((bf16[16,2,64,128]{3,2,1,0:T(8,128)(2,1)}), bf16[16,2,64,128]{3,2,1,0:T(8,128)(2,1)S(1)}, u32[]{:S(2)}, u32[]{:S(2)}) async-start(bf16[16,2,64,128]{3,2,1,0:T(8,128)(2,1)} %copy-done.5), calls=%async_computation.1 | async-start | bytes 1048576 | tf_op jit(solution)/shard_map/all_to_all | solution.py:270
  30.5 0.8 %copy-start = (bf16[256,1024]{1,0:T(8,128)(2,1)}, bf16[256,1024]{1,0:T(8,128)(2,1)S(1)}, u32[]{:S(2)}) copy-start(bf16[256,1024]{1,0:T(8,128)(2,1)S(1)} %get-tuple-element.45.gc_ref) | copy-start | bytes 1572868
  36.9 1.0 %copy-start.1 = (bf16[256,1024]{1,0:T(8,128)(2,1)S(1)}, bf16[256,1024]{1,0:T(8,128)(2,1)}, u32[]{:S(2)}) copy-start(bf16[256,1024]{1,0:T(8,128)(2,1)} %copy-done) | copy-start | bytes 1572868
  39.5 19.5 %all-to-all-start.2 = ((bf16[16,96,128]{2,1,0:T(8,128)(2,1)}), bf16[16,96,128]{2,1,0:T(8,128)(2,1)S(1)}, u32[]{:S(2)}, u32[]{:S(2)}) async-start(bf16[16,96,128]{2,1,0:T(8,128)(2,1)} %get-tuple-element.46), calls=%async_computation.2 | async-start | bytes 786432 | tf_op jit(solution)/shard_map/all_to_all | solution.py:270
  47.2 5.7 %collective-permute-start.5 = (bf16[16,1024]{1,0:T(8,128)(2,1)S(1)}, bf16[16,1024]{1,0:T(8,128)(2,1)S(1)}, u32[]{:S(2)}, u32[]{:S(2)}) collective-permute-start(bf16[16,1024]{1,0:T(8,128)(2,1)S(1)} %get-tuple-element.55), channel_id=1, source_target_pairs={{2,0},{3,1},{4,2},{5,3},{6,4},{7,5},{8,6},{9,7},{10,8},{11,9},{12,... | collective-permute-start | bytes 98312 | tf_op jit(solution)/shard_map/ppermute | solution.py:267
  48.5 4.4 %copy-start.2 = (bf16[256,1024]{1,0:T(8,128)(2,1)S(1)}, bf16[256,1024]{1,0:T(8,128)(2,1)}, u32[]{:S(2)}) copy-start(bf16[256,1024]{1,0:T(8,128)(2,1)} %copy-done) | copy-start | bytes 1572868
  50.0 0.8 %copy-start.3 = (bf16[256,1024]{1,0:T(8,128)(2,1)}, bf16[256,1024]{1,0:T(8,128)(2,1)S(1)}, u32[]{:S(2)}) copy-start(bf16[256,1024]{1,0:T(8,128)(2,1)S(1)} %get-tuple-element.49.gq_ref) | copy-start | bytes 1572868
  52.9 6.1 %copy-start.4 = (bf16[256,1024]{1,0:T(8,128)(2,1)S(1)}, bf16[256,1024]{1,0:T(8,128)(2,1)}, u32[]{:S(2)}) copy-start(bf16[256,1024]{1,0:T(8,128)(2,1)} %copy-done.3) | copy-start | bytes 1572868
  54.8 0.8 %copy-start.6 = (bf16[2,128,1024]{2,1,0:T(8,128)(2,1)}, bf16[2,128,1024]{2,1,0:T(8,128)(2,1)S(1)}, u32[]{:S(2)}) copy-start(bf16[2,128,1024]{2,1,0:T(8,128)(2,1)S(1)} %get-tuple-element.57.own_ref) | copy-start | bytes 1572868
  55.6 5.2 %collective-permute-start.6 = (bf16[2,128,1024]{2,1,0:T(8,128)(2,1)}, bf16[2,128,1024]{2,1,0:T(8,128)(2,1)S(1)}, u32[]{:S(2)}, u32[]{:S(2)}) collective-permute-start(bf16[2,128,1024]{2,1,0:T(8,128)(2,1)} %get-tuple-element.58), channel_id=1, source_target_pairs={{0,1},{1,0},{2,3},{3,2},{4,5},{5,4},{6,7},{7,6},{8,9},{9,8},{10,11... | collective-permute-start | bytes 1572872 | tf_op jit(solution)/shard_map/ppermute | solution.py:263
  59.0 1.7 %copy-start.7 = (bf16[2,128,1024]{2,1,0:T(8,128)(2,1)S(1)}, bf16[2,128,1024]{2,1,0:T(8,128)(2,1)}, u32[]{:S(2)}) copy-start(bf16[2,128,1024]{2,1,0:T(8,128)(2,1)} %copy-done.6) | copy-start | bytes 1572868
  59.4 2.4 %collective-permute-start.3 = (bf16[128,1024]{1,0:T(8,128)(2,1)S(1)}, bf16[128,1024]{1,0:T(8,128)(2,1)S(1)}, u32[]{:S(2)}, u32[]{:S(2)}) collective-permute-start(bf16[128,1024]{1,0:T(8,128)(2,1)S(1)} %get-tuple-element.51), channel_id=1, source_target_pairs={{0,1},{1,0},{2,3},{3,2},{4,5},{5,4},{6,7},{7,6},{8,9},{9,8},{10,11... | collective-permute-start | bytes 786440 | tf_op jit(solution)/shard_map/ppermute | solution.py:263
  59.5 2.3 %collective-permute-start.4 = (f32[32,128]{1,0:T(8,128)S(1)}, f32[32,128]{1,0:T(8,128)S(1)}, u32[]{:S(2)}, u32[]{:S(2)}) collective-permute-start(f32[32,128]{1,0:T(8,128)S(1)} %get-tuple-element.52.taps_ref), channel_id=1, source_target_pairs={{0,1},{1,0},{2,3},{3,2},{4,5},{5,4},{6,7},{7,6},{8,9},{9,8},{10,11... | collective-permute-start | bytes 49160 | tf_op jit(solution)/shard_map/ppermute | solution.py:263

commit v4 on v3

--- a/solution.py
+++ b/solution.py
@@ -19,7 +19,7 @@
 BF16 = jnp.bfloat16
 VMEM = pl.BlockSpec(memory_space=pltpu.VMEM)
 SMEM = pl.BlockSpec(memory_space=pltpu.SMEM)
-HBM = pl.BlockSpec(memory_space=pl.ANY)
+ANY = pl.BlockSpec(memory_space=pl.ANY)
 PARAMS = pltpu.CompilerParams(vmem_limit_bytes=16 * 1024 * 1024)
 
 
@@ -35,13 +35,14 @@
     return pl.ds(pl.multiple_of(core * size, size), size)
 
 
-def call(kernel, outs, core, arrays, scratch=(), space=VMEM):
+def call(kernel, outs, core, arrays, scratch=(), given=None, made=None, aliases={}):
     return pl.pallas_call(
         kernel,
         out_shape=outs,
-        in_specs=[SMEM] + [space] * len(arrays),
-        out_specs=jax.tree.map(lambda _: VMEM, outs),
+        in_specs=[SMEM] + (given or [VMEM] * len(arrays)),
+        out_specs=made or jax.tree.map(lambda _: VMEM, outs),
         scratch_shapes=scratch,
+        input_output_aliases=aliases,
         compiler_params=PARAMS,
     )(core, *arrays)
 
@@ -50,7 +51,7 @@
     return jax.ShapeDtypeStruct(dims, dtype)
 
 
-def split_kernel(core_ref, a_ref, b_ref, own_ref, send_ref, sems):
+def split_kernel(core_ref, a_ref, b_ref, after_ref, own_ref, send_ref, sems):
     core = core_ref[0]
     copies = []
     for n, ref in enumerate((a_ref, b_ref)):
@@ -64,6 +65,30 @@
         copy.wait()
 
 
+def query_state_kernel(
+    core_ref, q_ref, g_ref, keep_ref, give_ref, held_ref, sems
+):
+    core = core_ref[0]
+    copies = [
+        pltpu.make_async_copy(ref, held_ref.at[n], sems.at[n])
+        for n, ref in enumerate((q_ref, g_ref))
+    ]
+    for copy in copies:
+        copy.start()
+    for copy in copies:
+        copy.wait()
+    for side, out in ((1 - core, give_ref), (core, keep_ref)):
+        for i in range(HALF):
+            at = pl.ds(pl.multiple_of(side * WIDE + i * DH, DH), DH)
+            out[i] = dot(held_ref[0, :, at], held_ref[1, :, at], (0, 0)).astype(BF16)
+
+
+def add_kernel(core_ref, keep_ref, recv_ref, out_ref, done_ref):
+    for i in range(HALF):
+        out_ref[i] = (keep_ref[i].astype(F32) + recv_ref[i].astype(F32)).astype(BF16)
+    done_ref[...] = jnp.zeros(done_ref.shape, F32)
+
+
 def gather(core, own_ref, recv_ref, refs):
     rows = own_ref.shape[1]
     for n, ref in enumerate(refs):
@@ -71,14 +96,23 @@
         ref[half_of(1 - core, rows), :] = recv_ref[n]
 
 
-def query_state_kernel(core_ref, own_ref, recv_ref, q_ref, g_ref, state_ref):
+def gather_query_kernel(core_ref, own_ref, recv_ref, k_ref, q_ref, g_ref, edge_ref, far_ref, sem):
     gather(core_ref[0], own_ref, recv_ref, (q_ref, g_ref))
-    for i in range(HALF):
-        at = columns(i)
-        state_ref[i] = dot(q_ref[:, at], g_ref[:, at], (0, 0)).astype(BF16)
-
-
-def gather_kernel(core_ref, own_ref, recv_ref, k_ref, v_ref, tail_ref):
+    copy = pltpu.make_async_copy(q_ref, far_ref, sem)
+    copy.start()
+    first = lax.broadcasted_iota(jnp.int32, (HALO, HALO), 0)
+    unseen = first > lax.broadcasted_iota(jnp.int32, (HALO, HALO), 1)
+    for i in range(HALF):
+        at = columns(i)
+        q, g, k = q_ref[:HALO, at], g_ref[:HALO, at], k_ref[:HALO, at]
+        score = jnp.where(unseen, dot(k, q, (1, 1)), 0.0).astype(BF16)
+        edge = dot(score, g, (1, 0))
+        both = jnp.concatenate([-edge[:EDGE], k.astype(F32)[:EDGE]], axis=0)
+        edge_ref[:, at] = both.astype(BF16)
+    copy.wait()
+
+
+def gather_key_kernel(core_ref, own_ref, recv_ref, k_ref, v_ref, tail_ref):
     gather(core_ref[0], own_ref, recv_ref, (k_ref, v_ref))
     tail_ref[...] = v_ref[v_ref.shape[0] - HALO :, :]
 
@@ -98,7 +132,15 @@
     return first <= lax.broadcasted_iota(jnp.int32, (rows, rows), 1)
 
 
-def score_kernel(core_ref, q_ref, g_ref, k_ref, state_ref, gc_ref, edge_ref):
+def add_taps(taps_ref, head, grad, parts):
+    for j, part in enumerate(parts):
+        row = j * HALF + head
+        taps_ref[row : row + 1, :] = jnp.sum(grad * part, axis=0, keepdims=True)
+
+
+def score_kernel(
+    core_ref, q_ref, g_ref, k_ref, v_ref, halo_ref, gc_ref, taps_ref
+):
     seen = later(q_ref.shape[0])
     for i in range(HALF):
         at = columns(i)
@@ -106,9 +148,7 @@
         score = jnp.where(seen, dot(k, q_ref[:, at], (1, 1)), 0.0).astype(BF16)
         gc = dot(score, g_ref[:, at], (1, 0))
         gc_ref[:, at] = gc.astype(BF16)
-        edge = gc[:HALO] - dot(k[:HALO], state_ref[i], (1, 0))
-        both = jnp.concatenate([edge[:EDGE], k[:HALO].astype(F32)[:EDGE]], axis=0)
-        edge_ref[:, at] = both.astype(BF16)
+        add_taps(taps_ref, i, gc, lagged(v_ref, halo_ref, at))
 
 
 def conv_kernel(core_ref, k_ref, v_ref, halo_ref, w_ref, c_ref, state_ref):
@@ -133,17 +173,6 @@
     done_ref[...] = jnp.zeros(done_ref.shape, F32)
 
 
-def attn_kernel(core_ref, q_ref, g_ref, k_ref, c_ref, done_ref, gq_ref, gk_ref):
-    seen = later(q_ref.shape[0])
-    for i in range(HALF):
-        at = columns(i)
-        c, g = c_ref[:, at], g_ref[:, at]
-        turned = jnp.where(seen, dot(c, g, (1, 1)), 0.0)
-        gk_ref[:, at] = dot(turned.astype(BF16), q_ref[:, at], (1, 0)).astype(BF16)
-        attn = jnp.where(seen.T, dot(g, c, (1, 1)), 0.0)
-        gq_ref[:, at] = dot(attn.astype(BF16), k_ref[:, at], (1, 0)).astype(BF16)
-
-
 def head_state(read, head, depth):
     parts = DH // depth
     if depth % HALO == 0:
@@ -153,21 +182,33 @@
 
 
 def tap_kernel(
-    core_ref, chip_ref, k_ref, gc_ref, v_ref, halo_ref, out_ref, done_ref, taps_ref, *, scale, order
+    core_ref,
+    chip_ref,
+    k_ref,
+    v_ref,
+    halo_ref,
+    near_ref,
+    edge_ref,
+    out_ref,
+    done_ref,
+    taps_ref,
+    *,
+    scale,
+    order,
 ):
     depth = chip_ref.shape[2]
+    start = out_ref.shape[1] - CW * HALF
     for i in range(HALF):
         at = columns(i)
         suffix = head_state(lambda n: chip_ref[n, 0], i, depth)
-        gc = scale * (gc_ref[:, at].astype(F32) + dot(k_ref[:, at], suffix, (1, 0)))
-        for j, part in enumerate(lagged(v_ref, halo_ref, at)):
-            row = j * HALF + i
-            taps_ref[row : row + 1, :] = jnp.sum(gc * part, axis=0, keepdims=True)
+        grad = dot(k_ref[:, at], suffix, (1, 0))
+        add_taps(taps_ref, i, grad, lagged(v_ref, halo_ref, at))
+    weights = (scale * (near_ref[...] + taps_ref[...])).astype(BF16)
     total = jnp.zeros((depth, DH), F32)
-    weights = taps_ref[...].astype(BF16)
-    start = out_ref.shape[1] - CW * HALF
     for n in order:
         out_ref[n, :depth] = total.astype(BF16)
+        if depth < start:
+            out_ref[n, depth:start] = jnp.zeros((start - depth, DH), BF16)
         total = total + chip_ref[n, 1].astype(F32)
         out_ref[n, start:] = weights
     done_ref[...] = jnp.zeros(done_ref.shape, F32)
@@ -176,26 +217,37 @@
 def query_side_kernel(
     core_ref,
     chip_ref,
+    q_ref,
+    g_ref,
     k_ref,
     c_ref,
-    gk_ref,
     gc_ref,
     edge_ref,
     w_ref,
     done_ref,
+    gk_ref,
+    gv_ref,
+    send_ref,
+    gq_ref,
     own_ref,
-    send_ref,
+    sems,
     *,
     scale,
 ):
     core = core_ref[0]
     rows = k_ref.shape[0]
     depth = chip_ref.shape[2]
+    seen = later(rows)
     for i in range(HALF):
         at = columns(i)
         suffix = head_state(lambda n: chip_ref[n, 0], i, depth)
-        gk = scale * (gk_ref[:, at].astype(F32) + dot(c_ref[:, at], suffix, (1, 1)))
-        gc = scale * (gc_ref[:, at].astype(F32) + dot(k_ref[:, at], suffix, (1, 0)))
+        c, g, k = c_ref[:, at], g_ref[:, at], k_ref[:, at]
+        attn = jnp.where(seen.T, dot(g, c, (1, 1)), 0.0)
+        gq_ref[:, at] = dot(attn.astype(BF16), k, (1, 0)).astype(BF16)
+        turned = jnp.where(seen, dot(c, g, (1, 1)), 0.0)
+        gk = dot(turned.astype(BF16), q_ref[:, at], (1, 0))
+        gk = scale * (gk + dot(c, suffix, (1, 1)))
+        gc = scale * (gc_ref[:, at].astype(F32) + dot(k, suffix, (1, 0)))
         edge = edge_ref[:, at]
         after = dot(edge, suffix, (1, 0))[EDGE:] + edge.astype(F32)[:EDGE]
         ext = jnp.concatenate([gc, scale * after], axis=0)
@@ -207,6 +259,18 @@
             low, high = value[: rows // 2].astype(BF16), value[rows // 2 :].astype(BF16)
             own_ref[n, :, at] = jnp.where(core == 0, low, high)
             send_ref[n, :, at] = jnp.where(core == 0, high, low)
+    put(own_ref, core, (gk_ref, gv_ref), sems)
+
+
+def put(half_ref, side, refs, sems):
+    copies = [
+        pltpu.make_async_copy(half_ref.at[n], ref.at[:, half_of(side, WIDE)], sems.at[n])
+        for n, ref in enumerate(refs)
+    ]
+    for copy in copies:
+        copy.start()
+    for copy in copies:
+        copy.wait()
 
 
 def key_side_kernel(
@@ -228,11 +292,8 @@
     taps_ref[...] = total
 
 
-def join_kernel(core_ref, own_ref, recv_ref, a_ref, b_ref):
-    core = core_ref[0]
-    for n, ref in enumerate((a_ref, b_ref)):
-        ref[:, half_of(core, WIDE)] = own_ref[n]
-        ref[:, half_of(1 - core, WIDE)] = recv_ref[n]
+def join_kernel(core_ref, recv_ref, _, __, gk_ref, gv_ref, sems):
+    put(recv_ref, 1 - core_ref[0], (gk_ref, gv_ref), sems)
 
 
 def finish_kernel(core_ref, own_ref, recv_ref, taps_ref, far_ref, gq_ref, gw_ref):
@@ -269,25 +330,61 @@
     def turn(value):
         return lax.all_to_all(value, AXES, 0, 0, axis_index_groups=groups, tiled=True)
 
-    def split(*arrays):
-        arrays = [pltpu.with_memory_space_constraint(a, pltpu.HBM) for a in arrays]
-        sems = [pltpu.SemaphoreType.DMA((2, 2))]
-        return call(split_kernel, (pair, pair), core, arrays, sems, HBM)
-
     pair = shape((2, rows, WIDE))
     block = shape((2 * rows, WIDE))
+    far_block = pltpu.HBM((2 * rows, WIDE), BF16)
     states = shape((HALF, DH, DH))
     edges = shape((HALO, WIDE))
     flag = shape((8, DH), F32)
-    qg_own, qg_send = split(queries, grad_out)
+    dma = pltpu.SemaphoreType.DMA
+    queries, grad_out, keys, values = (
+        pltpu.with_memory_space_constraint(a, pltpu.HBM)
+        for a in (queries, grad_out, keys, values)
+    )
+    q_keep, q_give = call(
+        query_state_kernel,
+        (states, states),
+        core,
+        [queries, grad_out],
+        [pltpu.VMEM((2, rows, width), BF16), dma((2,))],
+        [ANY] * 2,
+    )
+    q_recv = swap(q_give)
+    kv_own, kv_send = call(
+        split_kernel,
+        (pair, pair),
+        core,
+        [keys, values, q_keep],
+        [dma((2, 2))],
+        [ANY, ANY, VMEM],
+    )
+    kv_recv = swap(kv_send)
+    q_sent, added = call(
+        add_kernel,
+        (states, flag),
+        core,
+        [q_keep, q_recv],
+    )
+    q_turned = turn(q_sent.reshape(chips, depth, DH))
+    qg_own, qg_send = call(
+        split_kernel,
+        (pair, pair),
+        core,
+        [queries, grad_out, added],
+        [dma((2, 2))],
+        [ANY, ANY, VMEM],
+    )
     qg_recv = swap(qg_send)
-    kv_own, kv_send = split(keys, values)
-    kv_recv = swap(kv_send)
-    q, g, q_state = call(query_state_kernel, (block, block, states), core, [qg_own, qg_recv])
-    q_turned = turn(q_state.reshape(chips, depth, DH))
-    k, v, tail = call(gather_kernel, (block, block, edges), core, [kv_own, kv_recv])
+    k, v, tail = call(gather_key_kernel, (block, block, edges), core, [kv_own, kv_recv])
     halo = shifted(tail, 2)
-    gc, edge = call(score_kernel, (block, edges), core, [q, g, k, q_state])
+    q, g, edge, q_far = call(
+        gather_query_kernel,
+        (block, block, edges, far_block),
+        core,
+        [qg_own, qg_recv, k],
+        [dma(())],
+        made=(VMEM, VMEM, VMEM, ANY),
+    )
     c, k_state = call(conv_kernel, (block, states), core, [k, v, halo, conv_weight])
     both, turned = call(
         functools.partial(turn_kernel, order=order),
@@ -296,21 +393,26 @@
         [q_turned, k_state.reshape(chips, depth, DH)],
     )
     both = turn(both)
+    gc, taps = call(
+        score_kernel, (far_block, shape((CW * HALF, DH), F32)), core, [q, g, k, v, halo]
+    )
     edge = shifted(edge, -2)
-    gq, gk = call(attn_kernel, (block, block), core, [q, g, k, c, turned])
     last, tapped = call(
         functools.partial(tap_kernel, scale=scale, order=order),
         (shape((chips, max(depth, HALO) + CW * HALF, DH)), flag),
         core,
-        [both, k, gc, v, halo],
+        [both, k, v, halo, taps, edge],
         [pltpu.VMEM((CW * HALF, DH), F32)],
     )
     last = turn(last)
-    kv_grad, kv_give = call(
+    full = shape((rows, width))
+    grad_keys, grad_values, kv_give, gq = call(
         functools.partial(query_side_kernel, scale=scale),
-        (pair, pair),
-        core,
-        [both, k, c, gk, gc, edge, conv_weight, tapped],
+        (full, full, pair, block),
+        core,
+        [both, q_far, g, k, c, gc, edge, conv_weight, tapped],
+        [pltpu.VMEM((2, rows, WIDE), BF16), dma((2,))],
+        made=(ANY, ANY, VMEM, VMEM),
     )
     kv_got = swap(kv_give)
     q_grad, q_give, taps = call(
@@ -321,8 +423,16 @@
     )
     q_got = swap(q_give)
     far = swap(taps)
-    full = shape((rows, width))
-    grad_keys, grad_values = call(join_kernel, (full, full), core, [kv_grad, kv_got])
+    grad_keys, grad_values = call(
+        join_kernel,
+        (full, full),
+        core,
+        [kv_got, grad_keys, grad_values],
+        [dma((2,))],
+        [VMEM, ANY, ANY],
+        (ANY, ANY),
+        {2: 0, 3: 1},
+    )
     grad_queries, grad_weight = call(
         finish_kernel, (full, shape((CW, width), F32)), core, [q_grad, q_got, taps, far]
     )

time: 63.6 us -> 62.4 us (0.981)
  waiting for transfers between devices: 11.5 us -> 6.93 us
  starting transfers between devices: 31.2 us -> 34.5 us
  Pallas kernels: 15 us -> 17.2 us
  local copies, waits for them, and re-layouts: 4.22 us -> 2.08 us
    all_to_all x3, waiting for transfers between devices: 6.53 us -> 1 us  [turn(): lax.all_to_all(value, AXES, 0, 0, axis_index_groups=groups, tiled=True)]
    ppermute x5 -> x6, starting transfers between devices: 4.66 us -> 8.8 us  [swap(): return lax.ppermute(value, AXES, [(d, d ^ 1) for d in range(count)])]
    pallas_call x13 -> x14, Pallas kernels: 15 us -> 17.2 us  [call(): pl.pallas_call(kernel, out_shape=outs, in_specs=[SMEM] + (given or [VMEM]...]
    unnamed x18 -> x6, local copies, waits for them, and re-layouts: 4.22 us -> 2.08 us
    ppermute x5 -> x6, waiting for transfers between devices: 0.81 us -> 1.84 us  [swap(): return lax.ppermute(value, AXES, [(d, d ^ 1) for d in range(count)])]
    all_to_all x3, starting transfers between devices: 23.1 us -> 22.2 us  [turn(): lax.all_to_all(value, AXES, 0, 0, axis_index_groups=groups, tiled=True)]
  transfers between devices with their start and end apart: 10 -> 11, of which waited for: 5 -> 5; matrix products, arithmetic and copies ran while one was open for 0% -> 0% of each run, Pallas kernels for 18% -> 20%
where the time goes in v4:
time: 62.4 us; the launch traced here: 61.4 us
  starting transfers between devices  34.5 us (55%)
  Pallas kernels  17.2 us (28%)
  waiting for transfers between devices  6.93 us (11%)
  local copies, waits for them, and re-layouts  2.08 us (3%)
  between operations  0.75 us (1%)
    all_to_all x3, starting transfers between devices, turn(): lax.all_to_all(value, AXES, 0, 0, axis_index_groups=groups, tiled=True)  22.2 us
    pallas_call x14, Pallas kernels, call(): pl.pallas_call(kernel, out_shape=outs, in_specs=[SMEM] + (given or [VMEM]...  17.2 us
    ppermute x6, starting transfers between devices, swap(): return lax.ppermute(value, AXES, [(d, d ^ 1) for d in range(count)])  8.8 us
    ppermute x2, waiting for transfers between devices, shifted(): return lax.ppermute(value, AXES, pairs)  4.09 us
    ppermute x2, starting transfers between devices, shifted(): return lax.ppermute(value, AXES, pairs)  3.48 us
    unnamed x6, local copies, waits for them, and re-layouts  2.08 us
    ppermute x6, waiting for transfers between devices, swap(): return lax.ppermute(value, AXES, [(d, d ^ 1) for d in range(count)])  1.84 us
  transfers between devices with their start and end apart: 11, of which 5 were waited for; matrix products, arithmetic and copies ran while one was open for 0% of the time, Pallas kernels for 20%

profile of v4, /device:TPU:1, one launch (start us, length us, event | category | flops | bytes accessed | tf_op | source)
XLA Modules:
  0.0 61.4 jit_solution(5663251431862964449)
XLA Ops:
  0.6 1.7 %shard_map.84 = (bf16[8,128,128]{2,1,0:T(8,128)(2,1)S(1)}, bf16[8,128,128]{2,1,0:T(8,128)(2,1)S(1)}) custom-call(s32[1]{0:T(128)} %bitcast.core_ref, bf16[128,2048]{1,0:T(8,128)(2,1)} %a_ref.3, bf16[128,2048]{1,0:T(8,128)(2,1)} %b_ref.3), custom_call_target="tpu_custom_call" | custom-call | tf_op jit(solution)/shard_map/pallas_call | solution.py:39
  2.3 0.1 collective-permute-start
  2.5 1.2 %shard_map.86 = (bf16[2,128,1024]{2,1,0:T(8,128)(2,1)S(1)}, bf16[2,128,1024]{2,1,0:T(8,128)(2,1)S(1)}) custom-call(s32[1]{0:T(128)} %bitcast.core_ref, bf16[128,2048]{1,0:T(8,128)(2,1)} %a_ref.2, bf16[128,2048]{1,0:T(8,128)(2,1)} %b_ref.2, bf16[8,128,128]{2,1,0:T(8,128)(2,1)S(1)} %get-tuple-element.37.keep_ref.after_ref), custom_call_target="tpu_custom_call" | custom-call | tf_op jit(solution)/shard_map/pallas_call | solution.py:39
  3.7 0.5 collective-permute-start.1
  4.2 0.8 %shard_map.85 = (bf16[8,128,128]{2,1,0:T(8,128)(2,1)}, f32[8,128]{1,0:T(8,128)S(1)}) custom-call(s32[1]{0:T(128)} %bitcast.core_ref, bf16[8,128,128]{2,1,0:T(8,128)(2,1)S(1)} %get-tuple-element.37.keep_ref.after_ref, bf16[8,128,128]{2,1,0:T(8,128)(2,1)S(1)} %collective-permute-done.recv_ref), custom_call_target="tpu_custom_call" | custom-call | tf_op jit(solution)/shard_map/pallas_call | solution.py:39
  5.0 7.8 %all-to-all-start = ((bf16[16,64,128]{2,1,0:T(8,128)(2,1)}), bf16[16,64,128]{2,1,0:T(8,128)(2,1)S(1)}, u32[]{:S(2)}, u32[]{:S(2)}) async-start(bf16[16,64,128]{2,1,0:T(8,128)(2,1)} %bitcast.1), calls=%async_computation | async-start | bytes 524288 | tf_op jit(solution)/shard_map/all_to_all | solution.py:331
  12.8 0.1 shard_map.87
  12.9 2.2 %collective-permute-start.2 = (bf16[16,1024]{1,0:T(8,128)(2,1)S(1)}, bf16[16,1024]{1,0:T(8,128)(2,1)S(1)}, u32[]{:S(2)}, u32[]{:S(2)}) collective-permute-start(bf16[16,1024]{1,0:T(8,128)(2,1)S(1)} %get-tuple-element.44), channel_id=1, source_target_pairs={{0,2},{1,3},{2,4},{3,5},{4,6},{5,7},{6,8},{7,9},{8,10},{9,11},{10,... | collective-permute-start | bytes 98312 | tf_op jit(solution)/shard_map/ppermute | solution.py:328
  15.1 2.1 %collective-permute-done.2.halo_ref = bf16[16,1024]{1,0:T(8,128)(2,1)S(1)} collective-permute-done((bf16[16,1024]{1,0:T(8,128)(2,1)S(1)}, bf16[16,1024]{1,0:T(8,128)(2,1)S(1)}, u32[]{:S(2)}, u32[]{:S(2)}) %collective-permute-start.2) | collective-permute-done | bytes 32800 | tf_op jit(solution)/shard_map/ppermute | solution.py:328
  17.1 0.8 %shard_map.88 = (bf16[256,1024]{1,0:T(8,128)(2,1)S(1)}, bf16[8,128,128]{2,1,0:T(8,128)(2,1)S(1)}) custom-call(s32[1]{0:T(128)} %bitcast.core_ref, bf16[256,1024]{1,0:T(8,128)(2,1)S(1)} %get-tuple-element.42.k_ref, bf16[256,1024]{1,0:T(8,128)(2,1)S(1)} %get-tuple-element.43.v_ref, bf16[16,1024]{1,0:T(8,128)(2,1)S(1)} %collective-permute-done.2.halo_ref, ...), custom_call_target="tpu_custom_call" | custom-call | tf_op jit(solution)/shard_map/pallas_call | solution.py:39
  18.0 1.0 %all-to-all-done.q_ref = bf16[16,64,128]{2,1,0:T(8,128)(2,1)S(1)} async-done(((bf16[16,64,128]{2,1,0:T(8,128)(2,1)}), bf16[16,64,128]{2,1,0:T(8,128)(2,1)S(1)}, u32[]{:S(2)}, u32[]{:S(2)}) %all-to-all-start) | async-done | bytes 262176 | tf_op jit(solution)/shard_map/all_to_all | solution.py:331
  19.0 0.8 %shard_map.89 = (bf16[16,2,64,128]{3,2,1,0:T(8,128)(2,1)}, f32[8,128]{1,0:T(8,128)}) custom-call(s32[1]{0:T(128)} %bitcast.core_ref, bf16[16,64,128]{2,1,0:T(8,128)(2,1)S(1)} %all-to-all-done.q_ref, bf16[16,64,128]{2,1,0:T(8,128)(2,1)S(1)} %bitcast.3), custom_call_target="tpu_custom_call" | custom-call | tf_op jit(solution)/shard_map/pallas_call | solution.py:39
  19.8 7.6 %all-to-all-start.1 = ((bf16[16,2,64,128]{3,2,1,0:T(8,128)(2,1)}), bf16[16,2,64,128]{3,2,1,0:T(8,128)(2,1)S(1)}, u32[]{:S(2)}, u32[]{:S(2)}) async-start(bf16[16,2,64,128]{3,2,1,0:T(8,128)(2,1)} %get-tuple-element.46), calls=%async_computation.1 | async-start | bytes 1048576 | tf_op jit(solution)/shard_map/all_to_all | solution.py:331
  27.4 1.2 %shard_map.90 = (bf16[2,128,1024]{2,1,0:T(8,128)(2,1)S(1)}, bf16[2,128,1024]{2,1,0:T(8,128)(2,1)S(1)}) custom-call(s32[1]{0:T(128)} %bitcast.core_ref, bf16[128,2048]{1,0:T(8,128)(2,1)} %a_ref.3, bf16[128,2048]{1,0:T(8,128)(2,1)} %b_ref.3, f32[8,128]{1,0:T(8,128)S(1)} %get-tuple-element.47.after_ref), custom_call_target="tpu_custom_call" | custom-call | tf_op jit(solution)/shard_map/pallas_call | solution.py:39
  28.6 2.8 %collective-permute-start.3 = (bf16[2,128,1024]{2,1,0:T(8,128)(2,1)S(1)}, bf16[2,128,1024]{2,1,0:T(8,128)(2,1)S(1)}, u32[]{:S(2)}, u32[]{:S(2)}) collective-permute-start(bf16[2,128,1024]{2,1,0:T(8,128)(2,1)S(1)} %get-tuple-element.49), channel_id=1, source_target_pairs={{0,1},{1,0},{2,3},{3,2},{4,5},{5,4},{6,7},{7,6},{8,9},{9,8},{10,11... | collective-permute-start | bytes 1572872 | tf_op jit(solution)/shard_map/ppermute | solution.py:324
  31.4 1.5 %collective-permute-done.3.recv_ref = bf16[2,128,1024]{2,1,0:T(8,128)(2,1)S(1)} collective-permute-done((bf16[2,128,1024]{2,1,0:T(8,128)(2,1)S(1)}, bf16[2,128,1024]{2,1,0:T(8,128)(2,1)S(1)}, u32[]{:S(2)}, u32[]{:S(2)}) %collective-permute-start.3) | collective-permute-done | bytes 524320 | tf_op jit(solution)/shard_map/ppermute | solution.py:324
  33.0 0.9 %shard_map.91 = (bf16[256,1024]{1,0:T(8,128)(2,1)S(1)}, bf16[256,1024]{1,0:T(8,128)(2,1)S(1)}, bf16[16,1024]{1,0:T(8,128)(2,1)S(1)}, bf16[256,1024]{1,0:T(8,128)(2,1)}) custom-call(s32[1]{0:T(128)} %bitcast.core_ref, bf16[2,128,1024]{2,1,0:T(8,128)(2,1)S(1)} %get-tuple-element.48.own_ref, bf16[2,128,1024]{2,1,0:T(8,128)(2,1)S(1)} %collective-permute-done.3.recv_ref, ...), custom_call_target="tpu_custom_call" | custom-call | tf_op jit(solution)/shard_map/pallas_call | solution.py:39
  33.8 1.3 %collective-permute-start.4 = (bf16[16,1024]{1,0:T(8,128)(2,1)S(1)}, bf16[16,1024]{1,0:T(8,128)(2,1)S(1)}, u32[]{:S(2)}, u32[]{:S(2)}) collective-permute-start(bf16[16,1024]{1,0:T(8,128)(2,1)S(1)} %get-tuple-element.53), channel_id=1, source_target_pairs={{2,0},{3,1},{4,2},{5,3},{6,4},{7,5},{8,6},{9,7},{10,8},{11,9},{12,... | collective-permute-start | bytes 98312 | tf_op jit(solution)/shard_map/ppermute | solution.py:328
  35.1 1.8 %shard_map.92 = (bf16[256,1024]{1,0:T(8,128)(2,1)}, f32[32,128]{1,0:T(8,128)S(1)}) custom-call(s32[1]{0:T(128)} %bitcast.core_ref, bf16[256,1024]{1,0:T(8,128)(2,1)S(1)} %get-tuple-element.50.q_ref, bf16[256,1024]{1,0:T(8,128)(2,1)S(1)} %get-tuple-element.51.g_ref, bf16[256,1024]{1,0:T(8,128)(2,1)S(1)} %get-tuple-element.42.k_ref, ...), custom_call_target="tpu_custom_call" | custom-call | tf_op jit(solution)/shard_map/pallas_call | solution.py:39
  37.0 2.0 %collective-permute-done.4.edge_ref = bf16[16,1024]{1,0:T(8,128)(2,1)S(1)} collective-permute-done((bf16[16,1024]{1,0:T(8,128)(2,1)S(1)}, bf16[16,1024]{1,0:T(8,128)(2,1)S(1)}, u32[]{:S(2)}, u32[]{:S(2)}) %collective-permute-start.4) | collective-permute-done | bytes 32800 | tf_op jit(solution)/shard_map/ppermute | solution.py:328
  39.0 1.5 %shard_map.93 = (bf16[16,96,128]{2,1,0:T(8,128)(2,1)}, f32[8,128]{1,0:T(8,128)S(1)}) custom-call(s32[1]{0:T(128)} %bitcast.core_ref, bf16[16,2,64,128]{3,2,1,0:T(8,128)(2,1)S(1)} %all-to-all-done.1.chip_ref, bf16[256,1024]{1,0:T(8,128)(2,1)S(1)} %get-tuple-element.42.k_ref, bf16[256,1024]{1,0:T(8,128)(2,1)S(1)} %get-tuple-element.43.v_ref, ...), custom_call_target="tpu_custom_call" | custom-call | tf_op jit(solution)/shard_map/pallas_call | solution.py:39
  40.5 6.8 %all-to-all-start.2 = ((bf16[16,96,128]{2,1,0:T(8,128)(2,1)}), bf16[16,96,128]{2,1,0:T(8,128)(2,1)S(1)}, u32[]{:S(2)}, u32[]{:S(2)}) async-start(bf16[16,96,128]{2,1,0:T(8,128)(2,1)} %get-tuple-element.54), calls=%async_computation.2 | async-start | bytes 786432 | tf_op jit(solution)/shard_map/all_to_all | solution.py:331
  47.4 1.0 %copy-done = bf16[256,1024]{1,0:T(8,128)(2,1)S(1)} copy-done((bf16[256,1024]{1,0:T(8,128)(2,1)S(1)}, bf16[256,1024]{1,0:T(8,128)(2,1)}, u32[]{:S(2)}) %copy-start) | copy-done | bytes 524312
  48.4 1.0 %copy-done.1 = bf16[256,1024]{1,0:T(8,128)(2,1)S(1)} copy-done((bf16[256,1024]{1,0:T(8,128)(2,1)S(1)}, bf16[256,1024]{1,0:T(8,128)(2,1)}, u32[]{:S(2)}) %copy-start.1) | copy-done | bytes 524312
  49.5 4.3 %shard_map.94 = (bf16[128,2048]{1,0:T(8,128)(2,1)}, bf16[128,2048]{1,0:T(8,128)(2,1)}, bf16[2,128,1024]{2,1,0:T(8,128)(2,1)}, bf16[256,1024]{1,0:T(8,128)(2,1)S(1)}) custom-call(s32[1]{0:T(128)} %bitcast.core_ref, bf16[16,2,64,128]{3,2,1,0:T(8,128)(2,1)S(1)} %all-to-all-done.1.chip_ref, bf16[256,1024]{1,0:T(8,128)(2,1)S(1)} %copy-done, ...), custom_call_target="tpu_custom_call" | custom-call | tf_op jit(solution)/shard_map/pallas_call | solution.py:39
  53.7 2.1 %collective-permute-start.7 = (bf16[2,128,1024]{2,1,0:T(8,128)(2,1)}, bf16[2,128,1024]{2,1,0:T(8,128)(2,1)S(1)}, u32[]{:S(2)}, u32[]{:S(2)}) collective-permute-start(bf16[2,128,1024]{2,1,0:T(8,128)(2,1)} %get-tuple-element.64), channel_id=1, source_target_pairs={{0,1},{1,0},{2,3},{3,2},{4,5},{5,4},{6,7},{7,6},{8,9},{9,8},{10,11... | collective-permute-start | bytes 1572872 | tf_op jit(solution)/shard_map/ppermute | solution.py:324
  55.8 0.4 shard_map.95
  56.2 3.2 %collective-permute-start.5 = (bf16[128,1024]{1,0:T(8,128)(2,1)S(1)}, bf16[128,1024]{1,0:T(8,128)(2,1)S(1)}, u32[]{:S(2)}, u32[]{:S(2)}) collective-permute-start(bf16[128,1024]{1,0:T(8,128)(2,1)S(1)} %get-tuple-element.61), channel_id=1, source_target_pairs={{0,1},{1,0},{2,3},{3,2},{4,5},{5,4},{6,7},{7,6},{8,9},{9,8},{10,11... | collective-permute-start | bytes 786440 | tf_op jit(solution)/shard_map/ppermute | solution.py:324
  59.4 0.1 collective-permute-start.6
  59.4 0.8 %shard_map.97 = (bf16[128,2048]{1,0:T(8,128)(2,1)}, bf16[128,2048]{1,0:T(8,128)(2,1)}) custom-call(s32[1]{0:T(128)} %bitcast.core_ref, bf16[2,128,1024]{2,1,0:T(8,128)(2,1)S(1)} %collective-permute-done.7.recv_ref, bf16[128,2048]{1,0:T(8,128)(2,1)} %get-tuple-element.65._, ...), custom_call_target="tpu_custom_call", output_to_operand_aliasing={{0}: (2, {}), {1}: (3, {})} | custom-call | tf_op jit(solution)/shard_map/pallas_call | solution.py:39
  60.3 0.3 collective-permute-done.6.far_ref
  60.6 0.9 %shard_map.96 = (bf16[128,2048]{1,0:T(8,128)(2,1)}, f32[4,2048]{1,0:T(4,128)}) custom-call(s32[1]{0:T(128)} %bitcast.core_ref, bf16[128,1024]{1,0:T(8,128)(2,1)S(1)} %get-tuple-element.60.own_ref, bf16[128,1024]{1,0:T(8,128)(2,1)S(1)} %collective-permute-done.5.recv_ref, f32[32,128]{1,0:T(8,128)S(1)} %get-tuple-element.62.taps_ref, ...), custom_call_target="tpu_custom_call" | custom-call | tf_op jit(solution)/shard_map/pallas_call | solution.py:39
  (10 shorter events, 0.0 us)
Async XLA Ops:
  2.3 1.9 %collective-permute-start = (bf16[8,128,128]{2,1,0:T(8,128)(2,1)S(1)}, bf16[8,128,128]{2,1,0:T(8,128)(2,1)S(1)}, u32[]{:S(2)}, u32[]{:S(2)}) collective-permute-start(bf16[8,128,128]{2,1,0:T(8,128)(2,1)S(1)} %get-tuple-element.38), channel_id=1, source_target_pairs={{0,1},{1,0},{2,3},{3,2},{4,5},{5,4},{6,7},{7,6},{8,9},{9,8},{10,11... | collective-permute-start | bytes 786440 | tf_op jit(solution)/shard_map/ppermute | solution.py:324
  3.7 9.1 %collective-permute-start.1 = (bf16[2,128,1024]{2,1,0:T(8,128)(2,1)S(1)}, bf16[2,128,1024]{2,1,0:T(8,128)(2,1)S(1)}, u32[]{:S(2)}, u32[]{:S(2)}) collective-permute-start(bf16[2,128,1024]{2,1,0:T(8,128)(2,1)S(1)} %get-tuple-element.41), channel_id=1, source_target_pairs={{0,1},{1,0},{2,3},{3,2},{4,5},{5,4},{6,7},{7,6},{8,9},{9,8},{10,11... | collective-permute-start | bytes 1572872 | tf_op jit(solution)/shard_map/ppermute | solution.py:324
  5.0 14.0 %all-to-all-start = ((bf16[16,64,128]{2,1,0:T(8,128)(2,1)}), bf16[16,64,128]{2,1,0:T(8,128)(2,1)S(1)}, u32[]{:S(2)}, u32[]{:S(2)}) async-start(bf16[16,64,128]{2,1,0:T(8,128)(2,1)} %bitcast.1), calls=%async_computation | async-start | bytes 524288 | tf_op jit(solution)/shard_map/all_to_all | solution.py:331
  12.8 4.4 %copy-start.2 = (f32[4,2048]{1,0:T(4,128)S(1)}, f32[4,2048]{1,0:T(4,128)}, u32[]{:S(2)}) copy-start(f32[4,2048]{1,0:T(4,128)} %w_ref.3) | copy-start | bytes 98308
  12.9 4.3 %collective-permute-start.2 = (bf16[16,1024]{1,0:T(8,128)(2,1)S(1)}, bf16[16,1024]{1,0:T(8,128)(2,1)S(1)}, u32[]{:S(2)}, u32[]{:S(2)}) collective-permute-start(bf16[16,1024]{1,0:T(8,128)(2,1)S(1)} %get-tuple-element.44), channel_id=1, source_target_pairs={{0,2},{1,3},{2,4},{3,5},{4,6},{5,7},{6,8},{7,9},{8,10},{9,11},{10,... | collective-permute-start | bytes 98312 | tf_op jit(solution)/shard_map/ppermute | solution.py:328
  19.8 19.2 %all-to-all-start.1 = ((bf16[16,2,64,128]{3,2,1,0:T(8,128)(2,1)}), bf16[16,2,64,128]{3,2,1,0:T(8,128)(2,1)S(1)}, u32[]{:S(2)}, u32[]{:S(2)}) async-start(bf16[16,2,64,128]{3,2,1,0:T(8,128)(2,1)} %get-tuple-element.46), calls=%async_computation.1 | async-start | bytes 1048576 | tf_op jit(solution)/shard_map/all_to_all | solution.py:331
  28.6 4.4 %collective-permute-start.3 = (bf16[2,128,1024]{2,1,0:T(8,128)(2,1)S(1)}, bf16[2,128,1024]{2,1,0:T(8,128)(2,1)S(1)}, u32[]{:S(2)}, u32[]{:S(2)}) collective-permute-start(bf16[2,128,1024]{2,1,0:T(8,128)(2,1)S(1)} %get-tuple-element.49), channel_id=1, source_target_pairs={{0,1},{1,0},{2,3},{3,2},{4,5},{5,4},{6,7},{7,6},{8,9},{9,8},{10,11... | collective-permute-start | bytes 1572872 | tf_op jit(solution)/shard_map/ppermute | solution.py:324
  33.8 5.2 %collective-permute-start.4 = (bf16[16,1024]{1,0:T(8,128)(2,1)S(1)}, bf16[16,1024]{1,0:T(8,128)(2,1)S(1)}, u32[]{:S(2)}, u32[]{:S(2)}) collective-permute-start(bf16[16,1024]{1,0:T(8,128)(2,1)S(1)} %get-tuple-element.53), channel_id=1, source_target_pairs={{2,0},{3,1},{4,2},{5,3},{6,4},{7,5},{8,6},{9,7},{10,8},{11,9},{12,... | collective-permute-start | bytes 98312 | tf_op jit(solution)/shard_map/ppermute | solution.py:328
  40.5 15.3 %all-to-all-start.2 = ((bf16[16,96,128]{2,1,0:T(8,128)(2,1)}), bf16[16,96,128]{2,1,0:T(8,128)(2,1)S(1)}, u32[]{:S(2)}, u32[]{:S(2)}) async-start(bf16[16,96,128]{2,1,0:T(8,128)(2,1)} %get-tuple-element.54), calls=%async_computation.2 | async-start | bytes 786432 | tf_op jit(solution)/shard_map/all_to_all | solution.py:331
  47.4 1.0 %copy-start = (bf16[256,1024]{1,0:T(8,128)(2,1)S(1)}, bf16[256,1024]{1,0:T(8,128)(2,1)}, u32[]{:S(2)}) copy-start(bf16[256,1024]{1,0:T(8,128)(2,1)} %get-tuple-element.55.q_ref) | copy-start | bytes 1572868
  48.4 1.0 %copy-start.1 = (bf16[256,1024]{1,0:T(8,128)(2,1)S(1)}, bf16[256,1024]{1,0:T(8,128)(2,1)}, u32[]{:S(2)}) copy-start(bf16[256,1024]{1,0:T(8,128)(2,1)} %get-tuple-element.57.gc_ref) | copy-start | bytes 1572868
  53.7 5.7 %collective-permute-start.7 = (bf16[2,128,1024]{2,1,0:T(8,128)(2,1)}, bf16[2,128,1024]{2,1,0:T(8,128)(2,1)S(1)}, u32[]{:S(2)}, u32[]{:S(2)}) collective-permute-start(bf16[2,128,1024]{2,1,0:T(8,128)(2,1)} %get-tuple-element.64), channel_id=1, source_target_pairs={{0,1},{1,0},{2,3},{3,2},{4,5},{5,4},{6,7},{7,6},{8,9},{9,8},{10,11... | collective-permute-start | bytes 1572872 | tf_op jit(solution)/shard_map/ppermute | solution.py:324
  56.2 4.4 %collective-permute-start.5 = (bf16[128,1024]{1,0:T(8,128)(2,1)S(1)}, bf16[128,1024]{1,0:T(8,128)(2,1)S(1)}, u32[]{:S(2)}, u32[]{:S(2)}) collective-permute-start(bf16[128,1024]{1,0:T(8,128)(2,1)S(1)} %get-tuple-element.61), channel_id=1, source_target_pairs={{0,1},{1,0},{2,3},{3,2},{4,5},{5,4},{6,7},{7,6},{8,9},{9,8},{10,11... | collective-permute-start | bytes 786440 | tf_op jit(solution)/shard_map/ppermute | solution.py:324
  59.4 1.2 %collective-permute-start.6 = (f32[32,128]{1,0:T(8,128)S(1)}, f32[32,128]{1,0:T(8,128)S(1)}, u32[]{:S(2)}, u32[]{:S(2)}) collective-permute-start(f32[32,128]{1,0:T(8,128)S(1)} %get-tuple-element.62.taps_ref), channel_id=1, source_target_pairs={{0,1},{1,0},{2,3},{3,2},{4,5},{5,4},{6,7},{7,6},{8,9},{9,8},{10,11... | collective-permute-start | bytes 49160 | tf_op jit(solution)/shard_map/ppermute | solution.py:324

commit v5 on v4

--- a/solution.py
+++ b/solution.py
@@ -132,6 +132,11 @@
     return first <= lax.broadcasted_iota(jnp.int32, (rows, rows), 1)
 
 
+def tap_states(wide_ref, head, k, parts):
+    for j, part in enumerate(parts):
+        wide_ref[head, j] = dot(k, part.astype(BF16), (0, 0)).astype(BF16)
+
+
 def add_taps(taps_ref, head, grad, parts):
     for j, part in enumerate(parts):
         row = j * HALF + head
@@ -139,7 +144,7 @@
 
 
 def score_kernel(
-    core_ref, q_ref, g_ref, k_ref, v_ref, halo_ref, gc_ref, taps_ref
+    core_ref, q_ref, g_ref, k_ref, v_ref, halo_ref, gc_ref, taps_ref, wide_ref
 ):
     seen = later(q_ref.shape[0])
     for i in range(HALF):
@@ -148,28 +153,62 @@
         score = jnp.where(seen, dot(k, q_ref[:, at], (1, 1)), 0.0).astype(BF16)
         gc = dot(score, g_ref[:, at], (1, 0))
         gc_ref[:, at] = gc.astype(BF16)
-        add_taps(taps_ref, i, gc, lagged(v_ref, halo_ref, at))
-
-
-def conv_kernel(core_ref, k_ref, v_ref, halo_ref, w_ref, c_ref, state_ref):
+        parts = lagged(v_ref, halo_ref, at)
+        add_taps(taps_ref, i, gc, parts)
+        tap_states(wide_ref, i, k, parts)
+
+
+def convolved(w_ref, core, head, parts):
+    taps = tap_rows(w_ref, core, head)
+    acc = taps[0:1] * parts[0]
+    for j in range(1, CW):
+        acc = acc + taps[j : j + 1] * parts[j]
+    return acc
+
+
+def conv_kernel(core_ref, k_ref, v_ref, w_ref, c_ref, state_ref):
+    rows = v_ref.shape[0]
+    body = lax.broadcasted_iota(jnp.int32, (rows, DH), 0) >= HALO
     for i in range(HALF):
         at = columns(i)
-        taps = tap_rows(w_ref, core_ref[0], i)
-        parts = lagged(v_ref, halo_ref, at)
-        acc = taps[0:1] * parts[0]
-        for j in range(1, CW):
-            acc = acc + taps[j : j + 1] * parts[j]
-        c = acc.astype(BF16)
+        v = v_ref[:, at].astype(F32)
+        ext = jnp.concatenate([jnp.zeros((HALO, DH), F32), v], axis=0)
+        parts = [ext[HALO - j : HALO - j + rows] for j in range(CW)]
+        c = jnp.where(body, convolved(w_ref, core_ref[0], i, parts), 0.0).astype(BF16)
         c_ref[:, at] = c
-        state_ref[i] = dot(k_ref[:, at], c, (0, 0)).astype(BF16)
-
-
-def turn_kernel(core_ref, q_ref, state_ref, out_ref, done_ref, *, order):
+        state_ref[i] = dot(k_ref[:, at], c, (0, 0))
+
+
+def turn_kernel(
+    core_ref,
+    q_ref,
+    state_ref,
+    k_ref,
+    v_ref,
+    halo_ref,
+    w_ref,
+    out_ref,
+    head_ref,
+    done_ref,
+    *,
+    order,
+):
+    depth = q_ref.shape[1]
+    for i in range(HALF):
+        at = columns(i)
+        start = v_ref[:HALO, at].astype(F32)
+        ext = jnp.concatenate([halo_ref[:, at].astype(F32), start], axis=0)
+        parts = [ext[HALO - j : 2 * HALO - j] for j in range(CW)]
+        c = convolved(w_ref, core_ref[0], i, parts).astype(BF16)
+        head_ref[:, at] = c
+        state = state_ref[i] + dot(k_ref[:HALO, at], c, (0, 0))
+        for n in range(DH // depth):
+            part = state[n * depth : (n + 1) * depth].astype(BF16)
+            out_ref[i * (DH // depth) + n, 1] = part
     total = jnp.zeros(q_ref.shape[1:], F32)
     for n in reversed(order):
         out_ref[n, 0] = total.astype(BF16)
         total = total + q_ref[n].astype(F32)
-        out_ref[n, 1] = state_ref[n]
     done_ref[...] = jnp.zeros(done_ref.shape, F32)
 
 
@@ -184,53 +223,62 @@
 def tap_kernel(
     core_ref,
     chip_ref,
-    k_ref,
-    v_ref,
-    halo_ref,
+    wide_ref,
     near_ref,
     edge_ref,
     out_ref,
     done_ref,
     taps_ref,
+    hold_ref,
+    weights_ref,
+    sems,
     *,
     scale,
-    order,
-):
-    depth = chip_ref.shape[2]
-    start = out_ref.shape[1] - CW * HALF
-    for i in range(HALF):
-        at = columns(i)
-        suffix = head_state(lambda n: chip_ref[n, 0], i, depth)
-        grad = dot(k_ref[:, at], suffix, (1, 0))
-        add_taps(taps_ref, i, grad, lagged(v_ref, halo_ref, at))
+    places,
+):
+    depth, size = chip_ref.shape[2], hold_ref.shape[1]
+    total = jnp.zeros((depth, DH), F32)
+    for n, slot in places:
+        hold_ref[slot, :depth] = total.astype(BF16)
+        if depth < size:
+            hold_ref[slot, depth:] = jnp.zeros((size - depth, DH), BF16)
+        total = total + chip_ref[n, 1].astype(F32)
+    states = pltpu.make_async_copy(hold_ref, out_ref.at[:, pl.ds(0, size)], sems.at[0])
+    states.start()
+    for i in range(HALF):
+        suffix = head_state(lambda n: chip_ref[n, 0], i, depth).astype(F32)
+        add_taps(taps_ref, i, suffix, [wide_ref[i, j].astype(F32) for j in range(CW)])
     weights = (scale * (near_ref[...] + taps_ref[...])).astype(BF16)
-    total = jnp.zeros((depth, DH), F32)
-    for n in order:
-        out_ref[n, :depth] = total.astype(BF16)
-        if depth < start:
-            out_ref[n, depth:start] = jnp.zeros((start - depth, DH), BF16)
-        total = total + chip_ref[n, 1].astype(F32)
-        out_ref[n, start:] = weights
+    for n in range(weights_ref.shape[0]):
+        weights_ref[n] = weights
+    place = out_ref.at[:, pl.ds(size, CW * HALF)]
+    weights = pltpu.make_async_copy(weights_ref, place, sems.at[1])
+    weights.start()
     done_ref[...] = jnp.zeros(done_ref.shape, F32)
+    states.wait()
+    weights.wait()
 
 
 def query_side_kernel(
     core_ref,
     chip_ref,
-    q_ref,
+    k_ref,
     g_ref,
-    k_ref,
-    c_ref,
-    gc_ref,
+    head_ref,
     edge_ref,
     w_ref,
     done_ref,
+    c_ref,
+    gc_ref,
+    q_ref,
     gk_ref,
     gv_ref,
     send_ref,
     gq_ref,
     own_ref,
+    hold_ref,
     sems,
+    fetch_sems,
     *,
     scale,
 ):
@@ -238,16 +286,25 @@
     rows = k_ref.shape[0]
     depth = chip_ref.shape[2]
     seen = later(rows)
+    fetches = [
+        pltpu.make_async_copy(ref, hold_ref.at[n], fetch_sems.at[n])
+        for n, ref in enumerate((c_ref, q_ref, gc_ref))
+    ]
+    for fetch in fetches:
+        fetch.start()
+    for fetch in fetches:
+        fetch.wait()
     for i in range(HALF):
         at = columns(i)
         suffix = head_state(lambda n: chip_ref[n, 0], i, depth)
-        c, g, k = c_ref[:, at], g_ref[:, at], k_ref[:, at]
+        c = jnp.concatenate([head_ref[:, at], hold_ref[0, HALO:, at]], axis=0)
+        g, k = g_ref[:, at], k_ref[:, at]
         attn = jnp.where(seen.T, dot(g, c, (1, 1)), 0.0)
         gq_ref[:, at] = dot(attn.astype(BF16), k, (1, 0)).astype(BF16)
         turned = jnp.where(seen, dot(c, g, (1, 1)), 0.0)
-        gk = dot(turned.astype(BF16), q_ref[:, at], (1, 0))
+        gk = dot(turned.astype(BF16), hold_ref[1, :, at], (1, 0))
         gk = scale * (gk + dot(c, suffix, (1, 1)))
-        gc = scale * (gc_ref[:, at].astype(F32) + dot(k, suffix, (1, 0)))
+        gc = scale * (hold_ref[2, :, at].astype(F32) + dot(k, suffix, (1, 0)))
         edge = edge_ref[:, at]
         after = dot(edge, suffix, (1, 0))[EDGE:] + edge.astype(F32)[:EDGE]
         ext = jnp.concatenate([gc, scale * after], axis=0)
@@ -274,14 +331,14 @@
 
 
 def key_side_kernel(
-    core_ref, chip_ref, g_ref, gq_ref, own_ref, send_ref, taps_ref, *, scale, depth
+    core_ref, chip_ref, g_ref, gq_ref, own_ref, send_ref, taps_ref, *, scale, depth, slots
 ):
     core = core_ref[0]
     rows = g_ref.shape[0]
     chips, size, _ = chip_ref.shape
     for i in range(HALF):
         at = columns(i)
-        prefix = head_state(lambda n: chip_ref[n, :depth], i, depth)
+        prefix = head_state(lambda n: chip_ref[slots[n], :depth], i, depth)
         gq = scale * (gq_ref[:, at].astype(F32) + dot(g_ref[:, at], prefix, (1, 1)))
         low, high = gq[: rows // 2].astype(BF16), gq[rows // 2 :].astype(BF16)
         own_ref[:, at] = jnp.where(core == 0, low, high)
@@ -296,16 +353,26 @@
     put(recv_ref, 1 - core_ref[0], (gk_ref, gv_ref), sems)
 
 
-def finish_kernel(core_ref, own_ref, recv_ref, taps_ref, far_ref, gq_ref, gw_ref):
+def finish_kernel(
+    core_ref, own_ref, recv_ref, taps_ref, far_ref, gq_ref, gw_ref, hold_ref, sems
+):
     core = core_ref[0]
-    gq_ref[:, half_of(core, WIDE)] = own_ref[...]
-    gq_ref[:, half_of(1 - core, WIDE)] = recv_ref[...]
+    copies = [
+        pltpu.make_async_copy(ref, gq_ref.at[:, half_of(side, WIDE)], sems.at[n])
+        for n, (side, ref) in enumerate(((1 - core, recv_ref), (core, own_ref)))
+    ]
+    for copy in copies:
+        copy.start()
     for side, ref in ((core, taps_ref), (1 - core, far_ref)):
         for i in range(HALF):
             at = pl.ds(pl.multiple_of(side * WIDE + i * DH, DH), DH)
             for j in range(CW):
                 row = j * HALF + i
-                gw_ref[j : j + 1, at] = ref[row : row + 1, :]
+                hold_ref[j : j + 1, at] = ref[row : row + 1, :]
+    copies.append(pltpu.make_async_copy(hold_ref, gw_ref, sems.at[2]))
+    copies[-1].start()
+    for copy in copies:
+        copy.wait()
 
 
 def local(queries, keys, values, grad_out, conv_weight):
@@ -316,9 +383,15 @@
     depth = WIDE // chips
     scale = (DH * rows * count) ** (-0.5)
     core = lax.rem(lax.axis_index("col"), 2).astype(jnp.int32).reshape(1)
-    listed = [r * line + (z + line // 2) % line for z in range(line) for r in range(lines)]
+    half = line // 2
+    along = [z for n in range(half) for z in (half + n, n)]
+    listed = [r * line + z for r in reversed(range(lines)) for z in along]
     groups = [[2 * p + c for p in listed] for c in range(2)]
     order = tuple(listed.index(p) for p in range(chips))
+    final = listed
+    final_groups = [[2 * p + c for p in final] for c in range(2)]
+    places = tuple((order[p], final.index(p)) for p in range(chips))
+    slots = tuple(final.index(p) for p in listed)
 
     def swap(value):
         return lax.ppermute(value, AXES, [(d, d ^ 1) for d in range(count)])
@@ -327,7 +400,7 @@
         pairs = [(d, d + by) for d in range(count) if 0 <= d + by < count]
         return lax.ppermute(value, AXES, pairs)
 
-    def turn(value):
+    def turn(value, groups):
         return lax.all_to_all(value, AXES, 0, 0, axis_index_groups=groups, tiled=True)
 
     pair = shape((2, rows, WIDE))
@@ -337,10 +410,12 @@
     edges = shape((HALO, WIDE))
     flag = shape((8, DH), F32)
     dma = pltpu.SemaphoreType.DMA
-    queries, grad_out, keys, values = (
-        pltpu.with_memory_space_constraint(a, pltpu.HBM)
-        for a in (queries, grad_out, keys, values)
-    )
+    padded = max(depth, HALO)
+
+    def in_hbm(value):
+        return pltpu.with_memory_space_constraint(value, pltpu.HBM)
+
+    queries, grad_out, keys, values = map(in_hbm, (queries, grad_out, keys, values))
     q_keep, q_give = call(
         query_state_kernel,
         (states, states),
@@ -365,7 +440,7 @@
         core,
         [q_keep, q_recv],
     )
-    q_turned = turn(q_sent.reshape(chips, depth, DH))
+    q_turned = turn(q_sent.reshape(chips, depth, DH), groups)
     qg_own, qg_send = call(
         split_kernel,
         (pair, pair),
@@ -385,38 +460,54 @@
         [dma(())],
         made=(VMEM, VMEM, VMEM, ANY),
     )
-    c, k_state = call(conv_kernel, (block, states), core, [k, v, halo, conv_weight])
-    both, turned = call(
+    c, k_state = call(
+        conv_kernel,
+        (far_block, shape((HALF, DH, DH), F32)),
+        core,
+        [k, v, conv_weight],
+    )
+    both, c_head, turned = call(
         functools.partial(turn_kernel, order=order),
-        (shape((chips, 2, depth, DH)), flag),
-        core,
-        [q_turned, k_state.reshape(chips, depth, DH)],
-    )
-    both = turn(both)
-    gc, taps = call(
-        score_kernel, (far_block, shape((CW * HALF, DH), F32)), core, [q, g, k, v, halo]
+        (shape((chips, 2, depth, DH)), edges, flag),
+        core,
+        [q_turned, k_state, k, v, halo, conv_weight],
+    )
+    both = turn(both, groups)
+    gc, taps, wide = call(
+        score_kernel,
+        (far_block, shape((CW * HALF, DH), F32), shape((HALF, CW, DH, DH))),
+        core,
+        [q, g, k, v, halo]
     )
     edge = shifted(edge, -2)
     last, tapped = call(
-        functools.partial(tap_kernel, scale=scale, order=order),
-        (shape((chips, max(depth, HALO) + CW * HALF, DH)), flag),
-        core,
-        [both, k, v, halo, taps, edge],
-        [pltpu.VMEM((CW * HALF, DH), F32)],
-    )
-    last = turn(last)
+        functools.partial(tap_kernel, scale=scale, places=places),
+        (pltpu.HBM((chips, padded + CW * HALF, DH), BF16), flag),
+        core,
+        [both, wide, taps, edge],
+        [
+            pltpu.VMEM((CW * HALF, DH), F32),
+            pltpu.VMEM((chips, padded, DH), BF16),
+            pltpu.VMEM((chips, CW * HALF, DH), BF16),
+            dma((2,)),
+        ],
+        made=(ANY, VMEM),
+    )
+    last = turn(last, final_groups)
     full = shape((rows, width))
     grad_keys, grad_values, kv_give, gq = call(
         functools.partial(query_side_kernel, scale=scale),
         (full, full, pair, block),
         core,
-        [both, q_far, g, k, c, gc, edge, conv_weight, tapped],
-        [pltpu.VMEM((2, rows, WIDE), BF16), dma((2,))],
-        made=(ANY, ANY, VMEM, VMEM),
+        [both, k, g, c_head, edge, conv_weight, tapped, *map(in_hbm, (c, gc, q_far))],
+        [pltpu.VMEM((2, rows, WIDE), BF16), pltpu.VMEM((3, 2 * rows, WIDE), BF16)]
+        + [dma((2,)), dma((3,))],
+        [VMEM] * 7 + [ANY] * 3,
+        (ANY, ANY, VMEM, VMEM),
     )
     kv_got = swap(kv_give)
     q_grad, q_give, taps = call(
-        functools.partial(key_side_kernel, scale=scale, depth=depth),
+        functools.partial(key_side_kernel, scale=scale, depth=depth, slots=slots),
         (shape((rows, WIDE)), shape((rows, WIDE)), shape((CW * HALF, DH), F32)),
         core,
         [last, g, gq],
@@ -434,7 +525,12 @@
         {2: 0, 3: 1},
     )
     grad_queries, grad_weight = call(
-        finish_kernel, (full, shape((CW, width), F32)), core, [q_grad, q_got, taps, far]
+        finish_kernel,
+        (full, shape((CW, width), F32)),
+        core,
+        [q_grad, q_got, taps, far],
+        [pltpu.VMEM((CW, width), F32), dma((3,))],
+        made=(ANY, ANY),
     )
     return grad_queries, grad_keys, grad_values, grad_weight
 

time: 62.4 us -> 60.1 us (0.963)
  local copies, waits for them, and re-layouts: 2.08 us -> 0.01 us
  waiting for transfers between devices: 6.93 us -> 5.11 us
  Pallas kernels: 17.2 us -> 18.7 us
    unnamed x6 -> x2, local copies, waits for them, and re-layouts: 2.08 us -> 0.01 us
    ppermute x2, waiting for transfers between devices: 4.09 us -> 2.4 us  [shifted(): return lax.ppermute(value, AXES, pairs)]
    pallas_call x14, Pallas kernels: 17.2 us -> 18.7 us  [call(): pl.pallas_call(kernel, out_shape=outs, in_specs=[SMEM] + (given or [VMEM]...]
  transfers between devices with their start and end apart: 11 -> 11, of which waited for: 5 -> 5; matrix products, arithmetic and copies ran while one was open for 0% -> 0% of each run, Pallas kernels for 20% -> 24%
where the time goes in v5:
time: 60.1 us; the launch traced here: 59.2 us
  starting transfers between devices  34.7 us (58%)
  Pallas kernels  18.7 us (31%)
  waiting for transfers between devices  5.11 us (9%)
  between operations  0.75 us (1%)
    all_to_all x3, starting transfers between devices, turn(): lax.all_to_all(value, AXES, 0, 0, axis_index_groups=groups, tiled=True)  22.7 us
    pallas_call x14, Pallas kernels, call(): pl.pallas_call(kernel, out_shape=outs, in_specs=[SMEM] + (given or [VMEM]...  18.7 us
    ppermute x6, starting transfers between devices, swap(): return lax.ppermute(value, AXES, [(d, d ^ 1) for d in range(count)])  8.5 us
    ppermute x2, starting transfers between devices, shifted(): return lax.ppermute(value, AXES, pairs)  3.5 us
    ppermute x2, waiting for transfers between devices, shifted(): return lax.ppermute(value, AXES, pairs)  2.4 us
    ppermute x6, waiting for transfers between devices, swap(): return lax.ppermute(value, AXES, [(d, d ^ 1) for d in range(count)])  1.84 us
  transfers between devices with their start and end apart: 11, of which 5 were waited for; matrix products, arithmetic and copies ran while one was open for 0% of the time, Pallas kernels for 24%

profile of v5, /device:TPU:1, one launch (start us, length us, event | category | flops | bytes accessed | tf_op | source)
XLA Modules:
  0.0 59.2 jit_solution(8142612133909698062)
XLA Ops:
  0.6 1.7 %shard_map.84 = (bf16[8,128,128]{2,1,0:T(8,128)(2,1)S(1)}, bf16[8,128,128]{2,1,0:T(8,128)(2,1)S(1)}) custom-call(s32[1]{0:T(128)} %bitcast.core_ref, bf16[128,2048]{1,0:T(8,128)(2,1)} %a_ref.3, bf16[128,2048]{1,0:T(8,128)(2,1)} %b_ref.3), custom_call_target="tpu_custom_call" | custom-call | tf_op jit(solution)/shard_map/pallas_call | solution.py:39
  2.3 0.1 collective-permute-start
  2.5 1.2 %shard_map.86 = (bf16[2,128,1024]{2,1,0:T(8,128)(2,1)S(1)}, bf16[2,128,1024]{2,1,0:T(8,128)(2,1)S(1)}) custom-call(s32[1]{0:T(128)} %bitcast.core_ref, bf16[128,2048]{1,0:T(8,128)(2,1)} %a_ref.2, bf16[128,2048]{1,0:T(8,128)(2,1)} %b_ref.2, bf16[8,128,128]{2,1,0:T(8,128)(2,1)S(1)} %get-tuple-element.39.keep_ref.after_ref), custom_call_target="tpu_custom_call" | custom-call | tf_op jit(solution)/shard_map/pallas_call | solution.py:39
  3.7 0.5 collective-permute-start.1
  4.2 0.0 collective-permute-done.recv_ref
  4.2 0.8 %shard_map.85 = (bf16[8,128,128]{2,1,0:T(8,128)(2,1)}, f32[8,128]{1,0:T(8,128)S(1)}) custom-call(s32[1]{0:T(128)} %bitcast.core_ref, bf16[8,128,128]{2,1,0:T(8,128)(2,1)S(1)} %get-tuple-element.39.keep_ref.after_ref, bf16[8,128,128]{2,1,0:T(8,128)(2,1)S(1)} %collective-permute-done.recv_ref), custom_call_target="tpu_custom_call" | custom-call | tf_op jit(solution)/shard_map/pallas_call | solution.py:39
  5.0 8.6 %all-to-all-start = ((bf16[16,64,128]{2,1,0:T(8,128)(2,1)}), bf16[16,64,128]{2,1,0:T(8,128)(2,1)S(1)}, u32[]{:S(2)}, u32[]{:S(2)}) async-start(bf16[16,64,128]{2,1,0:T(8,128)(2,1)} %bitcast.1), calls=%async_computation | async-start | bytes 524288 | tf_op jit(solution)/shard_map/all_to_all | solution.py:404
  13.6 0.0 copy-start
  13.6 0.1 shard_map.87
  13.7 2.2 %collective-permute-start.2 = (bf16[16,1024]{1,0:T(8,128)(2,1)S(1)}, bf16[16,1024]{1,0:T(8,128)(2,1)S(1)}, u32[]{:S(2)}, u32[]{:S(2)}) collective-permute-start(bf16[16,1024]{1,0:T(8,128)(2,1)S(1)} %get-tuple-element.47), channel_id=1, source_target_pairs={{0,2},{1,3},{2,4},{3,5},{4,6},{5,7},{6,8},{7,9},{8,10},{9,11},{10,... | collective-permute-start | bytes 98312 | tf_op jit(solution)/shard_map/ppermute | solution.py:401
  15.9 1.5 %shard_map.88 = (bf16[256,1024]{1,0:T(8,128)(2,1)}, f32[8,128,128]{2,1,0:T(8,128)S(1)}) custom-call(s32[1]{0:T(128)} %bitcast.core_ref, bf16[256,1024]{1,0:T(8,128)(2,1)S(1)} %get-tuple-element.44.k_ref, bf16[256,1024]{1,0:T(8,128)(2,1)S(1)} %get-tuple-element.45.v_ref, f32[4,2048]{1,0:T(4,128)S(1)} %copy-done), custom_call_target="tpu_custom_call" | custom-call | tf_op jit(solution)/shard_map/pallas_call | solution.py:39
  17.4 0.9 %collective-permute-done.2.halo_ref = bf16[16,1024]{1,0:T(8,128)(2,1)S(1)} collective-permute-done((bf16[16,1024]{1,0:T(8,128)(2,1)S(1)}, bf16[16,1024]{1,0:T(8,128)(2,1)S(1)}, u32[]{:S(2)}, u32[]{:S(2)}) %collective-permute-start.2) | collective-permute-done | bytes 32800 | tf_op jit(solution)/shard_map/ppermute | solution.py:401
  18.3 0.9 %all-to-all-done.q_ref = bf16[16,64,128]{2,1,0:T(8,128)(2,1)S(1)} async-done(((bf16[16,64,128]{2,1,0:T(8,128)(2,1)}), bf16[16,64,128]{2,1,0:T(8,128)(2,1)S(1)}, u32[]{:S(2)}, u32[]{:S(2)}) %all-to-all-start) | async-done | bytes 262176 | tf_op jit(solution)/shard_map/all_to_all | solution.py:404
  19.1 1.1 %shard_map.89 = (bf16[16,2,64,128]{3,2,1,0:T(8,128)(2,1)}, bf16[16,1024]{1,0:T(8,128)(2,1)S(1)}, f32[8,128]{1,0:T(8,128)}) custom-call(s32[1]{0:T(128)} %bitcast.core_ref, bf16[16,64,128]{2,1,0:T(8,128)(2,1)S(1)} %all-to-all-done.q_ref, f32[8,128,128]{2,1,0:T(8,128)S(1)} %get-tuple-element.46.state_ref, bf16[256,1024]{1,0:T(8,128)(2,1)S(1)} %get-tuple-element.44.k_ref, ...), custom_call_target="tpu_custom_call" | custom-call | tf_op jit(solution)/shard_map/pallas_call | solution.py:39
  20.2 7.3 %all-to-all-start.1 = ((bf16[16,2,64,128]{3,2,1,0:T(8,128)(2,1)}), bf16[16,2,64,128]{3,2,1,0:T(8,128)(2,1)S(1)}, u32[]{:S(2)}, u32[]{:S(2)}) async-start(bf16[16,2,64,128]{3,2,1,0:T(8,128)(2,1)} %get-tuple-element.48), calls=%async_computation.1 | async-start | bytes 1048576 | tf_op jit(solution)/shard_map/all_to_all | solution.py:404
  27.5 1.2 %shard_map.90 = (bf16[2,128,1024]{2,1,0:T(8,128)(2,1)S(1)}, bf16[2,128,1024]{2,1,0:T(8,128)(2,1)S(1)}) custom-call(s32[1]{0:T(128)} %bitcast.core_ref, bf16[128,2048]{1,0:T(8,128)(2,1)} %a_ref.3, bf16[128,2048]{1,0:T(8,128)(2,1)} %b_ref.3, f32[8,128]{1,0:T(8,128)S(1)} %get-tuple-element.49.after_ref), custom_call_target="tpu_custom_call" | custom-call | tf_op jit(solution)/shard_map/pallas_call | solution.py:39
  28.7 2.5 %collective-permute-start.3 = (bf16[2,128,1024]{2,1,0:T(8,128)(2,1)S(1)}, bf16[2,128,1024]{2,1,0:T(8,128)(2,1)S(1)}, u32[]{:S(2)}, u32[]{:S(2)}) collective-permute-start(bf16[2,128,1024]{2,1,0:T(8,128)(2,1)S(1)} %get-tuple-element.51), channel_id=1, source_target_pairs={{0,1},{1,0},{2,3},{3,2},{4,5},{5,4},{6,7},{7,6},{8,9},{9,8},{10,11... | collective-permute-start | bytes 1572872 | tf_op jit(solution)/shard_map/ppermute | solution.py:397
  31.3 1.5 %collective-permute-done.3.recv_ref = bf16[2,128,1024]{2,1,0:T(8,128)(2,1)S(1)} collective-permute-done((bf16[2,128,1024]{2,1,0:T(8,128)(2,1)S(1)}, bf16[2,128,1024]{2,1,0:T(8,128)(2,1)S(1)}, u32[]{:S(2)}, u32[]{:S(2)}) %collective-permute-start.3) | collective-permute-done | bytes 524320 | tf_op jit(solution)/shard_map/ppermute | solution.py:397
  32.8 0.9 %shard_map.91 = (bf16[256,1024]{1,0:T(8,128)(2,1)S(1)}, bf16[256,1024]{1,0:T(8,128)(2,1)S(1)}, bf16[16,1024]{1,0:T(8,128)(2,1)S(1)}, bf16[256,1024]{1,0:T(8,128)(2,1)}) custom-call(s32[1]{0:T(128)} %bitcast.core_ref, bf16[2,128,1024]{2,1,0:T(8,128)(2,1)S(1)} %get-tuple-element.50.own_ref, bf16[2,128,1024]{2,1,0:T(8,128)(2,1)S(1)} %collective-permute-done.3.recv_ref, ...), custom_call_target="tpu_custom_call" | custom-call | tf_op jit(solution)/shard_map/pallas_call | solution.py:39
  33.7 1.3 %collective-permute-start.4 = (bf16[16,1024]{1,0:T(8,128)(2,1)S(1)}, bf16[16,1024]{1,0:T(8,128)(2,1)S(1)}, u32[]{:S(2)}, u32[]{:S(2)}) collective-permute-start(bf16[16,1024]{1,0:T(8,128)(2,1)S(1)} %get-tuple-element.56), channel_id=1, source_target_pairs={{2,0},{3,1},{4,2},{5,3},{6,4},{7,5},{8,6},{9,7},{10,8},{11,9},{12,... | collective-permute-start | bytes 98312 | tf_op jit(solution)/shard_map/ppermute | solution.py:401
  35.0 2.5 %shard_map.92 = (bf16[256,1024]{1,0:T(8,128)(2,1)}, f32[32,128]{1,0:T(8,128)S(1)}, bf16[8,4,128,128]{3,2,1,0:T(8,128)(2,1)S(1)}) custom-call(s32[1]{0:T(128)} %bitcast.core_ref, bf16[256,1024]{1,0:T(8,128)(2,1)S(1)} %get-tuple-element.52.q_ref, bf16[256,1024]{1,0:T(8,128)(2,1)S(1)} %get-tuple-element.53.g_ref, ...), custom_call_target="tpu_custom_call" | custom-call | tf_op jit(solution)/shard_map/pallas_call | solution.py:39
  37.5 1.5 %collective-permute-done.4.edge_ref = bf16[16,1024]{1,0:T(8,128)(2,1)S(1)} collective-permute-done((bf16[16,1024]{1,0:T(8,128)(2,1)S(1)}, bf16[16,1024]{1,0:T(8,128)(2,1)S(1)}, u32[]{:S(2)}, u32[]{:S(2)}) %collective-permute-start.4) | collective-permute-done | bytes 32800 | tf_op jit(solution)/shard_map/ppermute | solution.py:401
  39.0 1.0 %shard_map.93 = (bf16[16,96,128]{2,1,0:T(8,128)(2,1)}, f32[8,128]{1,0:T(8,128)S(1)}) custom-call(s32[1]{0:T(128)} %bitcast.core_ref, bf16[16,2,64,128]{3,2,1,0:T(8,128)(2,1)S(1)} %all-to-all-done.1.chip_ref, bf16[8,4,128,128]{3,2,1,0:T(8,128)(2,1)S(1)} %get-tuple-element.54.wide_ref, f32[32,128]{1,0:T(8,128)S(1)} %get-tuple-element.55.near_ref, ...), custom_call_target="tpu_custom_call" | custom-call | tf_op jit(solution)/shard_map/pallas_call | solution.py:39
  40.0 6.8 %all-to-all-start.2 = ((bf16[16,96,128]{2,1,0:T(8,128)(2,1)}), bf16[16,96,128]{2,1,0:T(8,128)(2,1)S(1)}, u32[]{:S(2)}, u32[]{:S(2)}) async-start(bf16[16,96,128]{2,1,0:T(8,128)(2,1)} %get-tuple-element.57), calls=%async_computation.2 | async-start | bytes 786432 | tf_op jit(solution)/shard_map/all_to_all | solution.py:404
  46.8 4.8 %shard_map.94 = (bf16[128,2048]{1,0:T(8,128)(2,1)}, bf16[128,2048]{1,0:T(8,128)(2,1)}, bf16[2,128,1024]{2,1,0:T(8,128)(2,1)S(1)}, bf16[256,1024]{1,0:T(8,128)(2,1)S(1)}) custom-call(s32[1]{0:T(128)} %bitcast.core_ref, bf16[16,2,64,128]{3,2,1,0:T(8,128)(2,1)S(1)} %all-to-all-done.1.chip_ref, bf16[256,1024]{1,0:T(8,128)(2,1)S(1)} %get-tuple-element.44.k_ref, ...), custom_call_target="tpu_custom_call" | custom-call | tf_op jit(solution)/shard_map/pallas_call | solution.py:39
  51.6 2.0 %collective-permute-start.7 = (bf16[2,128,1024]{2,1,0:T(8,128)(2,1)S(1)}, bf16[2,128,1024]{2,1,0:T(8,128)(2,1)S(1)}, u32[]{:S(2)}, u32[]{:S(2)}) collective-permute-start(bf16[2,128,1024]{2,1,0:T(8,128)(2,1)S(1)} %get-tuple-element.68), channel_id=1, source_target_pairs={{0,1},{1,0},{2,3},{3,2},{4,5},{5,4},{6,7},{7,6},{8,9},{9,8},{10,11... | collective-permute-start | bytes 1572872 | tf_op jit(solution)/shard_map/ppermute | solution.py:397
  53.7 0.4 shard_map.95
  54.0 3.2 %collective-permute-start.5 = (bf16[128,1024]{1,0:T(8,128)(2,1)S(1)}, bf16[128,1024]{1,0:T(8,128)(2,1)S(1)}, u32[]{:S(2)}, u32[]{:S(2)}) collective-permute-start(bf16[128,1024]{1,0:T(8,128)(2,1)S(1)} %get-tuple-element.65), channel_id=1, source_target_pairs={{0,1},{1,0},{2,3},{3,2},{4,5},{5,4},{6,7},{7,6},{8,9},{9,8},{10,11... | collective-permute-start | bytes 786440 | tf_op jit(solution)/shard_map/ppermute | solution.py:397
  57.2 0.1 collective-permute-start.6
  57.3 0.8 %shard_map.97 = (bf16[128,2048]{1,0:T(8,128)(2,1)}, bf16[128,2048]{1,0:T(8,128)(2,1)}) custom-call(s32[1]{0:T(128)} %bitcast.core_ref, bf16[2,128,1024]{2,1,0:T(8,128)(2,1)S(1)} %collective-permute-done.7.recv_ref, bf16[128,2048]{1,0:T(8,128)(2,1)} %get-tuple-element.69._, ...), custom_call_target="tpu_custom_call", output_to_operand_aliasing={{0}: (2, {}), {1}: (3, {})} | custom-call | tf_op jit(solution)/shard_map/pallas_call | solution.py:39
  58.1 0.3 collective-permute-done.6.far_ref
  58.4 0.8 %shard_map.96 = (bf16[128,2048]{1,0:T(8,128)(2,1)}, f32[4,2048]{1,0:T(4,128)}) custom-call(s32[1]{0:T(128)} %bitcast.core_ref, bf16[128,1024]{1,0:T(8,128)(2,1)S(1)} %get-tuple-element.64.own_ref, bf16[128,1024]{1,0:T(8,128)(2,1)S(1)} %collective-permute-done.5.recv_ref, f32[32,128]{1,0:T(8,128)S(1)} %get-tuple-element.66.taps_ref, ...), custom_call_target="tpu_custom_call" | custom-call | tf_op jit(solution)/shard_map/pallas_call | solution.py:39
  (6 shorter events, 0.0 us)
Async XLA Ops:
  2.3 1.9 %collective-permute-start = (bf16[8,128,128]{2,1,0:T(8,128)(2,1)S(1)}, bf16[8,128,128]{2,1,0:T(8,128)(2,1)S(1)}, u32[]{:S(2)}, u32[]{:S(2)}) collective-permute-start(bf16[8,128,128]{2,1,0:T(8,128)(2,1)S(1)} %get-tuple-element.40), channel_id=1, source_target_pairs={{0,1},{1,0},{2,3},{3,2},{4,5},{5,4},{6,7},{7,6},{8,9},{9,8},{10,11... | collective-permute-start | bytes 786440 | tf_op jit(solution)/shard_map/ppermute | solution.py:397
  3.7 9.9 %collective-permute-start.1 = (bf16[2,128,1024]{2,1,0:T(8,128)(2,1)S(1)}, bf16[2,128,1024]{2,1,0:T(8,128)(2,1)S(1)}, u32[]{:S(2)}, u32[]{:S(2)}) collective-permute-start(bf16[2,128,1024]{2,1,0:T(8,128)(2,1)S(1)} %get-tuple-element.43), channel_id=1, source_target_pairs={{0,1},{1,0},{2,3},{3,2},{4,5},{5,4},{6,7},{7,6},{8,9},{9,8},{10,11... | collective-permute-start | bytes 1572872 | tf_op jit(solution)/shard_map/ppermute | solution.py:397
  5.0 14.2 %all-to-all-start = ((bf16[16,64,128]{2,1,0:T(8,128)(2,1)}), bf16[16,64,128]{2,1,0:T(8,128)(2,1)S(1)}, u32[]{:S(2)}, u32[]{:S(2)}) async-start(bf16[16,64,128]{2,1,0:T(8,128)(2,1)} %bitcast.1), calls=%async_computation | async-start | bytes 524288 | tf_op jit(solution)/shard_map/all_to_all | solution.py:404
  13.6 2.3 %copy-start = (f32[4,2048]{1,0:T(4,128)S(1)}, f32[4,2048]{1,0:T(4,128)}, u32[]{:S(2)}) copy-start(f32[4,2048]{1,0:T(4,128)} %w_ref.5) | copy-start | bytes 98308
  13.7 4.6 %collective-permute-start.2 = (bf16[16,1024]{1,0:T(8,128)(2,1)S(1)}, bf16[16,1024]{1,0:T(8,128)(2,1)S(1)}, u32[]{:S(2)}, u32[]{:S(2)}) collective-permute-start(bf16[16,1024]{1,0:T(8,128)(2,1)S(1)} %get-tuple-element.47), channel_id=1, source_target_pairs={{0,2},{1,3},{2,4},{3,5},{4,6},{5,7},{6,8},{7,9},{8,10},{9,11},{10,... | collective-permute-start | bytes 98312 | tf_op jit(solution)/shard_map/ppermute | solution.py:401
  20.2 18.8 %all-to-all-start.1 = ((bf16[16,2,64,128]{3,2,1,0:T(8,128)(2,1)}), bf16[16,2,64,128]{3,2,1,0:T(8,128)(2,1)S(1)}, u32[]{:S(2)}, u32[]{:S(2)}) async-start(bf16[16,2,64,128]{3,2,1,0:T(8,128)(2,1)} %get-tuple-element.48), calls=%async_computation.1 | async-start | bytes 1048576 | tf_op jit(solution)/shard_map/all_to_all | solution.py:404
  28.7 4.1 %collective-permute-start.3 = (bf16[2,128,1024]{2,1,0:T(8,128)(2,1)S(1)}, bf16[2,128,1024]{2,1,0:T(8,128)(2,1)S(1)}, u32[]{:S(2)}, u32[]{:S(2)}) collective-permute-start(bf16[2,128,1024]{2,1,0:T(8,128)(2,1)S(1)} %get-tuple-element.51), channel_id=1, source_target_pairs={{0,1},{1,0},{2,3},{3,2},{4,5},{5,4},{6,7},{7,6},{8,9},{9,8},{10,11... | collective-permute-start | bytes 1572872 | tf_op jit(solution)/shard_map/ppermute | solution.py:397
  33.7 5.2 %collective-permute-start.4 = (bf16[16,1024]{1,0:T(8,128)(2,1)S(1)}, bf16[16,1024]{1,0:T(8,128)(2,1)S(1)}, u32[]{:S(2)}, u32[]{:S(2)}) collective-permute-start(bf16[16,1024]{1,0:T(8,128)(2,1)S(1)} %get-tuple-element.56), channel_id=1, source_target_pairs={{2,0},{3,1},{4,2},{5,3},{6,4},{7,5},{8,6},{9,7},{10,8},{11,9},{12,... | collective-permute-start | bytes 98312 | tf_op jit(solution)/shard_map/ppermute | solution.py:401
  40.0 13.7 %all-to-all-start.2 = ((bf16[16,96,128]{2,1,0:T(8,128)(2,1)}), bf16[16,96,128]{2,1,0:T(8,128)(2,1)S(1)}, u32[]{:S(2)}, u32[]{:S(2)}) async-start(bf16[16,96,128]{2,1,0:T(8,128)(2,1)} %get-tuple-element.57), calls=%async_computation.2 | async-start | bytes 786432 | tf_op jit(solution)/shard_map/all_to_all | solution.py:404
  51.6 5.7 %collective-permute-start.7 = (bf16[2,128,1024]{2,1,0:T(8,128)(2,1)S(1)}, bf16[2,128,1024]{2,1,0:T(8,128)(2,1)S(1)}, u32[]{:S(2)}, u32[]{:S(2)}) collective-permute-start(bf16[2,128,1024]{2,1,0:T(8,128)(2,1)S(1)} %get-tuple-element.68), channel_id=1, source_target_pairs={{0,1},{1,0},{2,3},{3,2},{4,5},{5,4},{6,7},{7,6},{8,9},{9,8},{10,11... | collective-permute-start | bytes 1572872 | tf_op jit(solution)/shard_map/ppermute | solution.py:397
  54.0 4.4 %collective-permute-start.5 = (bf16[128,1024]{1,0:T(8,128)(2,1)S(1)}, bf16[128,1024]{1,0:T(8,128)(2,1)S(1)}, u32[]{:S(2)}, u32[]{:S(2)}) collective-permute-start(bf16[128,1024]{1,0:T(8,128)(2,1)S(1)} %get-tuple-element.65), channel_id=1, source_target_pairs={{0,1},{1,0},{2,3},{3,2},{4,5},{5,4},{6,7},{7,6},{8,9},{9,8},{10,11... | collective-permute-start | bytes 786440 | tf_op jit(solution)/shard_map/ppermute | solution.py:397
  57.2 1.2 %collective-permute-start.6 = (f32[32,128]{1,0:T(8,128)S(1)}, f32[32,128]{1,0:T(8,128)S(1)}, u32[]{:S(2)}, u32[]{:S(2)}) collective-permute-start(f32[32,128]{1,0:T(8,128)S(1)} %get-tuple-element.66.taps_ref), channel_id=1, source_target_pairs={{0,1},{1,0},{2,3},{3,2},{4,5},{5,4},{6,7},{7,6},{8,9},{9,8},{10,11... | collective-permute-start | bytes 49160 | tf_op jit(solution)/shard_map/ppermute | solution.py:397

commit v6 on v5

--- a/solution.py
+++ b/solution.py
@@ -12,7 +12,8 @@
 CW = 4
 HALF = HEADS // 2
 WIDE = HALF * DH
-EDGE = 8
+EDGE = 4
+TILE = 8
 HALO = 16
 AXES = ("row", "col")
 F32 = jnp.float32
@@ -51,6 +52,24 @@
     return jax.ShapeDtypeStruct(dims, dtype)
 
 
+def split_key_kernel(
+    core_ref, k_ref, v_ref, q_ref, g_ref, after_ref, own_ref, send_ref, sems
+):
+    core = core_ref[0]
+    rows = k_ref.shape[0]
+    copies = []
+    for n, refs in enumerate(((k_ref, q_ref), (v_ref, g_ref))):
+        for m, (out, side) in enumerate(((send_ref, 1 - core), (own_ref, core))):
+            for e, (ref, first, size) in enumerate(zip(refs, (0, rows), (rows, HALO))):
+                part = ref.at[pl.ds(0, size), half_of(side, WIDE)]
+                place = out.at[n, pl.ds(first, size)]
+                copies.append(pltpu.make_async_copy(part, place, sems.at[n, m, e]))
+    for copy in copies:
+        copy.start()
+    for copy in copies:
+        copy.wait()
+
+
 def split_kernel(core_ref, a_ref, b_ref, after_ref, own_ref, send_ref, sems):
     core = core_ref[0]
     copies = []
@@ -90,37 +109,44 @@
 
 
 def gather(core, own_ref, recv_ref, refs):
-    rows = own_ref.shape[1]
     for n, ref in enumerate(refs):
-        ref[half_of(core, rows), :] = own_ref[n]
-        ref[half_of(1 - core, rows), :] = recv_ref[n]
-
-
-def gather_query_kernel(core_ref, own_ref, recv_ref, k_ref, q_ref, g_ref, edge_ref, far_ref, sem):
+        rows = ref.shape[0] // 2
+        ref[half_of(core, rows), :] = own_ref[n, :rows]
+        ref[half_of(1 - core, rows), :] = recv_ref[n, :rows]
+
+
+def gather_query_kernel(core_ref, own_ref, recv_ref, q_ref, g_ref, far_ref, sem):
     gather(core_ref[0], own_ref, recv_ref, (q_ref, g_ref))
     copy = pltpu.make_async_copy(q_ref, far_ref, sem)
     copy.start()
+    copy.wait()
+
+
+def gather_key_kernel(core_ref, own_ref, recv_ref, k_ref, v_ref, tail_ref, edge_ref):
+    core = core_ref[0]
+    gather(core, own_ref, recv_ref, (k_ref, v_ref))
+    rows = k_ref.shape[0]
+    tails, edges = [], []
     first = lax.broadcasted_iota(jnp.int32, (HALO, HALO), 0)
     unseen = first > lax.broadcasted_iota(jnp.int32, (HALO, HALO), 1)
     for i in range(HALF):
         at = columns(i)
-        q, g, k = q_ref[:HALO, at], g_ref[:HALO, at], k_ref[:HALO, at]
+        q, g = (
+            jnp.where(core == 0, own_ref[n, rows // 2 :, at], recv_ref[n, rows // 2 :, at])
+            for n in range(2)
+        )
+        k = k_ref[:HALO, at]
         score = jnp.where(unseen, dot(k, q, (1, 1)), 0.0).astype(BF16)
-        edge = dot(score, g, (1, 0))
-        both = jnp.concatenate([-edge[:EDGE], k.astype(F32)[:EDGE]], axis=0)
-        edge_ref[:, at] = both.astype(BF16)
-    copy.wait()
-
-
-def gather_key_kernel(core_ref, own_ref, recv_ref, k_ref, v_ref, tail_ref):
-    gather(core_ref[0], own_ref, recv_ref, (k_ref, v_ref))
-    tail_ref[...] = v_ref[v_ref.shape[0] - HALO :, :]
-
-
-def lagged(v_ref, halo_ref, at):
-    ext = jnp.concatenate([halo_ref[:, at].astype(F32), v_ref[:, at].astype(F32)], axis=0)
-    rows = v_ref.shape[0]
-    return [ext[HALO - j : HALO - j + rows] for j in range(CW)]
+        edges += [-dot(score, g, (1, 0))[:EDGE], k.astype(F32)[:EDGE]]
+        tails.append(v_ref[rows - HALO :, at].astype(F32)[HALO - EDGE :])
+    tail_ref[...] = jnp.concatenate(tails, axis=0).astype(BF16)
+    edge_ref[...] = jnp.concatenate(edges, axis=0).astype(BF16)
+
+
+def lagged(v, halo_ref, head):
+    halo = halo_ref[...].astype(F32)[head * EDGE : (head + 1) * EDGE]
+    ext = jnp.concatenate([jnp.zeros((TILE - EDGE, DH), F32), halo, v.astype(F32)], axis=0)
+    return [ext[TILE - j : TILE - j + v.shape[0]] for j in range(CW)]
 
 
 def tap_rows(w_ref, core, head):
@@ -153,7 +179,7 @@
         score = jnp.where(seen, dot(k, q_ref[:, at], (1, 1)), 0.0).astype(BF16)
         gc = dot(score, g_ref[:, at], (1, 0))
         gc_ref[:, at] = gc.astype(BF16)
-        parts = lagged(v_ref, halo_ref, at)
+        parts = lagged(v_ref[:, at], halo_ref, i)
         add_taps(taps_ref, i, gc, parts)
         tap_states(wide_ref, i, k, parts)
 
@@ -196,9 +222,7 @@
     depth = q_ref.shape[1]
     for i in range(HALF):
         at = columns(i)
-        start = v_ref[:HALO, at].astype(F32)
-        ext = jnp.concatenate([halo_ref[:, at].astype(F32), start], axis=0)
-        parts = [ext[HALO - j : 2 * HALO - j] for j in range(CW)]
+        parts = lagged(v_ref[:HALO, at], halo_ref, i)
         c = convolved(w_ref, core_ref[0], i, parts).astype(BF16)
         head_ref[:, at] = c
         state = state_ref[i] + dot(k_ref[:HALO, at], c, (0, 0))
@@ -305,9 +329,9 @@
         gk = dot(turned.astype(BF16), hold_ref[1, :, at], (1, 0))
         gk = scale * (gk + dot(c, suffix, (1, 1)))
         gc = scale * (hold_ref[2, :, at].astype(F32) + dot(k, suffix, (1, 0)))
-        edge = edge_ref[:, at]
-        after = dot(edge, suffix, (1, 0))[EDGE:] + edge.astype(F32)[:EDGE]
-        ext = jnp.concatenate([gc, scale * after], axis=0)
+        edge = edge_ref[...].astype(F32)[2 * EDGE * i : 2 * EDGE * (i + 1)]
+        after = edge[:EDGE] + dot(edge.astype(BF16), suffix, (1, 0))[EDGE:]
+        ext = jnp.concatenate([gc, scale * after, jnp.zeros((TILE - EDGE, DH), F32)], axis=0)
         taps = tap_rows(w_ref, core, i)
         gv = taps[0:1] * gc
         for j in range(1, CW):
@@ -425,13 +449,14 @@
         [ANY] * 2,
     )
     q_recv = swap(q_give)
+    longer = shape((2, rows + HALO, WIDE))
     kv_own, kv_send = call(
-        split_kernel,
-        (pair, pair),
-        core,
-        [keys, values, q_keep],
-        [dma((2, 2))],
-        [ANY, ANY, VMEM],
+        split_key_kernel,
+        (longer, longer),
+        core,
+        [keys, values, queries, grad_out, q_keep],
+        [dma((2, 2, 2))],
+        [ANY] * 4 + [VMEM],
     )
     kv_recv = swap(kv_send)
     q_sent, added = call(
@@ -450,15 +475,20 @@
         [ANY, ANY, VMEM],
     )
     qg_recv = swap(qg_send)
-    k, v, tail = call(gather_key_kernel, (block, block, edges), core, [kv_own, kv_recv])
+    k, v, tail, edge = call(
+        gather_key_kernel,
+        (block, block, shape((EDGE * HALF, DH)), shape((2 * EDGE * HALF, DH))),
+        core,
+        [kv_own, kv_recv],
+    )
     halo = shifted(tail, 2)
-    q, g, edge, q_far = call(
+    q, g, q_far = call(
         gather_query_kernel,
-        (block, block, edges, far_block),
-        core,
-        [qg_own, qg_recv, k],
+        (block, block, far_block),
+        core,
+        [qg_own, qg_recv],
         [dma(())],
-        made=(VMEM, VMEM, VMEM, ANY),
+        made=(VMEM, VMEM, ANY),
     )
     c, k_state = call(
         conv_kernel,

time: 60.1 us -> 58.4 us (0.972)
  waiting for transfers between devices: 5.11 us -> 2.11 us
  starting transfers between devices: 34.7 us -> 35.6 us
    ppermute x2, waiting for transfers between devices: 2.4 us -> 0.16 us  [shifted(): return lax.ppermute(value, AXES, pairs)]
    ppermute x6, waiting for transfers between devices: 1.84 us -> 0.55 us  [swap(): return lax.ppermute(value, AXES, [(d, d ^ 1) for d in range(count)])]
    all_to_all x3, starting transfers between devices: 22.7 us -> 23.6 us  [turn(): lax.all_to_all(value, AXES, 0, 0, axis_index_groups=groups, tiled=True)]
  transfers between devices with their start and end apart: 11 -> 11, of which waited for: 5 -> 4; matrix products, arithmetic and copies ran while one was open for 0% -> 0% of each run, Pallas kernels for 24% -> 25%
where the time goes in v6:
time: 58.4 us; the launch traced here: 57.5 us
  starting transfers between devices  35.6 us (61%)
  Pallas kernels  19.1 us (33%)
  waiting for transfers between devices  2.11 us (4%)
  between operations  0.75 us (1%)
    all_to_all x3, starting transfers between devices, turn(): lax.all_to_all(value, AXES, 0, 0, axis_index_groups=groups, tiled=True)  23.6 us
    pallas_call x14, Pallas kernels, call(): pl.pallas_call(kernel, out_shape=outs, in_specs=[SMEM] + (given or [VMEM]...  19.1 us
    ppermute x6, starting transfers between devices, swap(): return lax.ppermute(value, AXES, [(d, d ^ 1) for d in range(count)])  8.5 us
    ppermute x2, starting transfers between devices, shifted(): return lax.ppermute(value, AXES, pairs)  3.48 us
    all_to_all x3, waiting for transfers between devices, turn(): lax.all_to_all(value, AXES, 0, 0, axis_index_groups=groups, tiled=True)  1.4 us
  transfers between devices with their start and end apart: 11, of which 4 were waited for; matrix products, arithmetic and copies ran while one was open for 0% of the time, Pallas kernels for 25%

profile of v6, /device:TPU:1, one launch (start us, length us, event | category | flops | bytes accessed | tf_op | source)
XLA Modules:
  0.0 57.5 jit_solution(13838778515468536295)
XLA Ops:
  0.6 1.7 %shard_map.84 = (bf16[8,128,128]{2,1,0:T(8,128)(2,1)S(1)}, bf16[8,128,128]{2,1,0:T(8,128)(2,1)S(1)}) custom-call(s32[1]{0:T(128)} %bitcast.core_ref, bf16[128,2048]{1,0:T(8,128)(2,1)} %a_ref.1, bf16[128,2048]{1,0:T(8,128)(2,1)} %b_ref.1), custom_call_target="tpu_custom_call" | custom-call | tf_op jit(solution)/shard_map/pallas_call | solution.py:40
  2.3 0.1 collective-permute-start
  2.5 1.3 %shard_map.86 = (bf16[2,144,1024]{2,1,0:T(8,128)(2,1)S(1)}, bf16[2,144,1024]{2,1,0:T(8,128)(2,1)S(1)}) custom-call(s32[1]{0:T(128)} %bitcast.core_ref, bf16[128,2048]{1,0:T(8,128)(2,1)} %k_ref.1, bf16[128,2048]{1,0:T(8,128)(2,1)} %v_ref.1, bf16[128,2048]{1,0:T(8,128)(2,1)} %a_ref.1, bf16[128,2048]{1,0:T(8,128)(2,1)} %b_ref.1, ...), custom_call_target="tpu_custom_call" | custom-call | tf_op jit(solution)/shard_map/pallas_call | solution.py:40
  3.8 0.5 collective-permute-start.1
  4.3 0.0 collective-permute-done.recv_ref
  4.3 0.8 %shard_map.85 = (bf16[8,128,128]{2,1,0:T(8,128)(2,1)}, f32[8,128]{1,0:T(8,128)S(1)}) custom-call(s32[1]{0:T(128)} %bitcast.core_ref, bf16[8,128,128]{2,1,0:T(8,128)(2,1)S(1)} %get-tuple-element.39.keep_ref.after_ref, bf16[8,128,128]{2,1,0:T(8,128)(2,1)S(1)} %collective-permute-done.recv_ref), custom_call_target="tpu_custom_call" | custom-call | tf_op jit(solution)/shard_map/pallas_call | solution.py:40
  5.1 8.6 %all-to-all-start = ((bf16[16,64,128]{2,1,0:T(8,128)(2,1)}), bf16[16,64,128]{2,1,0:T(8,128)(2,1)S(1)}, u32[]{:S(2)}, u32[]{:S(2)}) async-start(bf16[16,64,128]{2,1,0:T(8,128)(2,1)} %bitcast.1), calls=%async_computation | async-start | bytes 524288 | tf_op jit(solution)/shard_map/all_to_all | solution.py:428
  13.7 0.0 copy-start
  13.7 0.4 shard_map.87
  14.1 2.2 %collective-permute-start.2 = (bf16[32,128]{1,0:T(8,128)(2,1)S(1)}, bf16[32,128]{1,0:T(8,128)(2,1)S(1)}, u32[]{:S(2)}, u32[]{:S(2)}) collective-permute-start(bf16[32,128]{1,0:T(8,128)(2,1)S(1)} %get-tuple-element.47), channel_id=1, source_target_pairs={{0,2},{1,3},{2,4},{3,5},{4,6},{5,7},{6,8},{7,9},{8,10},{9,11},{10,... | collective-permute-start | bytes 24584 | tf_op jit(solution)/shard_map/ppermute | solution.py:425
  16.3 1.5 %shard_map.88 = (bf16[256,1024]{1,0:T(8,128)(2,1)}, f32[8,128,128]{2,1,0:T(8,128)S(1)}) custom-call(s32[1]{0:T(128)} %bitcast.core_ref, bf16[256,1024]{1,0:T(8,128)(2,1)S(1)} %get-tuple-element.44.k_ref, bf16[256,1024]{1,0:T(8,128)(2,1)S(1)} %get-tuple-element.45.v_ref, f32[4,2048]{1,0:T(4,128)S(1)} %copy-done), custom_call_target="tpu_custom_call" | custom-call | tf_op jit(solution)/shard_map/pallas_call | solution.py:40
  17.8 0.0 collective-permute-done.2.halo_ref
  17.8 1.4 %all-to-all-done.q_ref = bf16[16,64,128]{2,1,0:T(8,128)(2,1)S(1)} async-done(((bf16[16,64,128]{2,1,0:T(8,128)(2,1)}), bf16[16,64,128]{2,1,0:T(8,128)(2,1)S(1)}, u32[]{:S(2)}, u32[]{:S(2)}) %all-to-all-start) | async-done | bytes 262176 | tf_op jit(solution)/shard_map/all_to_all | solution.py:428
  19.2 1.1 %shard_map.89 = (bf16[16,2,64,128]{3,2,1,0:T(8,128)(2,1)}, bf16[16,1024]{1,0:T(8,128)(2,1)S(1)}, f32[8,128]{1,0:T(8,128)}) custom-call(s32[1]{0:T(128)} %bitcast.core_ref, bf16[16,64,128]{2,1,0:T(8,128)(2,1)S(1)} %all-to-all-done.q_ref, f32[8,128,128]{2,1,0:T(8,128)S(1)} %get-tuple-element.46.state_ref, bf16[256,1024]{1,0:T(8,128)(2,1)S(1)} %get-tuple-element.44.k_ref, ...), custom_call_target="tpu_custom_call" | custom-call | tf_op jit(solution)/shard_map/pallas_call | solution.py:40
  20.3 7.4 %all-to-all-start.1 = ((bf16[16,2,64,128]{3,2,1,0:T(8,128)(2,1)}), bf16[16,2,64,128]{3,2,1,0:T(8,128)(2,1)S(1)}, u32[]{:S(2)}, u32[]{:S(2)}) async-start(bf16[16,2,64,128]{3,2,1,0:T(8,128)(2,1)} %get-tuple-element.48), calls=%async_computation.1 | async-start | bytes 1048576 | tf_op jit(solution)/shard_map/all_to_all | solution.py:428
  27.7 1.2 %shard_map.90 = (bf16[2,128,1024]{2,1,0:T(8,128)(2,1)S(1)}, bf16[2,128,1024]{2,1,0:T(8,128)(2,1)S(1)}) custom-call(s32[1]{0:T(128)} %bitcast.core_ref, bf16[128,2048]{1,0:T(8,128)(2,1)} %a_ref.1, bf16[128,2048]{1,0:T(8,128)(2,1)} %b_ref.1, f32[8,128]{1,0:T(8,128)S(1)} %get-tuple-element.49.after_ref), custom_call_target="tpu_custom_call" | custom-call | tf_op jit(solution)/shard_map/pallas_call | solution.py:40
  28.9 2.5 %collective-permute-start.3 = (bf16[2,128,1024]{2,1,0:T(8,128)(2,1)S(1)}, bf16[2,128,1024]{2,1,0:T(8,128)(2,1)S(1)}, u32[]{:S(2)}, u32[]{:S(2)}) collective-permute-start(bf16[2,128,1024]{2,1,0:T(8,128)(2,1)S(1)} %get-tuple-element.51), channel_id=1, source_target_pairs={{0,1},{1,0},{2,3},{3,2},{4,5},{5,4},{6,7},{7,6},{8,9},{9,8},{10,11... | collective-permute-start | bytes 1572872 | tf_op jit(solution)/shard_map/ppermute | solution.py:421
  31.5 1.3 %collective-permute-start.4 = (bf16[64,128]{1,0:T(8,128)(2,1)S(1)}, bf16[64,128]{1,0:T(8,128)(2,1)S(1)}, u32[]{:S(2)}, u32[]{:S(2)}) collective-permute-start(bf16[64,128]{1,0:T(8,128)(2,1)S(1)} %get-tuple-element.56), channel_id=1, source_target_pairs={{2,0},{3,1},{4,2},{5,3},{6,4},{7,5},{8,6},{9,7},{10,8},{11,9},{12,... | collective-permute-start | bytes 49160 | tf_op jit(solution)/shard_map/ppermute | solution.py:425
  32.7 0.2 collective-permute-done.3.recv_ref
  33.0 0.9 %shard_map.91 = (bf16[256,1024]{1,0:T(8,128)(2,1)S(1)}, bf16[256,1024]{1,0:T(8,128)(2,1)S(1)}, bf16[256,1024]{1,0:T(8,128)(2,1)}) custom-call(s32[1]{0:T(128)} %bitcast.core_ref, bf16[2,128,1024]{2,1,0:T(8,128)(2,1)S(1)} %get-tuple-element.50.own_ref, bf16[2,128,1024]{2,1,0:T(8,128)(2,1)S(1)} %collective-permute-done.3.recv_ref), custom_call_target="tpu_custom_call" | custom-call | tf_op jit(solution)/shard_map/pallas_call | solution.py:40
  33.8 2.5 %shard_map.92 = (bf16[256,1024]{1,0:T(8,128)(2,1)}, f32[32,128]{1,0:T(8,128)S(1)}, bf16[8,4,128,128]{3,2,1,0:T(8,128)(2,1)S(1)}) custom-call(s32[1]{0:T(128)} %bitcast.core_ref, bf16[256,1024]{1,0:T(8,128)(2,1)S(1)} %get-tuple-element.52.q_ref, bf16[256,1024]{1,0:T(8,128)(2,1)S(1)} %get-tuple-element.53.g_ref, ...), custom_call_target="tpu_custom_call" | custom-call | tf_op jit(solution)/shard_map/pallas_call | solution.py:40
  36.3 0.1 collective-permute-done.4.edge_ref
  36.4 1.0 %shard_map.93 = (bf16[16,96,128]{2,1,0:T(8,128)(2,1)}, f32[8,128]{1,0:T(8,128)S(1)}) custom-call(s32[1]{0:T(128)} %bitcast.core_ref, bf16[16,2,64,128]{3,2,1,0:T(8,128)(2,1)S(1)} %all-to-all-done.1.chip_ref, bf16[8,4,128,128]{3,2,1,0:T(8,128)(2,1)S(1)} %get-tuple-element.54.wide_ref, f32[32,128]{1,0:T(8,128)S(1)} %get-tuple-element.55.near_ref, ...), custom_call_target="tpu_custom_call" | custom-call | tf_op jit(solution)/shard_map/pallas_call | solution.py:40
  37.4 7.6 %all-to-all-start.2 = ((bf16[16,96,128]{2,1,0:T(8,128)(2,1)}), bf16[16,96,128]{2,1,0:T(8,128)(2,1)S(1)}, u32[]{:S(2)}, u32[]{:S(2)}) async-start(bf16[16,96,128]{2,1,0:T(8,128)(2,1)} %get-tuple-element.57), calls=%async_computation.2 | async-start | bytes 786432 | tf_op jit(solution)/shard_map/all_to_all | solution.py:428
  45.0 4.9 %shard_map.94 = (bf16[128,2048]{1,0:T(8,128)(2,1)}, bf16[128,2048]{1,0:T(8,128)(2,1)}, bf16[2,128,1024]{2,1,0:T(8,128)(2,1)S(1)}, bf16[256,1024]{1,0:T(8,128)(2,1)S(1)}) custom-call(s32[1]{0:T(128)} %bitcast.core_ref, bf16[16,2,64,128]{3,2,1,0:T(8,128)(2,1)S(1)} %all-to-all-done.1.chip_ref, bf16[256,1024]{1,0:T(8,128)(2,1)S(1)} %get-tuple-element.44.k_ref, ...), custom_call_target="tpu_custom_call" | custom-call | tf_op jit(solution)/shard_map/pallas_call | solution.py:40
  49.9 3.1 %collective-permute-start.7 = (bf16[2,128,1024]{2,1,0:T(8,128)(2,1)S(1)}, bf16[2,128,1024]{2,1,0:T(8,128)(2,1)S(1)}, u32[]{:S(2)}, u32[]{:S(2)}) collective-permute-start(bf16[2,128,1024]{2,1,0:T(8,128)(2,1)S(1)} %get-tuple-element.68), channel_id=1, source_target_pairs={{0,1},{1,0},{2,3},{3,2},{4,5},{5,4},{6,7},{7,6},{8,9},{9,8},{10,11... | collective-permute-start | bytes 1572872 | tf_op jit(solution)/shard_map/ppermute | solution.py:421
  53.0 0.4 shard_map.95
  53.4 2.1 %collective-permute-start.5 = (bf16[128,1024]{1,0:T(8,128)(2,1)S(1)}, bf16[128,1024]{1,0:T(8,128)(2,1)S(1)}, u32[]{:S(2)}, u32[]{:S(2)}) collective-permute-start(bf16[128,1024]{1,0:T(8,128)(2,1)S(1)} %get-tuple-element.65), channel_id=1, source_target_pairs={{0,1},{1,0},{2,3},{3,2},{4,5},{5,4},{6,7},{7,6},{8,9},{9,8},{10,11... | collective-permute-start | bytes 786440 | tf_op jit(solution)/shard_map/ppermute | solution.py:421
  55.5 0.1 collective-permute-start.6
  55.6 0.8 %shard_map.97 = (bf16[128,2048]{1,0:T(8,128)(2,1)}, bf16[128,2048]{1,0:T(8,128)(2,1)}) custom-call(s32[1]{0:T(128)} %bitcast.core_ref, bf16[2,128,1024]{2,1,0:T(8,128)(2,1)S(1)} %collective-permute-done.7.recv_ref, bf16[128,2048]{1,0:T(8,128)(2,1)} %get-tuple-element.69._, ...), custom_call_target="tpu_custom_call", output_to_operand_aliasing={{0}: (2, {}), {1}: (3, {})} | custom-call | tf_op jit(solution)/shard_map/pallas_call | solution.py:40
  56.4 0.3 collective-permute-done.6.far_ref
  56.7 0.8 %shard_map.96 = (bf16[128,2048]{1,0:T(8,128)(2,1)}, f32[4,2048]{1,0:T(4,128)}) custom-call(s32[1]{0:T(128)} %bitcast.core_ref, bf16[128,1024]{1,0:T(8,128)(2,1)S(1)} %get-tuple-element.64.own_ref, bf16[128,1024]{1,0:T(8,128)(2,1)S(1)} %collective-permute-done.5.recv_ref, f32[32,128]{1,0:T(8,128)S(1)} %get-tuple-element.66.taps_ref, ...), custom_call_target="tpu_custom_call" | custom-call | tf_op jit(solution)/shard_map/pallas_call | solution.py:40
  (6 shorter events, 0.0 us)
Async XLA Ops:
  2.3 2.0 %collective-permute-start = (bf16[8,128,128]{2,1,0:T(8,128)(2,1)S(1)}, bf16[8,128,128]{2,1,0:T(8,128)(2,1)S(1)}, u32[]{:S(2)}, u32[]{:S(2)}) collective-permute-start(bf16[8,128,128]{2,1,0:T(8,128)(2,1)S(1)} %get-tuple-element.40), channel_id=1, source_target_pairs={{0,1},{1,0},{2,3},{3,2},{4,5},{5,4},{6,7},{7,6},{8,9},{9,8},{10,11... | collective-permute-start | bytes 786440 | tf_op jit(solution)/shard_map/ppermute | solution.py:421
  3.8 9.9 %collective-permute-start.1 = (bf16[2,144,1024]{2,1,0:T(8,128)(2,1)S(1)}, bf16[2,144,1024]{2,1,0:T(8,128)(2,1)S(1)}, u32[]{:S(2)}, u32[]{:S(2)}) collective-permute-start(bf16[2,144,1024]{2,1,0:T(8,128)(2,1)S(1)} %get-tuple-element.43), channel_id=1, source_target_pairs={{0,1},{1,0},{2,3},{3,2},{4,5},{5,4},{6,7},{7,6},{8,9},{9,8},{10,11... | collective-permute-start | bytes 1769480 | tf_op jit(solution)/shard_map/ppermute | solution.py:421
  5.1 14.2 %all-to-all-start = ((bf16[16,64,128]{2,1,0:T(8,128)(2,1)}), bf16[16,64,128]{2,1,0:T(8,128)(2,1)S(1)}, u32[]{:S(2)}, u32[]{:S(2)}) async-start(bf16[16,64,128]{2,1,0:T(8,128)(2,1)} %bitcast.1), calls=%async_computation | async-start | bytes 524288 | tf_op jit(solution)/shard_map/all_to_all | solution.py:428
  13.7 2.6 %copy-start = (f32[4,2048]{1,0:T(4,128)S(1)}, f32[4,2048]{1,0:T(4,128)}, u32[]{:S(2)}) copy-start(f32[4,2048]{1,0:T(4,128)} %w_ref.5) | copy-start | bytes 98308
  14.1 3.7 %collective-permute-start.2 = (bf16[32,128]{1,0:T(8,128)(2,1)S(1)}, bf16[32,128]{1,0:T(8,128)(2,1)S(1)}, u32[]{:S(2)}, u32[]{:S(2)}) collective-permute-start(bf16[32,128]{1,0:T(8,128)(2,1)S(1)} %get-tuple-element.47), channel_id=1, source_target_pairs={{0,2},{1,3},{2,4},{3,5},{4,6},{5,7},{6,8},{7,9},{8,10},{9,11},{10,... | collective-permute-start | bytes 24584 | tf_op jit(solution)/shard_map/ppermute | solution.py:425
  20.3 16.1 %all-to-all-start.1 = ((bf16[16,2,64,128]{3,2,1,0:T(8,128)(2,1)}), bf16[16,2,64,128]{3,2,1,0:T(8,128)(2,1)S(1)}, u32[]{:S(2)}, u32[]{:S(2)}) async-start(bf16[16,2,64,128]{3,2,1,0:T(8,128)(2,1)} %get-tuple-element.48), calls=%async_computation.1 | async-start | bytes 1048576 | tf_op jit(solution)/shard_map/all_to_all | solution.py:428
  28.9 4.1 %collective-permute-start.3 = (bf16[2,128,1024]{2,1,0:T(8,128)(2,1)S(1)}, bf16[2,128,1024]{2,1,0:T(8,128)(2,1)S(1)}, u32[]{:S(2)}, u32[]{:S(2)}) collective-permute-start(bf16[2,128,1024]{2,1,0:T(8,128)(2,1)S(1)} %get-tuple-element.51), channel_id=1, source_target_pairs={{0,1},{1,0},{2,3},{3,2},{4,5},{5,4},{6,7},{7,6},{8,9},{9,8},{10,11... | collective-permute-start | bytes 1572872 | tf_op jit(solution)/shard_map/ppermute | solution.py:421
  31.5 5.0 %collective-permute-start.4 = (bf16[64,128]{1,0:T(8,128)(2,1)S(1)}, bf16[64,128]{1,0:T(8,128)(2,1)S(1)}, u32[]{:S(2)}, u32[]{:S(2)}) collective-permute-start(bf16[64,128]{1,0:T(8,128)(2,1)S(1)} %get-tuple-element.56), channel_id=1, source_target_pairs={{2,0},{3,1},{4,2},{5,3},{6,4},{7,5},{8,6},{9,7},{10,8},{11,9},{12,... | collective-permute-start | bytes 49160 | tf_op jit(solution)/shard_map/ppermute | solution.py:425
  37.4 15.6 %all-to-all-start.2 = ((bf16[16,96,128]{2,1,0:T(8,128)(2,1)}), bf16[16,96,128]{2,1,0:T(8,128)(2,1)S(1)}, u32[]{:S(2)}, u32[]{:S(2)}) async-start(bf16[16,96,128]{2,1,0:T(8,128)(2,1)} %get-tuple-element.57), calls=%async_computation.2 | async-start | bytes 786432 | tf_op jit(solution)/shard_map/all_to_all | solution.py:428
  49.9 5.7 %collective-permute-start.7 = (bf16[2,128,1024]{2,1,0:T(8,128)(2,1)S(1)}, bf16[2,128,1024]{2,1,0:T(8,128)(2,1)S(1)}, u32[]{:S(2)}, u32[]{:S(2)}) collective-permute-start(bf16[2,128,1024]{2,1,0:T(8,128)(2,1)S(1)} %get-tuple-element.68), channel_id=1, source_target_pairs={{0,1},{1,0},{2,3},{3,2},{4,5},{5,4},{6,7},{7,6},{8,9},{9,8},{10,11... | collective-permute-start | bytes 1572872 | tf_op jit(solution)/shard_map/ppermute | solution.py:421
  53.4 3.3 %collective-permute-start.5 = (bf16[128,1024]{1,0:T(8,128)(2,1)S(1)}, bf16[128,1024]{1,0:T(8,128)(2,1)S(1)}, u32[]{:S(2)}, u32[]{:S(2)}) collective-permute-start(bf16[128,1024]{1,0:T(8,128)(2,1)S(1)} %get-tuple-element.65), channel_id=1, source_target_pairs={{0,1},{1,0},{2,3},{3,2},{4,5},{5,4},{6,7},{7,6},{8,9},{9,8},{10,11... | collective-permute-start | bytes 786440 | tf_op jit(solution)/shard_map/ppermute | solution.py:421
  55.5 1.2 %collective-permute-start.6 = (f32[32,128]{1,0:T(8,128)S(1)}, f32[32,128]{1,0:T(8,128)S(1)}, u32[]{:S(2)}, u32[]{:S(2)}) collective-permute-start(f32[32,128]{1,0:T(8,128)S(1)} %get-tuple-element.66.taps_ref), channel_id=1, source_target_pairs={{0,1},{1,0},{2,3},{3,2},{4,5},{5,4},{6,7},{7,6},{8,9},{9,8},{10,11... | collective-permute-start | bytes 49160 | tf_op jit(solution)/shard_map/ppermute | solution.py:421

commit v7 on v6

--- a/solution.py
+++ b/solution.py
@@ -122,11 +122,22 @@
     copy.wait()
 
 
-def gather_key_kernel(core_ref, own_ref, recv_ref, k_ref, v_ref, tail_ref, edge_ref):
+def tail_kernel(core_ref, own_ref, recv_ref, tail_ref):
+    rows = own_ref.shape[1] - HALO
+    tails = []
+    for i in range(HALF):
+        at = columns(i)
+        own, recv = (ref[1, rows - HALO : rows, at] for ref in (own_ref, recv_ref))
+        tail = jnp.where(core_ref[0] == 1, own, recv)
+        tails.append(tail.astype(F32)[HALO - EDGE :])
+    tail_ref[...] = jnp.concatenate(tails, axis=0).astype(BF16)
+
+
+def gather_key_kernel(core_ref, own_ref, recv_ref, k_ref, v_ref, edge_ref):
     core = core_ref[0]
     gather(core, own_ref, recv_ref, (k_ref, v_ref))
     rows = k_ref.shape[0]
-    tails, edges = [], []
+    edges = []
     first = lax.broadcasted_iota(jnp.int32, (HALO, HALO), 0)
     unseen = first > lax.broadcasted_iota(jnp.int32, (HALO, HALO), 1)
     for i in range(HALF):
@@ -138,8 +149,6 @@
         k = k_ref[:HALO, at]
         score = jnp.where(unseen, dot(k, q, (1, 1)), 0.0).astype(BF16)
         edges += [-dot(score, g, (1, 0))[:EDGE], k.astype(F32)[:EDGE]]
-        tails.append(v_ref[rows - HALO :, at].astype(F32)[HALO - EDGE :])
-    tail_ref[...] = jnp.concatenate(tails, axis=0).astype(BF16)
     edge_ref[...] = jnp.concatenate(edges, axis=0).astype(BF16)
 
 
@@ -217,7 +226,7 @@
     head_ref,
     done_ref,
     *,
-    order,
+    turns,
 ):
     depth = q_ref.shape[1]
     for i in range(HALF):
@@ -230,8 +239,8 @@
             part = state[n * depth : (n + 1) * depth].astype(BF16)
             out_ref[i * (DH // depth) + n, 1] = part
     total = jnp.zeros(q_ref.shape[1:], F32)
-    for n in reversed(order):
-        out_ref[n, 0] = total.astype(BF16)
+    for n, slot in reversed(turns):
+        out_ref[slot, 0] = total.astype(BF16)
         total = total + q_ref[n].astype(F32)
     done_ref[...] = jnp.zeros(done_ref.shape, F32)
 
@@ -253,34 +262,26 @@
     out_ref,
     done_ref,
     taps_ref,
-    hold_ref,
-    weights_ref,
-    sems,
     *,
     scale,
     places,
-):
-    depth, size = chip_ref.shape[2], hold_ref.shape[1]
+    ways,
+):
+    depth = chip_ref.shape[2]
+    size = out_ref.shape[1] - CW * HALF
     total = jnp.zeros((depth, DH), F32)
     for n, slot in places:
-        hold_ref[slot, :depth] = total.astype(BF16)
+        out_ref[slot, :depth] = total.astype(BF16)
         if depth < size:
-            hold_ref[slot, depth:] = jnp.zeros((size - depth, DH), BF16)
+            out_ref[slot, depth:size] = jnp.zeros((size - depth, DH), BF16)
         total = total + chip_ref[n, 1].astype(F32)
-    states = pltpu.make_async_copy(hold_ref, out_ref.at[:, pl.ds(0, size)], sems.at[0])
-    states.start()
-    for i in range(HALF):
-        suffix = head_state(lambda n: chip_ref[n, 0], i, depth).astype(F32)
+    for i in range(HALF):
+        suffix = head_state(lambda n: chip_ref[ways[n], 0], i, depth).astype(F32)
         add_taps(taps_ref, i, suffix, [wide_ref[i, j].astype(F32) for j in range(CW)])
     weights = (scale * (near_ref[...] + taps_ref[...])).astype(BF16)
-    for n in range(weights_ref.shape[0]):
-        weights_ref[n] = weights
-    place = out_ref.at[:, pl.ds(size, CW * HALF)]
-    weights = pltpu.make_async_copy(weights_ref, place, sems.at[1])
-    weights.start()
+    for n in range(out_ref.shape[0]):
+        out_ref[n, size:] = weights
     done_ref[...] = jnp.zeros(done_ref.shape, F32)
-    states.wait()
-    weights.wait()
 
 
 def query_side_kernel(
@@ -305,6 +306,7 @@
     fetch_sems,
     *,
     scale,
+    ways,
 ):
     core = core_ref[0]
     rows = k_ref.shape[0]
@@ -320,7 +322,7 @@
         fetch.wait()
     for i in range(HALF):
         at = columns(i)
-        suffix = head_state(lambda n: chip_ref[n, 0], i, depth)
+        suffix = head_state(lambda n: chip_ref[ways[n], 0], i, depth)
         c = jnp.concatenate([head_ref[:, at], hold_ref[0, HALO:, at]], axis=0)
         g, k = g_ref[:, at], k_ref[:, at]
         attn = jnp.where(seen.T, dot(g, c, (1, 1)), 0.0)
@@ -373,28 +375,29 @@
     taps_ref[...] = total
 
 
-def join_kernel(core_ref, recv_ref, _, __, gk_ref, gv_ref, sems):
-    put(recv_ref, 1 - core_ref[0], (gk_ref, gv_ref), sems)
+def join_kernel(core_ref, recv_ref, own_ref, _, __, gk_ref, gv_ref, gq_ref, sems, sem):
+    core = core_ref[0]
+    copy = pltpu.make_async_copy(own_ref, gq_ref.at[:, half_of(core, WIDE)], sem)
+    copy.start()
+    put(recv_ref, 1 - core, (gk_ref, gv_ref), sems)
+    copy.wait()
 
 
 def finish_kernel(
-    core_ref, own_ref, recv_ref, taps_ref, far_ref, gq_ref, gw_ref, hold_ref, sems
-):
-    core = core_ref[0]
-    copies = [
-        pltpu.make_async_copy(ref, gq_ref.at[:, half_of(side, WIDE)], sems.at[n])
-        for n, (side, ref) in enumerate(((1 - core, recv_ref), (core, own_ref)))
-    ]
-    for copy in copies:
-        copy.start()
+    core_ref, recv_ref, taps_ref, far_ref, _, gq_ref, gw_ref, hold_ref, sems
+):
+    core = core_ref[0]
+    place = gq_ref.at[:, half_of(1 - core, WIDE)]
+    copies = [pltpu.make_async_copy(recv_ref, place, sems.at[0])]
+    copies[0].start()
     for side, ref in ((core, taps_ref), (1 - core, far_ref)):
         for i in range(HALF):
             at = pl.ds(pl.multiple_of(side * WIDE + i * DH, DH), DH)
             for j in range(CW):
                 row = j * HALF + i
                 hold_ref[j : j + 1, at] = ref[row : row + 1, :]
-    copies.append(pltpu.make_async_copy(hold_ref, gw_ref, sems.at[2]))
-    copies[-1].start()
+    copies.append(pltpu.make_async_copy(hold_ref, gw_ref, sems.at[1]))
+    copies[1].start()
     for copy in copies:
         copy.wait()
 
@@ -408,14 +411,18 @@
     scale = (DH * rows * count) ** (-0.5)
     core = lax.rem(lax.axis_index("col"), 2).astype(jnp.int32).reshape(1)
     half = line // 2
-    along = [z for n in range(half) for z in (half + n, n)]
-    listed = [r * line + z for r in reversed(range(lines)) for z in along]
-    groups = [[2 * p + c for p in listed] for c in range(2)]
-    order = tuple(listed.index(p) for p in range(chips))
-    final = listed
-    final_groups = [[2 * p + c for p in final] for c in range(2)]
-    places = tuple((order[p], final.index(p)) for p in range(chips))
-    slots = tuple(final.index(p) for p in listed)
+    split = [*reversed(range(half)), *range(half, line)]
+    mixed = [z for n in range(half) for z in (half + n, n)]
+    lists = [
+        [r * line + z for r in reversed(range(lines)) for z in along]
+        for along in (split, mixed, mixed)
+    ]
+    groups = [[[2 * p + c for p in each] for c in range(2)] for each in lists]
+    spots = [[each.index(p) for p in range(chips)] for each in lists]
+    turns = tuple(zip(spots[0], spots[1]))
+    places = tuple(zip(spots[1], spots[2]))
+    ways = tuple(spots[1][p] for p in lists[0])
+    slots = tuple(spots[2][p] for p in lists[1])
 
     def swap(value):
         return lax.ppermute(value, AXES, [(d, d ^ 1) for d in range(count)])
@@ -465,7 +472,7 @@
         core,
         [q_keep, q_recv],
     )
-    q_turned = turn(q_sent.reshape(chips, depth, DH), groups)
+    q_turned = turn(q_sent.reshape(chips, depth, DH), groups[0])
     qg_own, qg_send = call(
         split_kernel,
         (pair, pair),
@@ -475,9 +482,10 @@
         [ANY, ANY, VMEM],
     )
     qg_recv = swap(qg_send)
-    k, v, tail, edge = call(
+    tail = call(tail_kernel, shape((EDGE * HALF, DH)), core, [kv_own, kv_recv])
+    k, v, edge = call(
         gather_key_kernel,
-        (block, block, shape((EDGE * HALF, DH)), shape((2 * EDGE * HALF, DH))),
+        (block, block, shape((2 * EDGE * HALF, DH))),
         core,
         [kv_own, kv_recv],
     )
@@ -497,12 +505,12 @@
         [k, v, conv_weight],
     )
     both, c_head, turned = call(
-        functools.partial(turn_kernel, order=order),
+        functools.partial(turn_kernel, turns=turns),
         (shape((chips, 2, depth, DH)), edges, flag),
         core,
         [q_turned, k_state, k, v, halo, conv_weight],
     )
-    both = turn(both, groups)
+    both = turn(both, groups[1])
     gc, taps, wide = call(
         score_kernel,
         (far_block, shape((CW * HALF, DH), F32), shape((HALF, CW, DH, DH))),
@@ -511,22 +519,16 @@
     )
     edge = shifted(edge, -2)
     last, tapped = call(
-        functools.partial(tap_kernel, scale=scale, places=places),
-        (pltpu.HBM((chips, padded + CW * HALF, DH), BF16), flag),
+        functools.partial(tap_kernel, scale=scale, places=places, ways=ways),
+        (shape((chips, padded + CW * HALF, DH)), flag),
         core,
         [both, wide, taps, edge],
-        [
-            pltpu.VMEM((CW * HALF, DH), F32),
-            pltpu.VMEM((chips, padded, DH), BF16),
-            pltpu.VMEM((chips, CW * HALF, DH), BF16),
-            dma((2,)),
-        ],
-        made=(ANY, VMEM),
-    )
-    last = turn(last, final_groups)
+        [pltpu.VMEM((CW * HALF, DH), F32)],
+    )
+    last = turn(last, groups[2])
     full = shape((rows, width))
     grad_keys, grad_values, kv_give, gq = call(
-        functools.partial(query_side_kernel, scale=scale),
+        functools.partial(query_side_kernel, scale=scale, ways=ways),
         (full, full, pair, block),
         core,
         [both, k, g, c_head, edge, conv_weight, tapped, *map(in_hbm, (c, gc, q_far))],
@@ -544,23 +546,25 @@
     )
     q_got = swap(q_give)
     far = swap(taps)
-    grad_keys, grad_values = call(
+    grad_keys, grad_values, grad_queries = call(
         join_kernel,
-        (full, full),
-        core,
-        [kv_got, grad_keys, grad_values],
-        [dma((2,))],
-        [VMEM, ANY, ANY],
-        (ANY, ANY),
-        {2: 0, 3: 1},
+        (full, full, full),
+        core,
+        [kv_got, q_grad, grad_keys, grad_values],
+        [dma((2,)), dma(())],
+        [VMEM, VMEM, ANY, ANY],
+        (ANY, ANY, ANY),
+        {3: 0, 4: 1},
     )
     grad_queries, grad_weight = call(
         finish_kernel,
         (full, shape((CW, width), F32)),
         core,
-        [q_grad, q_got, taps, far],
-        [pltpu.VMEM((CW, width), F32), dma((3,))],
-        made=(ANY, ANY),
+        [q_got, taps, far, grad_queries],
+        [pltpu.VMEM((CW, width), F32), dma((2,))],
+        [VMEM, VMEM, VMEM, ANY],
+        (ANY, ANY),
+        {4: 0},
     )
     return grad_queries, grad_keys, grad_values, grad_weight
 

time: 58.4 us -> 57.4 us (0.983)
  starting transfers between devices: 35.6 us -> 33.9 us
    all_to_all x3, starting transfers between devices: 23.6 us -> 21.9 us  [turn(): lax.all_to_all(value, AXES, 0, 0, axis_index_groups=groups, tiled=True)]
    all_to_all x3, waiting for transfers between devices: 1.4 us -> 2.04 us  [turn(): lax.all_to_all(value, AXES, 0, 0, axis_index_groups=groups, tiled=True)]
    pallas_call x14 -> x15, Pallas kernels: 19.1 us -> 19.2 us  [call(): pl.pallas_call(kernel, out_shape=outs, in_specs=[SMEM] + (given or [VMEM]...]
  transfers between devices with their start and end apart: 11 -> 11, of which waited for: 4 -> 4; matrix products, arithmetic and copies ran while one was open for 0% -> 0% of each run, Pallas kernels for 25% -> 26%
where the time goes in v7:
time: 57.4 us; the launch traced here: 56.5 us
  starting transfers between devices  33.9 us (59%)
  Pallas kernels  19.2 us (33%)
  waiting for transfers between devices  2.62 us (5%)
  between operations  0.75 us (1%)
    all_to_all x3, starting transfers between devices, turn(): lax.all_to_all(value, AXES, 0, 0, axis_index_groups=groups, tiled=True)  21.9 us
    pallas_call x15, Pallas kernels, call(): pl.pallas_call(kernel, out_shape=outs, in_specs=[SMEM] + (given or [VMEM]...  19.2 us
    ppermute x6, starting transfers between devices, swap(): return lax.ppermute(value, AXES, [(d, d ^ 1) for d in range(count)])  8.58 us
    ppermute x2, starting transfers between devices, shifted(): return lax.ppermute(value, AXES, pairs)  3.47 us
    all_to_all x3, waiting for transfers between devices, turn(): lax.all_to_all(value, AXES, 0, 0, axis_index_groups=groups, tiled=True)  2.04 us
  transfers between devices with their start and end apart: 11, of which 4 were waited for; matrix products, arithmetic and copies ran while one was open for 0% of the time, Pallas kernels for 26%

profile of v7, /device:TPU:1, one launch (start us, length us, event | category | flops | bytes accessed | tf_op | source)
XLA Modules:
  0.0 56.5 jit_solution(7695253569689189978)
XLA Ops:
  0.6 1.7 %shard_map.84 = (bf16[8,128,128]{2,1,0:T(8,128)(2,1)S(1)}, bf16[8,128,128]{2,1,0:T(8,128)(2,1)S(1)}) custom-call(s32[1]{0:T(128)} %bitcast.core_ref, bf16[128,2048]{1,0:T(8,128)(2,1)} %a_ref.1, bf16[128,2048]{1,0:T(8,128)(2,1)} %b_ref.1), custom_call_target="tpu_custom_call" | custom-call | tf_op jit(solution)/shard_map/pallas_call | solution.py:40
  2.3 0.1 collective-permute-start
  2.5 1.3 %shard_map.86 = (bf16[2,144,1024]{2,1,0:T(8,128)(2,1)S(1)}, bf16[2,144,1024]{2,1,0:T(8,128)(2,1)S(1)}) custom-call(s32[1]{0:T(128)} %bitcast.core_ref, bf16[128,2048]{1,0:T(8,128)(2,1)} %k_ref.1, bf16[128,2048]{1,0:T(8,128)(2,1)} %v_ref.1, bf16[128,2048]{1,0:T(8,128)(2,1)} %a_ref.1, bf16[128,2048]{1,0:T(8,128)(2,1)} %b_ref.1, ...), custom_call_target="tpu_custom_call" | custom-call | tf_op jit(solution)/shard_map/pallas_call | solution.py:40
  3.8 0.5 collective-permute-start.1
  4.3 0.0 collective-permute-done.recv_ref
  4.3 0.8 %shard_map.85 = (bf16[8,128,128]{2,1,0:T(8,128)(2,1)}, f32[8,128]{1,0:T(8,128)S(1)}) custom-call(s32[1]{0:T(128)} %bitcast.core_ref, bf16[8,128,128]{2,1,0:T(8,128)(2,1)S(1)} %get-tuple-element.39.keep_ref.after_ref, bf16[8,128,128]{2,1,0:T(8,128)(2,1)S(1)} %collective-permute-done.recv_ref), custom_call_target="tpu_custom_call" | custom-call | tf_op jit(solution)/shard_map/pallas_call | solution.py:40
  5.1 7.8 %all-to-all-start = ((bf16[16,64,128]{2,1,0:T(8,128)(2,1)}), bf16[16,64,128]{2,1,0:T(8,128)(2,1)S(1)}, u32[]{:S(2)}, u32[]{:S(2)}) async-start(bf16[16,64,128]{2,1,0:T(8,128)(2,1)} %bitcast.1), calls=%async_computation | async-start | bytes 524288 | tf_op jit(solution)/shard_map/all_to_all | solution.py:435
  12.9 0.0 copy-start
  12.9 2.2 %collective-permute-start.2 = (bf16[32,128]{1,0:T(8,128)(2,1)S(1)}, bf16[32,128]{1,0:T(8,128)(2,1)S(1)}, u32[]{:S(2)}, u32[]{:S(2)}) collective-permute-start(bf16[32,128]{1,0:T(8,128)(2,1)S(1)} %shard_map.89), channel_id=1, source_target_pairs={{0,2},{1,3},{2,4},{3,5},{4,6},{5,7},{6,8},{7,9},{8,10},{9,11},{10,... | collective-permute-start | bytes 24584 | tf_op jit(solution)/shard_map/ppermute | solution.py:432
  15.1 0.5 shard_map.87
  15.6 0.0 copy-done
  15.6 1.5 %shard_map.88 = (bf16[256,1024]{1,0:T(8,128)(2,1)}, f32[8,128,128]{2,1,0:T(8,128)S(1)}) custom-call(s32[1]{0:T(128)} %bitcast.core_ref, bf16[256,1024]{1,0:T(8,128)(2,1)S(1)} %get-tuple-element.44.k_ref, bf16[256,1024]{1,0:T(8,128)(2,1)S(1)} %get-tuple-element.45.v_ref, f32[4,2048]{1,0:T(4,128)S(1)} %copy-done), custom_call_target="tpu_custom_call" | custom-call | tf_op jit(solution)/shard_map/pallas_call | solution.py:40
  17.0 2.0 %all-to-all-done.q_ref = bf16[16,64,128]{2,1,0:T(8,128)(2,1)S(1)} async-done(((bf16[16,64,128]{2,1,0:T(8,128)(2,1)}), bf16[16,64,128]{2,1,0:T(8,128)(2,1)S(1)}, u32[]{:S(2)}, u32[]{:S(2)}) %all-to-all-start) | async-done | bytes 262176 | tf_op jit(solution)/shard_map/all_to_all | solution.py:435
  19.1 1.1 %shard_map.90 = (bf16[16,2,64,128]{3,2,1,0:T(8,128)(2,1)}, bf16[16,1024]{1,0:T(8,128)(2,1)S(1)}, f32[8,128]{1,0:T(8,128)}) custom-call(s32[1]{0:T(128)} %bitcast.core_ref, bf16[16,64,128]{2,1,0:T(8,128)(2,1)S(1)} %all-to-all-done.q_ref, f32[8,128,128]{2,1,0:T(8,128)S(1)} %get-tuple-element.46.state_ref, bf16[256,1024]{1,0:T(8,128)(2,1)S(1)} %get-tuple-element.44.k_ref, ...), custom_call_target="tpu_custom_call" | custom-call | tf_op jit(solution)/shard_map/pallas_call | solution.py:40
  20.1 6.6 %all-to-all-start.1 = ((bf16[16,2,64,128]{3,2,1,0:T(8,128)(2,1)}), bf16[16,2,64,128]{3,2,1,0:T(8,128)(2,1)S(1)}, u32[]{:S(2)}, u32[]{:S(2)}) async-start(bf16[16,2,64,128]{3,2,1,0:T(8,128)(2,1)} %get-tuple-element.47), calls=%async_computation.1 | async-start | bytes 1048576 | tf_op jit(solution)/shard_map/all_to_all | solution.py:435
  26.7 1.2 %shard_map.91 = (bf16[2,128,1024]{2,1,0:T(8,128)(2,1)S(1)}, bf16[2,128,1024]{2,1,0:T(8,128)(2,1)S(1)}) custom-call(s32[1]{0:T(128)} %bitcast.core_ref, bf16[128,2048]{1,0:T(8,128)(2,1)} %a_ref.1, bf16[128,2048]{1,0:T(8,128)(2,1)} %b_ref.1, f32[8,128]{1,0:T(8,128)S(1)} %get-tuple-element.48.after_ref), custom_call_target="tpu_custom_call" | custom-call | tf_op jit(solution)/shard_map/pallas_call | solution.py:40
  27.9 2.6 %collective-permute-start.3 = (bf16[2,128,1024]{2,1,0:T(8,128)(2,1)S(1)}, bf16[2,128,1024]{2,1,0:T(8,128)(2,1)S(1)}, u32[]{:S(2)}, u32[]{:S(2)}) collective-permute-start(bf16[2,128,1024]{2,1,0:T(8,128)(2,1)S(1)} %get-tuple-element.50), channel_id=1, source_target_pairs={{0,1},{1,0},{2,3},{3,2},{4,5},{5,4},{6,7},{7,6},{8,9},{9,8},{10,11... | collective-permute-start | bytes 1572872 | tf_op jit(solution)/shard_map/ppermute | solution.py:428
  30.6 1.3 %collective-permute-start.4 = (bf16[64,128]{1,0:T(8,128)(2,1)S(1)}, bf16[64,128]{1,0:T(8,128)(2,1)S(1)}, u32[]{:S(2)}, u32[]{:S(2)}) collective-permute-start(bf16[64,128]{1,0:T(8,128)(2,1)S(1)} %get-tuple-element.55), channel_id=1, source_target_pairs={{2,0},{3,1},{4,2},{5,3},{6,4},{7,5},{8,6},{9,7},{10,8},{11,9},{12,... | collective-permute-start | bytes 49160 | tf_op jit(solution)/shard_map/ppermute | solution.py:432
  31.9 0.2 collective-permute-done.3.recv_ref
  32.1 0.9 %shard_map.92 = (bf16[256,1024]{1,0:T(8,128)(2,1)S(1)}, bf16[256,1024]{1,0:T(8,128)(2,1)S(1)}, bf16[256,1024]{1,0:T(8,128)(2,1)}) custom-call(s32[1]{0:T(128)} %bitcast.core_ref, bf16[2,128,1024]{2,1,0:T(8,128)(2,1)S(1)} %get-tuple-element.49.own_ref, bf16[2,128,1024]{2,1,0:T(8,128)(2,1)S(1)} %collective-permute-done.3.recv_ref), custom_call_target="tpu_custom_call" | custom-call | tf_op jit(solution)/shard_map/pallas_call | solution.py:40
  33.0 2.5 %shard_map.93 = (bf16[256,1024]{1,0:T(8,128)(2,1)}, f32[32,128]{1,0:T(8,128)S(1)}, bf16[8,4,128,128]{3,2,1,0:T(8,128)(2,1)S(1)}) custom-call(s32[1]{0:T(128)} %bitcast.core_ref, bf16[256,1024]{1,0:T(8,128)(2,1)S(1)} %get-tuple-element.51.q_ref, bf16[256,1024]{1,0:T(8,128)(2,1)S(1)} %get-tuple-element.52.g_ref, ...), custom_call_target="tpu_custom_call" | custom-call | tf_op jit(solution)/shard_map/pallas_call | solution.py:40
  35.4 0.1 collective-permute-done.4.edge_ref
  35.6 1.0 %shard_map.94 = (bf16[16,96,128]{2,1,0:T(8,128)(2,1)}, f32[8,128]{1,0:T(8,128)S(1)}) custom-call(s32[1]{0:T(128)} %bitcast.core_ref, bf16[16,2,64,128]{3,2,1,0:T(8,128)(2,1)S(1)} %all-to-all-done.1.chip_ref, bf16[8,4,128,128]{3,2,1,0:T(8,128)(2,1)S(1)} %get-tuple-element.53.wide_ref, f32[32,128]{1,0:T(8,128)S(1)} %get-tuple-element.54.near_ref, ...), custom_call_target="tpu_custom_call" | custom-call | tf_op jit(solution)/shard_map/pallas_call | solution.py:40
  36.6 7.5 %all-to-all-start.2 = ((bf16[16,96,128]{2,1,0:T(8,128)(2,1)}), bf16[16,96,128]{2,1,0:T(8,128)(2,1)S(1)}, u32[]{:S(2)}, u32[]{:S(2)}) async-start(bf16[16,96,128]{2,1,0:T(8,128)(2,1)} %get-tuple-element.56), calls=%async_computation.2 | async-start | bytes 786432 | tf_op jit(solution)/shard_map/all_to_all | solution.py:435
  44.1 4.9 %shard_map.95 = (bf16[128,2048]{1,0:T(8,128)(2,1)}, bf16[128,2048]{1,0:T(8,128)(2,1)}, bf16[2,128,1024]{2,1,0:T(8,128)(2,1)S(1)}, bf16[256,1024]{1,0:T(8,128)(2,1)S(1)}) custom-call(s32[1]{0:T(128)} %bitcast.core_ref, bf16[16,2,64,128]{3,2,1,0:T(8,128)(2,1)S(1)} %all-to-all-done.1.chip_ref, bf16[256,1024]{1,0:T(8,128)(2,1)S(1)} %get-tuple-element.44.k_ref, ...), custom_call_target="tpu_custom_call" | custom-call | tf_op jit(solution)/shard_map/pallas_call | solution.py:40
  48.9 3.1 %collective-permute-start.7 = (bf16[2,128,1024]{2,1,0:T(8,128)(2,1)S(1)}, bf16[2,128,1024]{2,1,0:T(8,128)(2,1)S(1)}, u32[]{:S(2)}, u32[]{:S(2)}) collective-permute-start(bf16[2,128,1024]{2,1,0:T(8,128)(2,1)S(1)} %get-tuple-element.65), channel_id=1, source_target_pairs={{0,1},{1,0},{2,3},{3,2},{4,5},{5,4},{6,7},{7,6},{8,9},{9,8},{10,11... | collective-permute-start | bytes 1572872 | tf_op jit(solution)/shard_map/ppermute | solution.py:428
  52.1 0.4 shard_map.96
  52.4 2.1 %collective-permute-start.5 = (bf16[128,1024]{1,0:T(8,128)(2,1)S(1)}, bf16[128,1024]{1,0:T(8,128)(2,1)S(1)}, u32[]{:S(2)}, u32[]{:S(2)}) collective-permute-start(bf16[128,1024]{1,0:T(8,128)(2,1)S(1)} %get-tuple-element.63), channel_id=1, source_target_pairs={{0,1},{1,0},{2,3},{3,2},{4,5},{5,4},{6,7},{7,6},{8,9},{9,8},{10,11... | collective-permute-start | bytes 786440 | tf_op jit(solution)/shard_map/ppermute | solution.py:428
  54.5 0.1 collective-permute-start.6
  54.6 0.9 %shard_map.97 = (bf16[128,2048]{1,0:T(8,128)(2,1)}, bf16[128,2048]{1,0:T(8,128)(2,1)}, bf16[128,2048]{1,0:T(8,128)(2,1)}) custom-call(s32[1]{0:T(128)} %bitcast.core_ref, bf16[2,128,1024]{2,1,0:T(8,128)(2,1)S(1)} %collective-permute-done.7.recv_ref, bf16[128,1024]{1,0:T(8,128)(2,1)S(1)} %get-tuple-element.66.own_ref, ...), custom_call_target="tpu_custom_call", output_to_operand_aliasing={{0}: (3, {}), {1}: (4, {})} | custom-call | tf_op jit(solution)/shard_map/pallas_call | solution.py:40
  55.5 0.2 collective-permute-done.6.far_ref
  55.7 0.7 %shard_map.98 = (bf16[128,2048]{1,0:T(8,128)(2,1)}, f32[4,2048]{1,0:T(4,128)}) custom-call(s32[1]{0:T(128)} %bitcast.core_ref, bf16[128,1024]{1,0:T(8,128)(2,1)S(1)} %collective-permute-done.5.recv_ref, f32[32,128]{1,0:T(8,128)S(1)} %get-tuple-element.64.taps_ref, f32[32,128]{1,0:T(8,128)S(1)} %collective-permute-done.6.far_ref, ...), custom_call_target="tpu_custom_call", output_to_operand_aliasing={{0}: (4, {})} | custom-call | tf_op jit(solution)/shard_map/pallas_call | solution.py:40
  (7 shorter events, 0.0 us)
Async XLA Ops:
  2.3 2.0 %collective-permute-start = (bf16[8,128,128]{2,1,0:T(8,128)(2,1)S(1)}, bf16[8,128,128]{2,1,0:T(8,128)(2,1)S(1)}, u32[]{:S(2)}, u32[]{:S(2)}) collective-permute-start(bf16[8,128,128]{2,1,0:T(8,128)(2,1)S(1)} %get-tuple-element.40), channel_id=1, source_target_pairs={{0,1},{1,0},{2,3},{3,2},{4,5},{5,4},{6,7},{7,6},{8,9},{9,8},{10,11... | collective-permute-start | bytes 786440 | tf_op jit(solution)/shard_map/ppermute | solution.py:428
  3.8 9.1 %collective-permute-start.1 = (bf16[2,144,1024]{2,1,0:T(8,128)(2,1)S(1)}, bf16[2,144,1024]{2,1,0:T(8,128)(2,1)S(1)}, u32[]{:S(2)}, u32[]{:S(2)}) collective-permute-start(bf16[2,144,1024]{2,1,0:T(8,128)(2,1)S(1)} %get-tuple-element.43), channel_id=1, source_target_pairs={{0,1},{1,0},{2,3},{3,2},{4,5},{5,4},{6,7},{7,6},{8,9},{9,8},{10,11... | collective-permute-start | bytes 1769480 | tf_op jit(solution)/shard_map/ppermute | solution.py:428
  5.1 14.0 %all-to-all-start = ((bf16[16,64,128]{2,1,0:T(8,128)(2,1)}), bf16[16,64,128]{2,1,0:T(8,128)(2,1)S(1)}, u32[]{:S(2)}, u32[]{:S(2)}) async-start(bf16[16,64,128]{2,1,0:T(8,128)(2,1)} %bitcast.1), calls=%async_computation | async-start | bytes 524288 | tf_op jit(solution)/shard_map/all_to_all | solution.py:435
  12.9 2.7 %copy-start = (f32[4,2048]{1,0:T(4,128)S(1)}, f32[4,2048]{1,0:T(4,128)}, u32[]{:S(2)}) copy-start(f32[4,2048]{1,0:T(4,128)} %w_ref.5) | copy-start | bytes 98308
  12.9 4.1 %collective-permute-start.2 = (bf16[32,128]{1,0:T(8,128)(2,1)S(1)}, bf16[32,128]{1,0:T(8,128)(2,1)S(1)}, u32[]{:S(2)}, u32[]{:S(2)}) collective-permute-start(bf16[32,128]{1,0:T(8,128)(2,1)S(1)} %shard_map.89), channel_id=1, source_target_pairs={{0,2},{1,3},{2,4},{3,5},{4,6},{5,7},{6,8},{7,9},{8,10},{9,11},{10,... | collective-permute-start | bytes 24584 | tf_op jit(solution)/shard_map/ppermute | solution.py:432
  20.1 15.4 %all-to-all-start.1 = ((bf16[16,2,64,128]{3,2,1,0:T(8,128)(2,1)}), bf16[16,2,64,128]{3,2,1,0:T(8,128)(2,1)S(1)}, u32[]{:S(2)}, u32[]{:S(2)}) async-start(bf16[16,2,64,128]{3,2,1,0:T(8,128)(2,1)} %get-tuple-element.47), calls=%async_computation.1 | async-start | bytes 1048576 | tf_op jit(solution)/shard_map/all_to_all | solution.py:435
  27.9 4.2 %collective-permute-start.3 = (bf16[2,128,1024]{2,1,0:T(8,128)(2,1)S(1)}, bf16[2,128,1024]{2,1,0:T(8,128)(2,1)S(1)}, u32[]{:S(2)}, u32[]{:S(2)}) collective-permute-start(bf16[2,128,1024]{2,1,0:T(8,128)(2,1)S(1)} %get-tuple-element.50), channel_id=1, source_target_pairs={{0,1},{1,0},{2,3},{3,2},{4,5},{5,4},{6,7},{7,6},{8,9},{9,8},{10,11... | collective-permute-start | bytes 1572872 | tf_op jit(solution)/shard_map/ppermute | solution.py:428
  30.6 5.0 %collective-permute-start.4 = (bf16[64,128]{1,0:T(8,128)(2,1)S(1)}, bf16[64,128]{1,0:T(8,128)(2,1)S(1)}, u32[]{:S(2)}, u32[]{:S(2)}) collective-permute-start(bf16[64,128]{1,0:T(8,128)(2,1)S(1)} %get-tuple-element.55), channel_id=1, source_target_pairs={{2,0},{3,1},{4,2},{5,3},{6,4},{7,5},{8,6},{9,7},{10,8},{11,9},{12,... | collective-permute-start | bytes 49160 | tf_op jit(solution)/shard_map/ppermute | solution.py:432
  36.6 15.5 %all-to-all-start.2 = ((bf16[16,96,128]{2,1,0:T(8,128)(2,1)}), bf16[16,96,128]{2,1,0:T(8,128)(2,1)S(1)}, u32[]{:S(2)}, u32[]{:S(2)}) async-start(bf16[16,96,128]{2,1,0:T(8,128)(2,1)} %get-tuple-element.56), calls=%async_computation.2 | async-start | bytes 786432 | tf_op jit(solution)/shard_map/all_to_all | solution.py:435
  48.9 5.7 %collective-permute-start.7 = (bf16[2,128,1024]{2,1,0:T(8,128)(2,1)S(1)}, bf16[2,128,1024]{2,1,0:T(8,128)(2,1)S(1)}, u32[]{:S(2)}, u32[]{:S(2)}) collective-permute-start(bf16[2,128,1024]{2,1,0:T(8,128)(2,1)S(1)} %get-tuple-element.65), channel_id=1, source_target_pairs={{0,1},{1,0},{2,3},{3,2},{4,5},{5,4},{6,7},{7,6},{8,9},{9,8},{10,11... | collective-permute-start | bytes 1572872 | tf_op jit(solution)/shard_map/ppermute | solution.py:428
  52.4 3.3 %collective-permute-start.5 = (bf16[128,1024]{1,0:T(8,128)(2,1)S(1)}, bf16[128,1024]{1,0:T(8,128)(2,1)S(1)}, u32[]{:S(2)}, u32[]{:S(2)}) collective-permute-start(bf16[128,1024]{1,0:T(8,128)(2,1)S(1)} %get-tuple-element.63), channel_id=1, source_target_pairs={{0,1},{1,0},{2,3},{3,2},{4,5},{5,4},{6,7},{7,6},{8,9},{9,8},{10,11... | collective-permute-start | bytes 786440 | tf_op jit(solution)/shard_map/ppermute | solution.py:428
  54.5 1.2 %collective-permute-start.6 = (f32[32,128]{1,0:T(8,128)S(1)}, f32[32,128]{1,0:T(8,128)S(1)}, u32[]{:S(2)}, u32[]{:S(2)}) collective-permute-start(f32[32,128]{1,0:T(8,128)S(1)} %get-tuple-element.64.taps_ref), channel_id=1, source_target_pairs={{0,1},{1,0},{2,3},{3,2},{4,5},{5,4},{6,7},{7,6},{8,9},{9,8},{10,11... | collective-permute-start | bytes 49160 | tf_op jit(solution)/shard_map/ppermute | solution.py:428

commit v8 on v7

--- a/solution.py
+++ b/solution.py
@@ -412,10 +412,11 @@
     core = lax.rem(lax.axis_index("col"), 2).astype(jnp.int32).reshape(1)
     half = line // 2
     split = [*reversed(range(half)), *range(half, line)]
+    spread = sorted(range(line), key=lambda z: (abs(2 * z + 1 - line), -z))
     mixed = [z for n in range(half) for z in (half + n, n)]
     lists = [
         [r * line + z for r in reversed(range(lines)) for z in along]
-        for along in (split, mixed, mixed)
+        for along in (split, spread, mixed)
     ]
     groups = [[[2 * p + c for p in each] for c in range(2)] for each in lists]
     spots = [[each.index(p) for p in range(chips)] for each in lists]

time: 57.4 us -> 56.9 us (level)
  transfers between devices with their start and end apart: 11 -> 11, of which waited for: 4 -> 3; matrix products, arithmetic and copies ran while one was open for 0% -> 0% of each run, Pallas kernels for 26% -> 26%
where the time goes in v8:
time: 56.9 us; the launch traced here: 56 us
  starting transfers between devices  33.5 us (59%)
  Pallas kernels  19.2 us (34%)
  waiting for transfers between devices  2.5 us (4%)
  between operations  0.75 us (1%)
    all_to_all x3, starting transfers between devices, turn(): lax.all_to_all(value, AXES, 0, 0, axis_index_groups=groups, tiled=True)  21.5 us
    pallas_call x15, Pallas kernels, call(): pl.pallas_call(kernel, out_shape=outs, in_specs=[SMEM] + (given or [VMEM]...  19.2 us
    ppermute x6, starting transfers between devices, swap(): return lax.ppermute(value, AXES, [(d, d ^ 1) for d in range(count)])  8.58 us
    ppermute x2, starting transfers between devices, shifted(): return lax.ppermute(value, AXES, pairs)  3.47 us
    all_to_all x3, waiting for transfers between devices, turn(): lax.all_to_all(value, AXES, 0, 0, axis_index_groups=groups, tiled=True)  2.04 us
  transfers between devices with their start and end apart: 11, of which 3 were waited for; matrix products, arithmetic and copies ran while one was open for 0% of the time, Pallas kernels for 26%

profile of v8, /device:TPU:1, one launch (start us, length us, event | category | flops | bytes accessed | tf_op | source)
XLA Modules:
  0.0 56.0 jit_solution(14460175183494340283)
XLA Ops:
  0.6 1.7 %shard_map.84 = (bf16[8,128,128]{2,1,0:T(8,128)(2,1)S(1)}, bf16[8,128,128]{2,1,0:T(8,128)(2,1)S(1)}) custom-call(s32[1]{0:T(128)} %bitcast.core_ref, bf16[128,2048]{1,0:T(8,128)(2,1)} %a_ref.1, bf16[128,2048]{1,0:T(8,128)(2,1)} %b_ref.1), custom_call_target="tpu_custom_call" | custom-call | tf_op jit(solution)/shard_map/pallas_call | solution.py:40
  2.3 0.1 collective-permute-start
  2.5 1.3 %shard_map.86 = (bf16[2,144,1024]{2,1,0:T(8,128)(2,1)S(1)}, bf16[2,144,1024]{2,1,0:T(8,128)(2,1)S(1)}) custom-call(s32[1]{0:T(128)} %bitcast.core_ref, bf16[128,2048]{1,0:T(8,128)(2,1)} %k_ref.1, bf16[128,2048]{1,0:T(8,128)(2,1)} %v_ref.1, bf16[128,2048]{1,0:T(8,128)(2,1)} %a_ref.1, bf16[128,2048]{1,0:T(8,128)(2,1)} %b_ref.1, ...), custom_call_target="tpu_custom_call" | custom-call | tf_op jit(solution)/shard_map/pallas_call | solution.py:40
  3.8 0.5 collective-permute-start.1
  4.3 0.0 collective-permute-done.recv_ref
  4.3 0.8 %shard_map.85 = (bf16[8,128,128]{2,1,0:T(8,128)(2,1)}, f32[8,128]{1,0:T(8,128)S(1)}) custom-call(s32[1]{0:T(128)} %bitcast.core_ref, bf16[8,128,128]{2,1,0:T(8,128)(2,1)S(1)} %get-tuple-element.39.keep_ref.after_ref, bf16[8,128,128]{2,1,0:T(8,128)(2,1)S(1)} %collective-permute-done.recv_ref), custom_call_target="tpu_custom_call" | custom-call | tf_op jit(solution)/shard_map/pallas_call | solution.py:40
  5.1 7.8 %all-to-all-start = ((bf16[16,64,128]{2,1,0:T(8,128)(2,1)}), bf16[16,64,128]{2,1,0:T(8,128)(2,1)S(1)}, u32[]{:S(2)}, u32[]{:S(2)}) async-start(bf16[16,64,128]{2,1,0:T(8,128)(2,1)} %bitcast.1), calls=%async_computation | async-start | bytes 524288 | tf_op jit(solution)/shard_map/all_to_all | solution.py:436
  12.9 0.0 copy-start
  12.9 2.2 %collective-permute-start.2 = (bf16[32,128]{1,0:T(8,128)(2,1)S(1)}, bf16[32,128]{1,0:T(8,128)(2,1)S(1)}, u32[]{:S(2)}, u32[]{:S(2)}) collective-permute-start(bf16[32,128]{1,0:T(8,128)(2,1)S(1)} %shard_map.89), channel_id=1, source_target_pairs={{0,2},{1,3},{2,4},{3,5},{4,6},{5,7},{6,8},{7,9},{8,10},{9,11},{10,... | collective-permute-start | bytes 24584 | tf_op jit(solution)/shard_map/ppermute | solution.py:433
  15.1 0.5 shard_map.87
  15.6 0.0 copy-done
  15.6 1.5 %shard_map.88 = (bf16[256,1024]{1,0:T(8,128)(2,1)}, f32[8,128,128]{2,1,0:T(8,128)S(1)}) custom-call(s32[1]{0:T(128)} %bitcast.core_ref, bf16[256,1024]{1,0:T(8,128)(2,1)S(1)} %get-tuple-element.44.k_ref, bf16[256,1024]{1,0:T(8,128)(2,1)S(1)} %get-tuple-element.45.v_ref, f32[4,2048]{1,0:T(4,128)S(1)} %copy-done), custom_call_target="tpu_custom_call" | custom-call | tf_op jit(solution)/shard_map/pallas_call | solution.py:40
  17.0 2.0 %all-to-all-done.q_ref = bf16[16,64,128]{2,1,0:T(8,128)(2,1)S(1)} async-done(((bf16[16,64,128]{2,1,0:T(8,128)(2,1)}), bf16[16,64,128]{2,1,0:T(8,128)(2,1)S(1)}, u32[]{:S(2)}, u32[]{:S(2)}) %all-to-all-start) | async-done | bytes 262176 | tf_op jit(solution)/shard_map/all_to_all | solution.py:436
  19.1 1.1 %shard_map.90 = (bf16[16,2,64,128]{3,2,1,0:T(8,128)(2,1)}, bf16[16,1024]{1,0:T(8,128)(2,1)S(1)}, f32[8,128]{1,0:T(8,128)}) custom-call(s32[1]{0:T(128)} %bitcast.core_ref, bf16[16,64,128]{2,1,0:T(8,128)(2,1)S(1)} %all-to-all-done.q_ref, f32[8,128,128]{2,1,0:T(8,128)S(1)} %get-tuple-element.46.state_ref, bf16[256,1024]{1,0:T(8,128)(2,1)S(1)} %get-tuple-element.44.k_ref, ...), custom_call_target="tpu_custom_call" | custom-call | tf_op jit(solution)/shard_map/pallas_call | solution.py:40
  20.1 6.6 %all-to-all-start.1 = ((bf16[16,2,64,128]{3,2,1,0:T(8,128)(2,1)}), bf16[16,2,64,128]{3,2,1,0:T(8,128)(2,1)S(1)}, u32[]{:S(2)}, u32[]{:S(2)}) async-start(bf16[16,2,64,128]{3,2,1,0:T(8,128)(2,1)} %get-tuple-element.47), calls=%async_computation.1 | async-start | bytes 1048576 | tf_op jit(solution)/shard_map/all_to_all | solution.py:436
  26.7 1.2 %shard_map.91 = (bf16[2,128,1024]{2,1,0:T(8,128)(2,1)S(1)}, bf16[2,128,1024]{2,1,0:T(8,128)(2,1)S(1)}) custom-call(s32[1]{0:T(128)} %bitcast.core_ref, bf16[128,2048]{1,0:T(8,128)(2,1)} %a_ref.1, bf16[128,2048]{1,0:T(8,128)(2,1)} %b_ref.1, f32[8,128]{1,0:T(8,128)S(1)} %get-tuple-element.48.after_ref), custom_call_target="tpu_custom_call" | custom-call | tf_op jit(solution)/shard_map/pallas_call | solution.py:40
  27.9 2.6 %collective-permute-start.3 = (bf16[2,128,1024]{2,1,0:T(8,128)(2,1)S(1)}, bf16[2,128,1024]{2,1,0:T(8,128)(2,1)S(1)}, u32[]{:S(2)}, u32[]{:S(2)}) collective-permute-start(bf16[2,128,1024]{2,1,0:T(8,128)(2,1)S(1)} %get-tuple-element.50), channel_id=1, source_target_pairs={{0,1},{1,0},{2,3},{3,2},{4,5},{5,4},{6,7},{7,6},{8,9},{9,8},{10,11... | collective-permute-start | bytes 1572872 | tf_op jit(solution)/shard_map/ppermute | solution.py:429
  30.6 1.3 %collective-permute-start.4 = (bf16[64,128]{1,0:T(8,128)(2,1)S(1)}, bf16[64,128]{1,0:T(8,128)(2,1)S(1)}, u32[]{:S(2)}, u32[]{:S(2)}) collective-permute-start(bf16[64,128]{1,0:T(8,128)(2,1)S(1)} %get-tuple-element.55), channel_id=1, source_target_pairs={{2,0},{3,1},{4,2},{5,3},{6,4},{7,5},{8,6},{9,7},{10,8},{11,9},{12,... | collective-permute-start | bytes 49160 | tf_op jit(solution)/shard_map/ppermute | solution.py:433
  31.9 0.2 collective-permute-done.3.recv_ref
  32.1 0.9 %shard_map.92 = (bf16[256,1024]{1,0:T(8,128)(2,1)S(1)}, bf16[256,1024]{1,0:T(8,128)(2,1)S(1)}, bf16[256,1024]{1,0:T(8,128)(2,1)}) custom-call(s32[1]{0:T(128)} %bitcast.core_ref, bf16[2,128,1024]{2,1,0:T(8,128)(2,1)S(1)} %get-tuple-element.49.own_ref, bf16[2,128,1024]{2,1,0:T(8,128)(2,1)S(1)} %collective-permute-done.3.recv_ref), custom_call_target="tpu_custom_call" | custom-call | tf_op jit(solution)/shard_map/pallas_call | solution.py:40
  33.0 2.5 %shard_map.93 = (bf16[256,1024]{1,0:T(8,128)(2,1)}, f32[32,128]{1,0:T(8,128)S(1)}, bf16[8,4,128,128]{3,2,1,0:T(8,128)(2,1)S(1)}) custom-call(s32[1]{0:T(128)} %bitcast.core_ref, bf16[256,1024]{1,0:T(8,128)(2,1)S(1)} %get-tuple-element.51.q_ref, bf16[256,1024]{1,0:T(8,128)(2,1)S(1)} %get-tuple-element.52.g_ref, ...), custom_call_target="tpu_custom_call" | custom-call | tf_op jit(solution)/shard_map/pallas_call | solution.py:40
  35.4 0.0 collective-permute-done.4.edge_ref
  35.4 1.0 %shard_map.94 = (bf16[16,96,128]{2,1,0:T(8,128)(2,1)}, f32[8,128]{1,0:T(8,128)S(1)}) custom-call(s32[1]{0:T(128)} %bitcast.core_ref, bf16[16,2,64,128]{3,2,1,0:T(8,128)(2,1)S(1)} %all-to-all-done.1.chip_ref, bf16[8,4,128,128]{3,2,1,0:T(8,128)(2,1)S(1)} %get-tuple-element.53.wide_ref, f32[32,128]{1,0:T(8,128)S(1)} %get-tuple-element.54.near_ref, ...), custom_call_target="tpu_custom_call" | custom-call | tf_op jit(solution)/shard_map/pallas_call | solution.py:40
  36.5 7.1 %all-to-all-start.2 = ((bf16[16,96,128]{2,1,0:T(8,128)(2,1)}), bf16[16,96,128]{2,1,0:T(8,128)(2,1)S(1)}, u32[]{:S(2)}, u32[]{:S(2)}) async-start(bf16[16,96,128]{2,1,0:T(8,128)(2,1)} %get-tuple-element.56), calls=%async_computation.2 | async-start | bytes 786432 | tf_op jit(solution)/shard_map/all_to_all | solution.py:436
  43.6 4.9 %shard_map.95 = (bf16[128,2048]{1,0:T(8,128)(2,1)}, bf16[128,2048]{1,0:T(8,128)(2,1)}, bf16[2,128,1024]{2,1,0:T(8,128)(2,1)S(1)}, bf16[256,1024]{1,0:T(8,128)(2,1)S(1)}) custom-call(s32[1]{0:T(128)} %bitcast.core_ref, bf16[16,2,64,128]{3,2,1,0:T(8,128)(2,1)S(1)} %all-to-all-done.1.chip_ref, bf16[256,1024]{1,0:T(8,128)(2,1)S(1)} %get-tuple-element.44.k_ref, ...), custom_call_target="tpu_custom_call" | custom-call | tf_op jit(solution)/shard_map/pallas_call | solution.py:40
  48.5 3.8 %collective-permute-start.7 = (bf16[2,128,1024]{2,1,0:T(8,128)(2,1)S(1)}, bf16[2,128,1024]{2,1,0:T(8,128)(2,1)S(1)}, u32[]{:S(2)}, u32[]{:S(2)}) collective-permute-start(bf16[2,128,1024]{2,1,0:T(8,128)(2,1)S(1)} %get-tuple-element.65), channel_id=1, source_target_pairs={{0,1},{1,0},{2,3},{3,2},{4,5},{5,4},{6,7},{7,6},{8,9},{9,8},{10,11... | collective-permute-start | bytes 1572872 | tf_op jit(solution)/shard_map/ppermute | solution.py:429
  52.3 0.4 shard_map.96
  52.6 1.4 %collective-permute-start.5 = (bf16[128,1024]{1,0:T(8,128)(2,1)S(1)}, bf16[128,1024]{1,0:T(8,128)(2,1)S(1)}, u32[]{:S(2)}, u32[]{:S(2)}) collective-permute-start(bf16[128,1024]{1,0:T(8,128)(2,1)S(1)} %get-tuple-element.63), channel_id=1, source_target_pairs={{0,1},{1,0},{2,3},{3,2},{4,5},{5,4},{6,7},{7,6},{8,9},{9,8},{10,11... | collective-permute-start | bytes 786440 | tf_op jit(solution)/shard_map/ppermute | solution.py:429
  54.1 0.1 collective-permute-start.6
  54.1 0.9 %shard_map.97 = (bf16[128,2048]{1,0:T(8,128)(2,1)}, bf16[128,2048]{1,0:T(8,128)(2,1)}, bf16[128,2048]{1,0:T(8,128)(2,1)}) custom-call(s32[1]{0:T(128)} %bitcast.core_ref, bf16[2,128,1024]{2,1,0:T(8,128)(2,1)S(1)} %collective-permute-done.7.recv_ref, bf16[128,1024]{1,0:T(8,128)(2,1)S(1)} %get-tuple-element.66.own_ref, ...), custom_call_target="tpu_custom_call", output_to_operand_aliasing={{0}: (3, {}), {1}: (4, {})} | custom-call | tf_op jit(solution)/shard_map/pallas_call | solution.py:40
  55.0 0.2 collective-permute-done.6.far_ref
  55.2 0.7 %shard_map.98 = (bf16[128,2048]{1,0:T(8,128)(2,1)}, f32[4,2048]{1,0:T(4,128)}) custom-call(s32[1]{0:T(128)} %bitcast.core_ref, bf16[128,1024]{1,0:T(8,128)(2,1)S(1)} %collective-permute-done.5.recv_ref, f32[32,128]{1,0:T(8,128)S(1)} %get-tuple-element.64.taps_ref, f32[32,128]{1,0:T(8,128)S(1)} %collective-permute-done.6.far_ref, ...), custom_call_target="tpu_custom_call", output_to_operand_aliasing={{0}: (4, {})} | custom-call | tf_op jit(solution)/shard_map/pallas_call | solution.py:40
  (7 shorter events, 0.0 us)
Async XLA Ops:
  2.3 2.0 %collective-permute-start = (bf16[8,128,128]{2,1,0:T(8,128)(2,1)S(1)}, bf16[8,128,128]{2,1,0:T(8,128)(2,1)S(1)}, u32[]{:S(2)}, u32[]{:S(2)}) collective-permute-start(bf16[8,128,128]{2,1,0:T(8,128)(2,1)S(1)} %get-tuple-element.40), channel_id=1, source_target_pairs={{0,1},{1,0},{2,3},{3,2},{4,5},{5,4},{6,7},{7,6},{8,9},{9,8},{10,11... | collective-permute-start | bytes 786440 | tf_op jit(solution)/shard_map/ppermute | solution.py:429
  3.8 9.1 %collective-permute-start.1 = (bf16[2,144,1024]{2,1,0:T(8,128)(2,1)S(1)}, bf16[2,144,1024]{2,1,0:T(8,128)(2,1)S(1)}, u32[]{:S(2)}, u32[]{:S(2)}) collective-permute-start(bf16[2,144,1024]{2,1,0:T(8,128)(2,1)S(1)} %get-tuple-element.43), channel_id=1, source_target_pairs={{0,1},{1,0},{2,3},{3,2},{4,5},{5,4},{6,7},{7,6},{8,9},{9,8},{10,11... | collective-permute-start | bytes 1769480 | tf_op jit(solution)/shard_map/ppermute | solution.py:429
  5.1 14.0 %all-to-all-start = ((bf16[16,64,128]{2,1,0:T(8,128)(2,1)}), bf16[16,64,128]{2,1,0:T(8,128)(2,1)S(1)}, u32[]{:S(2)}, u32[]{:S(2)}) async-start(bf16[16,64,128]{2,1,0:T(8,128)(2,1)} %bitcast.1), calls=%async_computation | async-start | bytes 524288 | tf_op jit(solution)/shard_map/all_to_all | solution.py:436
  12.9 2.7 %copy-start = (f32[4,2048]{1,0:T(4,128)S(1)}, f32[4,2048]{1,0:T(4,128)}, u32[]{:S(2)}) copy-start(f32[4,2048]{1,0:T(4,128)} %w_ref.5) | copy-start | bytes 98308
  12.9 4.1 %collective-permute-start.2 = (bf16[32,128]{1,0:T(8,128)(2,1)S(1)}, bf16[32,128]{1,0:T(8,128)(2,1)S(1)}, u32[]{:S(2)}, u32[]{:S(2)}) collective-permute-start(bf16[32,128]{1,0:T(8,128)(2,1)S(1)} %shard_map.89), channel_id=1, source_target_pairs={{0,2},{1,3},{2,4},{3,5},{4,6},{5,7},{6,8},{7,9},{8,10},{9,11},{10,... | collective-permute-start | bytes 24584 | tf_op jit(solution)/shard_map/ppermute | solution.py:433
  20.1 15.3 %all-to-all-start.1 = ((bf16[16,2,64,128]{3,2,1,0:T(8,128)(2,1)}), bf16[16,2,64,128]{3,2,1,0:T(8,128)(2,1)S(1)}, u32[]{:S(2)}, u32[]{:S(2)}) async-start(bf16[16,2,64,128]{3,2,1,0:T(8,128)(2,1)} %get-tuple-element.47), calls=%async_computation.1 | async-start | bytes 1048576 | tf_op jit(solution)/shard_map/all_to_all | solution.py:436
  27.9 4.2 %collective-permute-start.3 = (bf16[2,128,1024]{2,1,0:T(8,128)(2,1)S(1)}, bf16[2,128,1024]{2,1,0:T(8,128)(2,1)S(1)}, u32[]{:S(2)}, u32[]{:S(2)}) collective-permute-start(bf16[2,128,1024]{2,1,0:T(8,128)(2,1)S(1)} %get-tuple-element.50), channel_id=1, source_target_pairs={{0,1},{1,0},{2,3},{3,2},{4,5},{5,4},{6,7},{7,6},{8,9},{9,8},{10,11... | collective-permute-start | bytes 1572872 | tf_op jit(solution)/shard_map/ppermute | solution.py:429
  30.6 4.9 %collective-permute-start.4 = (bf16[64,128]{1,0:T(8,128)(2,1)S(1)}, bf16[64,128]{1,0:T(8,128)(2,1)S(1)}, u32[]{:S(2)}, u32[]{:S(2)}) collective-permute-start(bf16[64,128]{1,0:T(8,128)(2,1)S(1)} %get-tuple-element.55), channel_id=1, source_target_pairs={{2,0},{3,1},{4,2},{5,3},{6,4},{7,5},{8,6},{9,7},{10,8},{11,9},{12,... | collective-permute-start | bytes 49160 | tf_op jit(solution)/shard_map/ppermute | solution.py:433
  36.5 15.8 %all-to-all-start.2 = ((bf16[16,96,128]{2,1,0:T(8,128)(2,1)}), bf16[16,96,128]{2,1,0:T(8,128)(2,1)S(1)}, u32[]{:S(2)}, u32[]{:S(2)}) async-start(bf16[16,96,128]{2,1,0:T(8,128)(2,1)} %get-tuple-element.56), calls=%async_computation.2 | async-start | bytes 786432 | tf_op jit(solution)/shard_map/all_to_all | solution.py:436
  48.5 5.7 %collective-permute-start.7 = (bf16[2,128,1024]{2,1,0:T(8,128)(2,1)S(1)}, bf16[2,128,1024]{2,1,0:T(8,128)(2,1)S(1)}, u32[]{:S(2)}, u32[]{:S(2)}) collective-permute-start(bf16[2,128,1024]{2,1,0:T(8,128)(2,1)S(1)} %get-tuple-element.65), channel_id=1, source_target_pairs={{0,1},{1,0},{2,3},{3,2},{4,5},{5,4},{6,7},{7,6},{8,9},{9,8},{10,11... | collective-permute-start | bytes 1572872 | tf_op jit(solution)/shard_map/ppermute | solution.py:429
  52.6 2.6 %collective-permute-start.5 = (bf16[128,1024]{1,0:T(8,128)(2,1)S(1)}, bf16[128,1024]{1,0:T(8,128)(2,1)S(1)}, u32[]{:S(2)}, u32[]{:S(2)}) collective-permute-start(bf16[128,1024]{1,0:T(8,128)(2,1)S(1)} %get-tuple-element.63), channel_id=1, source_target_pairs={{0,1},{1,0},{2,3},{3,2},{4,5},{5,4},{6,7},{7,6},{8,9},{9,8},{10,11... | collective-permute-start | bytes 786440 | tf_op jit(solution)/shard_map/ppermute | solution.py:429
  54.1 1.2 %collective-permute-start.6 = (f32[32,128]{1,0:T(8,128)S(1)}, f32[32,128]{1,0:T(8,128)S(1)}, u32[]{:S(2)}, u32[]{:S(2)}) collective-permute-start(f32[32,128]{1,0:T(8,128)S(1)} %get-tuple-element.64.taps_ref), channel_id=1, source_target_pairs={{0,1},{1,0},{2,3},{3,2},{4,5},{5,4},{6,7},{7,6},{8,9},{9,8},{10,11... | collective-permute-start | bytes 49160 | tf_op jit(solution)/shard_map/ppermute | solution.py:429

commit v9 on v8

--- a/solution.py
+++ b/solution.py
@@ -222,6 +222,7 @@
     v_ref,
     halo_ref,
     w_ref,
+    after_ref,
     out_ref,
     head_ref,
     done_ref,
@@ -474,15 +475,6 @@
         [q_keep, q_recv],
     )
     q_turned = turn(q_sent.reshape(chips, depth, DH), groups[0])
-    qg_own, qg_send = call(
-        split_kernel,
-        (pair, pair),
-        core,
-        [queries, grad_out, added],
-        [dma((2, 2))],
-        [ANY, ANY, VMEM],
-    )
-    qg_recv = swap(qg_send)
     tail = call(tail_kernel, shape((EDGE * HALF, DH)), core, [kv_own, kv_recv])
     k, v, edge = call(
         gather_key_kernel,
@@ -491,6 +483,21 @@
         [kv_own, kv_recv],
     )
     halo = shifted(tail, 2)
+    c, k_state = call(
+        conv_kernel,
+        (far_block, shape((HALF, DH, DH), F32)),
+        core,
+        [k, v, conv_weight],
+    )
+    qg_own, qg_send = call(
+        split_kernel,
+        (pair, pair),
+        core,
+        [queries, grad_out, k_state],
+        [dma((2, 2))],
+        [ANY, ANY, VMEM],
+    )
+    qg_recv = swap(qg_send)
     q, g, q_far = call(
         gather_query_kernel,
         (block, block, far_block),
@@ -499,17 +506,11 @@
         [dma(())],
         made=(VMEM, VMEM, ANY),
     )
-    c, k_state = call(
-        conv_kernel,
-        (far_block, shape((HALF, DH, DH), F32)),
-        core,
-        [k, v, conv_weight],
-    )
     both, c_head, turned = call(
         functools.partial(turn_kernel, turns=turns),
         (shape((chips, 2, depth, DH)), edges, flag),
         core,
-        [q_turned, k_state, k, v, halo, conv_weight],
+        [q_turned, k_state, k, v, halo, conv_weight, qg_own],
     )
     both = turn(both, groups[1])
     gc, taps, wide = call(

time: 56.9 us -> 56.8 us (level)
  waiting for transfers between devices: 2.5 us -> 1.33 us
  starting transfers between devices: 33.5 us -> 34.6 us
    all_to_all x3, waiting for transfers between devices: 2.04 us -> 0.81 us  [turn(): lax.all_to_all(value, AXES, 0, 0, axis_index_groups=groups, tiled=True)]
    all_to_all x3, starting transfers between devices: 21.5 us -> 22.6 us  [turn(): lax.all_to_all(value, AXES, 0, 0, axis_index_groups=groups, tiled=True)]
  transfers between devices with their start and end apart: 11 -> 11, of which waited for: 3 -> 4; matrix products, arithmetic and copies ran while one was open for 0% -> 0% of each run, Pallas kernels for 26% -> 26%
where the time goes in v9:
time: 56.8 us; the launch traced here: 55.9 us
  starting transfers between devices  34.6 us (61%)
  Pallas kernels  19.2 us (34%)
  waiting for transfers between devices  1.33 us (2%)
  between operations  0.75 us (1%)
    all_to_all x3, starting transfers between devices, turn(): lax.all_to_all(value, AXES, 0, 0, axis_index_groups=groups, tiled=True)  22.6 us
    pallas_call x15, Pallas kernels, call(): pl.pallas_call(kernel, out_shape=outs, in_specs=[SMEM] + (given or [VMEM]...  19.2 us
    ppermute x6, starting transfers between devices, swap(): return lax.ppermute(value, AXES, [(d, d ^ 1) for d in range(count)])  8.51 us
    ppermute x2, starting transfers between devices, shifted(): return lax.ppermute(value, AXES, pairs)  3.47 us
  transfers between devices with their start and end apart: 11, of which 4 were waited for; matrix products, arithmetic and copies ran while one was open for 0% of the time, Pallas kernels for 26%

profile of v9, /device:TPU:1, one launch (start us, length us, event | category | flops | bytes accessed | tf_op | source)
XLA Modules:
  0.0 55.9 jit_solution(7287160792834895210)
XLA Ops:
  0.6 1.7 %shard_map.84 = (bf16[8,128,128]{2,1,0:T(8,128)(2,1)S(1)}, bf16[8,128,128]{2,1,0:T(8,128)(2,1)S(1)}) custom-call(s32[1]{0:T(128)} %bitcast.core_ref, bf16[128,2048]{1,0:T(8,128)(2,1)} %a_ref.1, bf16[128,2048]{1,0:T(8,128)(2,1)} %b_ref.1), custom_call_target="tpu_custom_call" | custom-call | tf_op jit(solution)/shard_map/pallas_call | solution.py:40
  2.3 0.1 collective-permute-start
  2.5 1.3 %shard_map.86 = (bf16[2,144,1024]{2,1,0:T(8,128)(2,1)S(1)}, bf16[2,144,1024]{2,1,0:T(8,128)(2,1)S(1)}) custom-call(s32[1]{0:T(128)} %bitcast.core_ref, bf16[128,2048]{1,0:T(8,128)(2,1)} %k_ref.1, bf16[128,2048]{1,0:T(8,128)(2,1)} %v_ref.1, bf16[128,2048]{1,0:T(8,128)(2,1)} %a_ref.1, bf16[128,2048]{1,0:T(8,128)(2,1)} %b_ref.1, ...), custom_call_target="tpu_custom_call" | custom-call | tf_op jit(solution)/shard_map/pallas_call | solution.py:40
  3.8 0.5 collective-permute-start.1
  4.3 0.0 collective-permute-done.recv_ref
  4.3 0.8 %shard_map.85 = (bf16[8,128,128]{2,1,0:T(8,128)(2,1)}, f32[8,128]{1,0:T(8,128)}) custom-call(s32[1]{0:T(128)} %bitcast.core_ref, bf16[8,128,128]{2,1,0:T(8,128)(2,1)S(1)} %get-tuple-element.38.keep_ref.after_ref, bf16[8,128,128]{2,1,0:T(8,128)(2,1)S(1)} %collective-permute-done.recv_ref), custom_call_target="tpu_custom_call" | custom-call | tf_op jit(solution)/shard_map/pallas_call | solution.py:40
  5.1 7.8 %all-to-all-start = ((bf16[16,64,128]{2,1,0:T(8,128)(2,1)}), bf16[16,64,128]{2,1,0:T(8,128)(2,1)S(1)}, u32[]{:S(2)}, u32[]{:S(2)}) async-start(bf16[16,64,128]{2,1,0:T(8,128)(2,1)} %bitcast.1), calls=%async_computation | async-start | bytes 524288 | tf_op jit(solution)/shard_map/all_to_all | solution.py:437
  12.9 0.0 copy-start
  12.9 2.2 %collective-permute-start.2 = (bf16[32,128]{1,0:T(8,128)(2,1)S(1)}, bf16[32,128]{1,0:T(8,128)(2,1)S(1)}, u32[]{:S(2)}, u32[]{:S(2)}) collective-permute-start(bf16[32,128]{1,0:T(8,128)(2,1)S(1)} %shard_map.89), channel_id=1, source_target_pairs={{0,2},{1,3},{2,4},{3,5},{4,6},{5,7},{6,8},{7,9},{8,10},{9,11},{10,... | collective-permute-start | bytes 24584 | tf_op jit(solution)/shard_map/ppermute | solution.py:434
  15.1 0.5 shard_map.87
  15.6 0.0 copy-done
  15.6 1.5 %shard_map.88 = (bf16[256,1024]{1,0:T(8,128)(2,1)}, f32[8,128,128]{2,1,0:T(8,128)S(1)}) custom-call(s32[1]{0:T(128)} %bitcast.core_ref, bf16[256,1024]{1,0:T(8,128)(2,1)S(1)} %get-tuple-element.43.k_ref, bf16[256,1024]{1,0:T(8,128)(2,1)S(1)} %get-tuple-element.44.v_ref, f32[4,2048]{1,0:T(4,128)S(1)} %copy-done), custom_call_target="tpu_custom_call" | custom-call | tf_op jit(solution)/shard_map/pallas_call | solution.py:40
  17.0 1.2 %shard_map.90 = (bf16[2,128,1024]{2,1,0:T(8,128)(2,1)S(1)}, bf16[2,128,1024]{2,1,0:T(8,128)(2,1)S(1)}) custom-call(s32[1]{0:T(128)} %bitcast.core_ref, bf16[128,2048]{1,0:T(8,128)(2,1)} %a_ref.1, bf16[128,2048]{1,0:T(8,128)(2,1)} %b_ref.1, f32[8,128,128]{2,1,0:T(8,128)S(1)} %get-tuple-element.45.after_ref.state_ref), custom_call_target="tpu_custom_call" | custom-call | tf_op jit(solution)/shard_map/pallas_call | solution.py:40
  18.3 0.8 %all-to-all-done.q_ref = bf16[16,64,128]{2,1,0:T(8,128)(2,1)S(1)} async-done(((bf16[16,64,128]{2,1,0:T(8,128)(2,1)}), bf16[16,64,128]{2,1,0:T(8,128)(2,1)S(1)}, u32[]{:S(2)}, u32[]{:S(2)}) %all-to-all-start) | async-done | bytes 262176 | tf_op jit(solution)/shard_map/all_to_all | solution.py:437
  19.1 1.1 %shard_map.91 = (bf16[16,2,64,128]{3,2,1,0:T(8,128)(2,1)}, bf16[16,1024]{1,0:T(8,128)(2,1)S(1)}, f32[8,128]{1,0:T(8,128)}) custom-call(s32[1]{0:T(128)} %bitcast.core_ref, bf16[16,64,128]{2,1,0:T(8,128)(2,1)S(1)} %all-to-all-done.q_ref, f32[8,128,128]{2,1,0:T(8,128)S(1)} %get-tuple-element.45.after_ref.state_ref, ...), custom_call_target="tpu_custom_call" | custom-call | tf_op jit(solution)/shard_map/pallas_call | solution.py:40
  20.1 6.6 %all-to-all-start.1 = ((bf16[16,2,64,128]{3,2,1,0:T(8,128)(2,1)}), bf16[16,2,64,128]{3,2,1,0:T(8,128)(2,1)S(1)}, u32[]{:S(2)}, u32[]{:S(2)}) async-start(bf16[16,2,64,128]{3,2,1,0:T(8,128)(2,1)} %get-tuple-element.47), calls=%async_computation.1 | async-start | bytes 1048576 | tf_op jit(solution)/shard_map/all_to_all | solution.py:437
  26.7 2.6 %collective-permute-start.3 = (bf16[2,128,1024]{2,1,0:T(8,128)(2,1)S(1)}, bf16[2,128,1024]{2,1,0:T(8,128)(2,1)S(1)}, u32[]{:S(2)}, u32[]{:S(2)}) collective-permute-start(bf16[2,128,1024]{2,1,0:T(8,128)(2,1)S(1)} %get-tuple-element.48), channel_id=1, source_target_pairs={{0,1},{1,0},{2,3},{3,2},{4,5},{5,4},{6,7},{7,6},{8,9},{9,8},{10,11... | collective-permute-start | bytes 1572872 | tf_op jit(solution)/shard_map/ppermute | solution.py:430
  29.3 1.3 %collective-permute-start.4 = (bf16[64,128]{1,0:T(8,128)(2,1)S(1)}, bf16[64,128]{1,0:T(8,128)(2,1)S(1)}, u32[]{:S(2)}, u32[]{:S(2)}) collective-permute-start(bf16[64,128]{1,0:T(8,128)(2,1)S(1)} %get-tuple-element.53), channel_id=1, source_target_pairs={{2,0},{3,1},{4,2},{5,3},{6,4},{7,5},{8,6},{9,7},{10,8},{11,9},{12,... | collective-permute-start | bytes 49160 | tf_op jit(solution)/shard_map/ppermute | solution.py:434
  30.6 0.2 collective-permute-done.3.recv_ref
  30.8 0.9 %shard_map.92 = (bf16[256,1024]{1,0:T(8,128)(2,1)S(1)}, bf16[256,1024]{1,0:T(8,128)(2,1)S(1)}, bf16[256,1024]{1,0:T(8,128)(2,1)}) custom-call(s32[1]{0:T(128)} %bitcast.core_ref, bf16[2,128,1024]{2,1,0:T(8,128)(2,1)S(1)} %get-tuple-element.46.after_ref.own_ref, bf16[2,128,1024]{2,1,0:T(8,128)(2,1)S(1)} %collective-permute-done.3.recv_ref), custom_call_target="tpu_custom_call" | custom-call | tf_op jit(solution)/shard_map/pallas_call | solution.py:40
  31.7 2.5 %shard_map.93 = (bf16[256,1024]{1,0:T(8,128)(2,1)}, f32[32,128]{1,0:T(8,128)S(1)}, bf16[8,4,128,128]{3,2,1,0:T(8,128)(2,1)S(1)}) custom-call(s32[1]{0:T(128)} %bitcast.core_ref, bf16[256,1024]{1,0:T(8,128)(2,1)S(1)} %get-tuple-element.49.q_ref, bf16[256,1024]{1,0:T(8,128)(2,1)S(1)} %get-tuple-element.50.g_ref, ...), custom_call_target="tpu_custom_call" | custom-call | tf_op jit(solution)/shard_map/pallas_call | solution.py:40
  34.2 0.1 collective-permute-done.4.edge_ref
  34.2 1.0 %shard_map.94 = (bf16[16,96,128]{2,1,0:T(8,128)(2,1)}, f32[8,128]{1,0:T(8,128)S(1)}) custom-call(s32[1]{0:T(128)} %bitcast.core_ref, bf16[16,2,64,128]{3,2,1,0:T(8,128)(2,1)S(1)} %all-to-all-done.1.chip_ref, bf16[8,4,128,128]{3,2,1,0:T(8,128)(2,1)S(1)} %get-tuple-element.51.wide_ref, f32[32,128]{1,0:T(8,128)S(1)} %get-tuple-element.52.near_ref, ...), custom_call_target="tpu_custom_call" | custom-call | tf_op jit(solution)/shard_map/pallas_call | solution.py:40
  35.3 8.3 %all-to-all-start.2 = ((bf16[16,96,128]{2,1,0:T(8,128)(2,1)}), bf16[16,96,128]{2,1,0:T(8,128)(2,1)S(1)}, u32[]{:S(2)}, u32[]{:S(2)}) async-start(bf16[16,96,128]{2,1,0:T(8,128)(2,1)} %get-tuple-element.54), calls=%async_computation.2 | async-start | bytes 786432 | tf_op jit(solution)/shard_map/all_to_all | solution.py:437
  43.5 4.9 %shard_map.95 = (bf16[128,2048]{1,0:T(8,128)(2,1)}, bf16[128,2048]{1,0:T(8,128)(2,1)}, bf16[2,128,1024]{2,1,0:T(8,128)(2,1)S(1)}, bf16[256,1024]{1,0:T(8,128)(2,1)S(1)}) custom-call(s32[1]{0:T(128)} %bitcast.core_ref, bf16[16,2,64,128]{3,2,1,0:T(8,128)(2,1)S(1)} %all-to-all-done.1.chip_ref, bf16[256,1024]{1,0:T(8,128)(2,1)S(1)} %get-tuple-element.43.k_ref, ...), custom_call_target="tpu_custom_call" | custom-call | tf_op jit(solution)/shard_map/pallas_call | solution.py:40
  48.4 3.9 %collective-permute-start.7 = (bf16[2,128,1024]{2,1,0:T(8,128)(2,1)S(1)}, bf16[2,128,1024]{2,1,0:T(8,128)(2,1)S(1)}, u32[]{:S(2)}, u32[]{:S(2)}) collective-permute-start(bf16[2,128,1024]{2,1,0:T(8,128)(2,1)S(1)} %get-tuple-element.63), channel_id=1, source_target_pairs={{0,1},{1,0},{2,3},{3,2},{4,5},{5,4},{6,7},{7,6},{8,9},{9,8},{10,11... | collective-permute-start | bytes 1572872 | tf_op jit(solution)/shard_map/ppermute | solution.py:430
  52.3 0.4 shard_map.96
  52.6 1.4 %collective-permute-start.5 = (bf16[128,1024]{1,0:T(8,128)(2,1)S(1)}, bf16[128,1024]{1,0:T(8,128)(2,1)S(1)}, u32[]{:S(2)}, u32[]{:S(2)}) collective-permute-start(bf16[128,1024]{1,0:T(8,128)(2,1)S(1)} %get-tuple-element.61), channel_id=1, source_target_pairs={{0,1},{1,0},{2,3},{3,2},{4,5},{5,4},{6,7},{7,6},{8,9},{9,8},{10,11... | collective-permute-start | bytes 786440 | tf_op jit(solution)/shard_map/ppermute | solution.py:430
  54.0 0.1 collective-permute-start.6
  54.1 0.9 %shard_map.97 = (bf16[128,2048]{1,0:T(8,128)(2,1)}, bf16[128,2048]{1,0:T(8,128)(2,1)}, bf16[128,2048]{1,0:T(8,128)(2,1)}) custom-call(s32[1]{0:T(128)} %bitcast.core_ref, bf16[2,128,1024]{2,1,0:T(8,128)(2,1)S(1)} %collective-permute-done.7.recv_ref, bf16[128,1024]{1,0:T(8,128)(2,1)S(1)} %get-tuple-element.64.own_ref, ...), custom_call_target="tpu_custom_call", output_to_operand_aliasing={{0}: (3, {}), {1}: (4, {})} | custom-call | tf_op jit(solution)/shard_map/pallas_call | solution.py:40
  55.0 0.2 collective-permute-done.6.far_ref
  55.2 0.7 %shard_map.98 = (bf16[128,2048]{1,0:T(8,128)(2,1)}, f32[4,2048]{1,0:T(4,128)}) custom-call(s32[1]{0:T(128)} %bitcast.core_ref, bf16[128,1024]{1,0:T(8,128)(2,1)S(1)} %collective-permute-done.5.recv_ref, f32[32,128]{1,0:T(8,128)S(1)} %get-tuple-element.62.taps_ref, f32[32,128]{1,0:T(8,128)S(1)} %collective-permute-done.6.far_ref, ...), custom_call_target="tpu_custom_call", output_to_operand_aliasing={{0}: (4, {})} | custom-call | tf_op jit(solution)/shard_map/pallas_call | solution.py:40
  (7 shorter events, 0.0 us)
Async XLA Ops:
  2.3 2.0 %collective-permute-start = (bf16[8,128,128]{2,1,0:T(8,128)(2,1)S(1)}, bf16[8,128,128]{2,1,0:T(8,128)(2,1)S(1)}, u32[]{:S(2)}, u32[]{:S(2)}) collective-permute-start(bf16[8,128,128]{2,1,0:T(8,128)(2,1)S(1)} %get-tuple-element.39), channel_id=1, source_target_pairs={{0,1},{1,0},{2,3},{3,2},{4,5},{5,4},{6,7},{7,6},{8,9},{9,8},{10,11... | collective-permute-start | bytes 786440 | tf_op jit(solution)/shard_map/ppermute | solution.py:430
  3.8 9.1 %collective-permute-start.1 = (bf16[2,144,1024]{2,1,0:T(8,128)(2,1)S(1)}, bf16[2,144,1024]{2,1,0:T(8,128)(2,1)S(1)}, u32[]{:S(2)}, u32[]{:S(2)}) collective-permute-start(bf16[2,144,1024]{2,1,0:T(8,128)(2,1)S(1)} %get-tuple-element.42), channel_id=1, source_target_pairs={{0,1},{1,0},{2,3},{3,2},{4,5},{5,4},{6,7},{7,6},{8,9},{9,8},{10,11... | collective-permute-start | bytes 1769480 | tf_op jit(solution)/shard_map/ppermute | solution.py:430
  5.1 14.0 %all-to-all-start = ((bf16[16,64,128]{2,1,0:T(8,128)(2,1)}), bf16[16,64,128]{2,1,0:T(8,128)(2,1)S(1)}, u32[]{:S(2)}, u32[]{:S(2)}) async-start(bf16[16,64,128]{2,1,0:T(8,128)(2,1)} %bitcast.1), calls=%async_computation | async-start | bytes 524288 | tf_op jit(solution)/shard_map/all_to_all | solution.py:437
  12.9 2.7 %copy-start = (f32[4,2048]{1,0:T(4,128)S(1)}, f32[4,2048]{1,0:T(4,128)}, u32[]{:S(2)}) copy-start(f32[4,2048]{1,0:T(4,128)} %w_ref.5) | copy-start | bytes 98308
  12.9 5.3 %collective-permute-start.2 = (bf16[32,128]{1,0:T(8,128)(2,1)S(1)}, bf16[32,128]{1,0:T(8,128)(2,1)S(1)}, u32[]{:S(2)}, u32[]{:S(2)}) collective-permute-start(bf16[32,128]{1,0:T(8,128)(2,1)S(1)} %shard_map.89), channel_id=1, source_target_pairs={{0,2},{1,3},{2,4},{3,5},{4,6},{5,7},{6,8},{7,9},{8,10},{9,11},{10,... | collective-permute-start | bytes 24584 | tf_op jit(solution)/shard_map/ppermute | solution.py:434
  20.1 14.1 %all-to-all-start.1 = ((bf16[16,2,64,128]{3,2,1,0:T(8,128)(2,1)}), bf16[16,2,64,128]{3,2,1,0:T(8,128)(2,1)S(1)}, u32[]{:S(2)}, u32[]{:S(2)}) async-start(bf16[16,2,64,128]{3,2,1,0:T(8,128)(2,1)} %get-tuple-element.47), calls=%async_computation.1 | async-start | bytes 1048576 | tf_op jit(solution)/shard_map/all_to_all | solution.py:437
  26.7 4.1 %collective-permute-start.3 = (bf16[2,128,1024]{2,1,0:T(8,128)(2,1)S(1)}, bf16[2,128,1024]{2,1,0:T(8,128)(2,1)S(1)}, u32[]{:S(2)}, u32[]{:S(2)}) collective-permute-start(bf16[2,128,1024]{2,1,0:T(8,128)(2,1)S(1)} %get-tuple-element.48), channel_id=1, source_target_pairs={{0,1},{1,0},{2,3},{3,2},{4,5},{5,4},{6,7},{7,6},{8,9},{9,8},{10,11... | collective-permute-start | bytes 1572872 | tf_op jit(solution)/shard_map/ppermute | solution.py:430
  29.3 4.9 %collective-permute-start.4 = (bf16[64,128]{1,0:T(8,128)(2,1)S(1)}, bf16[64,128]{1,0:T(8,128)(2,1)S(1)}, u32[]{:S(2)}, u32[]{:S(2)}) collective-permute-start(bf16[64,128]{1,0:T(8,128)(2,1)S(1)} %get-tuple-element.53), channel_id=1, source_target_pairs={{2,0},{3,1},{4,2},{5,3},{6,4},{7,5},{8,6},{9,7},{10,8},{11,9},{12,... | collective-permute-start | bytes 49160 | tf_op jit(solution)/shard_map/ppermute | solution.py:434
  35.3 17.0 %all-to-all-start.2 = ((bf16[16,96,128]{2,1,0:T(8,128)(2,1)}), bf16[16,96,128]{2,1,0:T(8,128)(2,1)S(1)}, u32[]{:S(2)}, u32[]{:S(2)}) async-start(bf16[16,96,128]{2,1,0:T(8,128)(2,1)} %get-tuple-element.54), calls=%async_computation.2 | async-start | bytes 786432 | tf_op jit(solution)/shard_map/all_to_all | solution.py:437
  48.4 5.7 %collective-permute-start.7 = (bf16[2,128,1024]{2,1,0:T(8,128)(2,1)S(1)}, bf16[2,128,1024]{2,1,0:T(8,128)(2,1)S(1)}, u32[]{:S(2)}, u32[]{:S(2)}) collective-permute-start(bf16[2,128,1024]{2,1,0:T(8,128)(2,1)S(1)} %get-tuple-element.63), channel_id=1, source_target_pairs={{0,1},{1,0},{2,3},{3,2},{4,5},{5,4},{6,7},{7,6},{8,9},{9,8},{10,11... | collective-permute-start | bytes 1572872 | tf_op jit(solution)/shard_map/ppermute | solution.py:430
  52.6 2.6 %collective-permute-start.5 = (bf16[128,1024]{1,0:T(8,128)(2,1)S(1)}, bf16[128,1024]{1,0:T(8,128)(2,1)S(1)}, u32[]{:S(2)}, u32[]{:S(2)}) collective-permute-start(bf16[128,1024]{1,0:T(8,128)(2,1)S(1)} %get-tuple-element.61), channel_id=1, source_target_pairs={{0,1},{1,0},{2,3},{3,2},{4,5},{5,4},{6,7},{7,6},{8,9},{9,8},{10,11... | collective-permute-start | bytes 786440 | tf_op jit(solution)/shard_map/ppermute | solution.py:430
  54.0 1.2 %collective-permute-start.6 = (f32[32,128]{1,0:T(8,128)S(1)}, f32[32,128]{1,0:T(8,128)S(1)}, u32[]{:S(2)}, u32[]{:S(2)}) collective-permute-start(f32[32,128]{1,0:T(8,128)S(1)} %get-tuple-element.62.taps_ref), channel_id=1, source_target_pairs={{0,1},{1,0},{2,3},{3,2},{4,5},{5,4},{6,7},{7,6},{8,9},{9,8},{10,11... | collective-permute-start | bytes 49160 | tf_op jit(solution)/shard_map/ppermute | solution.py:430

commit v10 on v9

--- a/solution.py
+++ b/solution.py
@@ -416,8 +416,9 @@
     spread = sorted(range(line), key=lambda z: (abs(2 * z + 1 - line), -z))
     mixed = [z for n in range(half) for z in (half + n, n)]
     lists = [
-        [r * line + z for r in reversed(range(lines)) for z in along]
-        for along in (split, spread, mixed)
+        [r * line + z for z in split for r in reversed(range(lines))],
+        [r * line + z for r in reversed(range(lines)) for z in spread],
+        [r * line + z for r in reversed(range(lines)) for z in mixed],
     ]
     groups = [[[2 * p + c for p in each] for c in range(2)] for each in lists]
     spots = [[each.index(p) for p in range(chips)] for each in lists]

time: 56.8 us -> 56.8 us (level)
  no operation moved by 1% of the time
where the time goes in v10:
time: 56.8 us; the launch traced here: 55.9 us
  starting transfers between devices  34.6 us (61%)
  Pallas kernels  19.2 us (34%)
  waiting for transfers between devices  1.36 us (2%)
  between operations  0.76 us (1%)
    all_to_all x3, starting transfers between devices, turn(): lax.all_to_all(value, AXES, 0, 0, axis_index_groups=groups, tiled=True)  22.5 us
    pallas_call x15, Pallas kernels, call(): pl.pallas_call(kernel, out_shape=outs, in_specs=[SMEM] + (given or [VMEM]...  19.2 us
    ppermute x6, starting transfers between devices, swap(): return lax.ppermute(value, AXES, [(d, d ^ 1) for d in range(count)])  8.55 us
    ppermute x2, starting transfers between devices, shifted(): return lax.ppermute(value, AXES, pairs)  3.47 us
  transfers between devices with their start and end apart: 11, of which 4 were waited for; matrix products, arithmetic and copies ran while one was open for 0% of the time, Pallas kernels for 26%

profile of v10, /device:TPU:1, one launch (start us, length us, event | category | flops | bytes accessed | tf_op | source)
XLA Modules:
  0.0 55.9 jit_solution(16728912018275803687)
XLA Ops:
  0.6 1.7 %shard_map.84 = (bf16[8,128,128]{2,1,0:T(8,128)(2,1)S(1)}, bf16[8,128,128]{2,1,0:T(8,128)(2,1)S(1)}) custom-call(s32[1]{0:T(128)} %bitcast.core_ref, bf16[128,2048]{1,0:T(8,128)(2,1)} %a_ref.1, bf16[128,2048]{1,0:T(8,128)(2,1)} %b_ref.1), custom_call_target="tpu_custom_call" | custom-call | tf_op jit(solution)/shard_map/pallas_call | solution.py:40
  2.3 0.1 collective-permute-start
  2.5 1.3 %shard_map.86 = (bf16[2,144,1024]{2,1,0:T(8,128)(2,1)S(1)}, bf16[2,144,1024]{2,1,0:T(8,128)(2,1)S(1)}) custom-call(s32[1]{0:T(128)} %bitcast.core_ref, bf16[128,2048]{1,0:T(8,128)(2,1)} %k_ref.1, bf16[128,2048]{1,0:T(8,128)(2,1)} %v_ref.1, bf16[128,2048]{1,0:T(8,128)(2,1)} %a_ref.1, bf16[128,2048]{1,0:T(8,128)(2,1)} %b_ref.1, ...), custom_call_target="tpu_custom_call" | custom-call | tf_op jit(solution)/shard_map/pallas_call | solution.py:40
  3.8 0.5 collective-permute-start.1
  4.3 0.0 collective-permute-done.recv_ref
  4.3 0.8 %shard_map.85 = (bf16[8,128,128]{2,1,0:T(8,128)(2,1)}, f32[8,128]{1,0:T(8,128)}) custom-call(s32[1]{0:T(128)} %bitcast.core_ref, bf16[8,128,128]{2,1,0:T(8,128)(2,1)S(1)} %get-tuple-element.38.keep_ref.after_ref, bf16[8,128,128]{2,1,0:T(8,128)(2,1)S(1)} %collective-permute-done.recv_ref), custom_call_target="tpu_custom_call" | custom-call | tf_op jit(solution)/shard_map/pallas_call | solution.py:40
  5.1 7.8 %all-to-all-start = ((bf16[16,64,128]{2,1,0:T(8,128)(2,1)}), bf16[16,64,128]{2,1,0:T(8,128)(2,1)S(1)}, u32[]{:S(2)}, u32[]{:S(2)}) async-start(bf16[16,64,128]{2,1,0:T(8,128)(2,1)} %bitcast.1), calls=%async_computation | async-start | bytes 524288 | tf_op jit(solution)/shard_map/all_to_all | solution.py:438
  12.9 0.0 collective-permute-done.1.recv_ref
  12.9 0.0 copy-start
  12.9 2.2 %collective-permute-start.2 = (bf16[32,128]{1,0:T(8,128)(2,1)S(1)}, bf16[32,128]{1,0:T(8,128)(2,1)S(1)}, u32[]{:S(2)}, u32[]{:S(2)}) collective-permute-start(bf16[32,128]{1,0:T(8,128)(2,1)S(1)} %shard_map.89), channel_id=1, source_target_pairs={{0,2},{1,3},{2,4},{3,5},{4,6},{5,7},{6,8},{7,9},{8,10},{9,11},{10,... | collective-permute-start | bytes 24584 | tf_op jit(solution)/shard_map/ppermute | solution.py:435
  15.1 0.5 shard_map.87
  15.6 1.5 %shard_map.88 = (bf16[256,1024]{1,0:T(8,128)(2,1)}, f32[8,128,128]{2,1,0:T(8,128)S(1)}) custom-call(s32[1]{0:T(128)} %bitcast.core_ref, bf16[256,1024]{1,0:T(8,128)(2,1)S(1)} %get-tuple-element.43.k_ref, bf16[256,1024]{1,0:T(8,128)(2,1)S(1)} %get-tuple-element.44.v_ref, f32[4,2048]{1,0:T(4,128)S(1)} %copy-done), custom_call_target="tpu_custom_call" | custom-call | tf_op jit(solution)/shard_map/pallas_call | solution.py:40
  17.0 1.2 %shard_map.90 = (bf16[2,128,1024]{2,1,0:T(8,128)(2,1)S(1)}, bf16[2,128,1024]{2,1,0:T(8,128)(2,1)S(1)}) custom-call(s32[1]{0:T(128)} %bitcast.core_ref, bf16[128,2048]{1,0:T(8,128)(2,1)} %a_ref.1, bf16[128,2048]{1,0:T(8,128)(2,1)} %b_ref.1, f32[8,128,128]{2,1,0:T(8,128)S(1)} %get-tuple-element.45.after_ref.state_ref), custom_call_target="tpu_custom_call" | custom-call | tf_op jit(solution)/shard_map/pallas_call | solution.py:40
  18.3 0.8 %all-to-all-done.q_ref = bf16[16,64,128]{2,1,0:T(8,128)(2,1)S(1)} async-done(((bf16[16,64,128]{2,1,0:T(8,128)(2,1)}), bf16[16,64,128]{2,1,0:T(8,128)(2,1)S(1)}, u32[]{:S(2)}, u32[]{:S(2)}) %all-to-all-start) | async-done | bytes 262176 | tf_op jit(solution)/shard_map/all_to_all | solution.py:438
  19.1 1.1 %shard_map.91 = (bf16[16,2,64,128]{3,2,1,0:T(8,128)(2,1)}, bf16[16,1024]{1,0:T(8,128)(2,1)S(1)}, f32[8,128]{1,0:T(8,128)}) custom-call(s32[1]{0:T(128)} %bitcast.core_ref, bf16[16,64,128]{2,1,0:T(8,128)(2,1)S(1)} %all-to-all-done.q_ref, f32[8,128,128]{2,1,0:T(8,128)S(1)} %get-tuple-element.45.after_ref.state_ref, ...), custom_call_target="tpu_custom_call" | custom-call | tf_op jit(solution)/shard_map/pallas_call | solution.py:40
  20.2 6.5 %all-to-all-start.1 = ((bf16[16,2,64,128]{3,2,1,0:T(8,128)(2,1)}), bf16[16,2,64,128]{3,2,1,0:T(8,128)(2,1)S(1)}, u32[]{:S(2)}, u32[]{:S(2)}) async-start(bf16[16,2,64,128]{3,2,1,0:T(8,128)(2,1)} %get-tuple-element.47), calls=%async_computation.1 | async-start | bytes 1048576 | tf_op jit(solution)/shard_map/all_to_all | solution.py:438
  26.7 2.6 %collective-permute-start.3 = (bf16[2,128,1024]{2,1,0:T(8,128)(2,1)S(1)}, bf16[2,128,1024]{2,1,0:T(8,128)(2,1)S(1)}, u32[]{:S(2)}, u32[]{:S(2)}) collective-permute-start(bf16[2,128,1024]{2,1,0:T(8,128)(2,1)S(1)} %get-tuple-element.48), channel_id=1, source_target_pairs={{0,1},{1,0},{2,3},{3,2},{4,5},{5,4},{6,7},{7,6},{8,9},{9,8},{10,11... | collective-permute-start | bytes 1572872 | tf_op jit(solution)/shard_map/ppermute | solution.py:431
  29.3 1.3 %collective-permute-start.4 = (bf16[64,128]{1,0:T(8,128)(2,1)S(1)}, bf16[64,128]{1,0:T(8,128)(2,1)S(1)}, u32[]{:S(2)}, u32[]{:S(2)}) collective-permute-start(bf16[64,128]{1,0:T(8,128)(2,1)S(1)} %get-tuple-element.53), channel_id=1, source_target_pairs={{2,0},{3,1},{4,2},{5,3},{6,4},{7,5},{8,6},{9,7},{10,8},{11,9},{12,... | collective-permute-start | bytes 49160 | tf_op jit(solution)/shard_map/ppermute | solution.py:435
  30.6 0.2 collective-permute-done.3.recv_ref
  30.8 0.9 %shard_map.92 = (bf16[256,1024]{1,0:T(8,128)(2,1)S(1)}, bf16[256,1024]{1,0:T(8,128)(2,1)S(1)}, bf16[256,1024]{1,0:T(8,128)(2,1)}) custom-call(s32[1]{0:T(128)} %bitcast.core_ref, bf16[2,128,1024]{2,1,0:T(8,128)(2,1)S(1)} %get-tuple-element.46.after_ref.own_ref, bf16[2,128,1024]{2,1,0:T(8,128)(2,1)S(1)} %collective-permute-done.3.recv_ref), custom_call_target="tpu_custom_call" | custom-call | tf_op jit(solution)/shard_map/pallas_call | solution.py:40
  31.7 2.5 %shard_map.93 = (bf16[256,1024]{1,0:T(8,128)(2,1)}, f32[32,128]{1,0:T(8,128)S(1)}, bf16[8,4,128,128]{3,2,1,0:T(8,128)(2,1)S(1)}) custom-call(s32[1]{0:T(128)} %bitcast.core_ref, bf16[256,1024]{1,0:T(8,128)(2,1)S(1)} %get-tuple-element.49.q_ref, bf16[256,1024]{1,0:T(8,128)(2,1)S(1)} %get-tuple-element.50.g_ref, ...), custom_call_target="tpu_custom_call" | custom-call | tf_op jit(solution)/shard_map/pallas_call | solution.py:40
  34.2 0.1 collective-permute-done.4.edge_ref
  34.2 1.0 %shard_map.94 = (bf16[16,96,128]{2,1,0:T(8,128)(2,1)}, f32[8,128]{1,0:T(8,128)S(1)}) custom-call(s32[1]{0:T(128)} %bitcast.core_ref, bf16[16,2,64,128]{3,2,1,0:T(8,128)(2,1)S(1)} %all-to-all-done.1.chip_ref, bf16[8,4,128,128]{3,2,1,0:T(8,128)(2,1)S(1)} %get-tuple-element.51.wide_ref, f32[32,128]{1,0:T(8,128)S(1)} %get-tuple-element.52.near_ref, ...), custom_call_target="tpu_custom_call" | custom-call | tf_op jit(solution)/shard_map/pallas_call | solution.py:40
  35.3 8.2 %all-to-all-start.2 = ((bf16[16,96,128]{2,1,0:T(8,128)(2,1)}), bf16[16,96,128]{2,1,0:T(8,128)(2,1)S(1)}, u32[]{:S(2)}, u32[]{:S(2)}) async-start(bf16[16,96,128]{2,1,0:T(8,128)(2,1)} %get-tuple-element.54), calls=%async_computation.2 | async-start | bytes 786432 | tf_op jit(solution)/shard_map/all_to_all | solution.py:438
  43.5 4.9 %shard_map.95 = (bf16[128,2048]{1,0:T(8,128)(2,1)}, bf16[128,2048]{1,0:T(8,128)(2,1)}, bf16[2,128,1024]{2,1,0:T(8,128)(2,1)S(1)}, bf16[256,1024]{1,0:T(8,128)(2,1)S(1)}) custom-call(s32[1]{0:T(128)} %bitcast.core_ref, bf16[16,2,64,128]{3,2,1,0:T(8,128)(2,1)S(1)} %all-to-all-done.1.chip_ref, bf16[256,1024]{1,0:T(8,128)(2,1)S(1)} %get-tuple-element.43.k_ref, ...), custom_call_target="tpu_custom_call" | custom-call | tf_op jit(solution)/shard_map/pallas_call | solution.py:40
  48.4 3.9 %collective-permute-start.7 = (bf16[2,128,1024]{2,1,0:T(8,128)(2,1)S(1)}, bf16[2,128,1024]{2,1,0:T(8,128)(2,1)S(1)}, u32[]{:S(2)}, u32[]{:S(2)}) collective-permute-start(bf16[2,128,1024]{2,1,0:T(8,128)(2,1)S(1)} %get-tuple-element.63), channel_id=1, source_target_pairs={{0,1},{1,0},{2,3},{3,2},{4,5},{5,4},{6,7},{7,6},{8,9},{9,8},{10,11... | collective-permute-start | bytes 1572872 | tf_op jit(solution)/shard_map/ppermute | solution.py:431
  52.2 0.4 shard_map.96
  52.6 1.4 %collective-permute-start.5 = (bf16[128,1024]{1,0:T(8,128)(2,1)S(1)}, bf16[128,1024]{1,0:T(8,128)(2,1)S(1)}, u32[]{:S(2)}, u32[]{:S(2)}) collective-permute-start(bf16[128,1024]{1,0:T(8,128)(2,1)S(1)} %get-tuple-element.61), channel_id=1, source_target_pairs={{0,1},{1,0},{2,3},{3,2},{4,5},{5,4},{6,7},{7,6},{8,9},{9,8},{10,11... | collective-permute-start | bytes 786440 | tf_op jit(solution)/shard_map/ppermute | solution.py:431
  54.0 0.1 collective-permute-start.6
  54.0 0.9 %shard_map.97 = (bf16[128,2048]{1,0:T(8,128)(2,1)}, bf16[128,2048]{1,0:T(8,128)(2,1)}, bf16[128,2048]{1,0:T(8,128)(2,1)}) custom-call(s32[1]{0:T(128)} %bitcast.core_ref, bf16[2,128,1024]{2,1,0:T(8,128)(2,1)S(1)} %collective-permute-done.7.recv_ref, bf16[128,1024]{1,0:T(8,128)(2,1)S(1)} %get-tuple-element.64.own_ref, ...), custom_call_target="tpu_custom_call", output_to_operand_aliasing={{0}: (3, {}), {1}: (4, {})} | custom-call | tf_op jit(solution)/shard_map/pallas_call | solution.py:40
  54.9 0.2 collective-permute-done.6.far_ref
  55.1 0.7 %shard_map.98 = (bf16[128,2048]{1,0:T(8,128)(2,1)}, f32[4,2048]{1,0:T(4,128)}) custom-call(s32[1]{0:T(128)} %bitcast.core_ref, bf16[128,1024]{1,0:T(8,128)(2,1)S(1)} %collective-permute-done.5.recv_ref, f32[32,128]{1,0:T(8,128)S(1)} %get-tuple-element.62.taps_ref, f32[32,128]{1,0:T(8,128)S(1)} %collective-permute-done.6.far_ref, ...), custom_call_target="tpu_custom_call", output_to_operand_aliasing={{0}: (4, {})} | custom-call | tf_op jit(solution)/shard_map/pallas_call | solution.py:40
  (7 shorter events, 0.0 us)
Async XLA Ops:
  2.3 2.0 %collective-permute-start = (bf16[8,128,128]{2,1,0:T(8,128)(2,1)S(1)}, bf16[8,128,128]{2,1,0:T(8,128)(2,1)S(1)}, u32[]{:S(2)}, u32[]{:S(2)}) collective-permute-start(bf16[8,128,128]{2,1,0:T(8,128)(2,1)S(1)} %get-tuple-element.39), channel_id=1, source_target_pairs={{0,1},{1,0},{2,3},{3,2},{4,5},{5,4},{6,7},{7,6},{8,9},{9,8},{10,11... | collective-permute-start | bytes 786440 | tf_op jit(solution)/shard_map/ppermute | solution.py:431
  3.8 9.1 %collective-permute-start.1 = (bf16[2,144,1024]{2,1,0:T(8,128)(2,1)S(1)}, bf16[2,144,1024]{2,1,0:T(8,128)(2,1)S(1)}, u32[]{:S(2)}, u32[]{:S(2)}) collective-permute-start(bf16[2,144,1024]{2,1,0:T(8,128)(2,1)S(1)} %get-tuple-element.42), channel_id=1, source_target_pairs={{0,1},{1,0},{2,3},{3,2},{4,5},{5,4},{6,7},{7,6},{8,9},{9,8},{10,11... | collective-permute-start | bytes 1769480 | tf_op jit(solution)/shard_map/ppermute | solution.py:431
  5.1 14.0 %all-to-all-start = ((bf16[16,64,128]{2,1,0:T(8,128)(2,1)}), bf16[16,64,128]{2,1,0:T(8,128)(2,1)S(1)}, u32[]{:S(2)}, u32[]{:S(2)}) async-start(bf16[16,64,128]{2,1,0:T(8,128)(2,1)} %bitcast.1), calls=%async_computation | async-start | bytes 524288 | tf_op jit(solution)/shard_map/all_to_all | solution.py:438
  12.9 2.7 %copy-start = (f32[4,2048]{1,0:T(4,128)S(1)}, f32[4,2048]{1,0:T(4,128)}, u32[]{:S(2)}) copy-start(f32[4,2048]{1,0:T(4,128)} %w_ref.5) | copy-start | bytes 98308
  12.9 5.3 %collective-permute-start.2 = (bf16[32,128]{1,0:T(8,128)(2,1)S(1)}, bf16[32,128]{1,0:T(8,128)(2,1)S(1)}, u32[]{:S(2)}, u32[]{:S(2)}) collective-permute-start(bf16[32,128]{1,0:T(8,128)(2,1)S(1)} %shard_map.89), channel_id=1, source_target_pairs={{0,2},{1,3},{2,4},{3,5},{4,6},{5,7},{6,8},{7,9},{8,10},{9,11},{10,... | collective-permute-start | bytes 24584 | tf_op jit(solution)/shard_map/ppermute | solution.py:435
  20.2 14.1 %all-to-all-start.1 = ((bf16[16,2,64,128]{3,2,1,0:T(8,128)(2,1)}), bf16[16,2,64,128]{3,2,1,0:T(8,128)(2,1)S(1)}, u32[]{:S(2)}, u32[]{:S(2)}) async-start(bf16[16,2,64,128]{3,2,1,0:T(8,128)(2,1)} %get-tuple-element.47), calls=%async_computation.1 | async-start | bytes 1048576 | tf_op jit(solution)/shard_map/all_to_all | solution.py:438
  26.7 4.1 %collective-permute-start.3 = (bf16[2,128,1024]{2,1,0:T(8,128)(2,1)S(1)}, bf16[2,128,1024]{2,1,0:T(8,128)(2,1)S(1)}, u32[]{:S(2)}, u32[]{:S(2)}) collective-permute-start(bf16[2,128,1024]{2,1,0:T(8,128)(2,1)S(1)} %get-tuple-element.48), channel_id=1, source_target_pairs={{0,1},{1,0},{2,3},{3,2},{4,5},{5,4},{6,7},{7,6},{8,9},{9,8},{10,11... | collective-permute-start | bytes 1572872 | tf_op jit(solution)/shard_map/ppermute | solution.py:431
  29.3 4.9 %collective-permute-start.4 = (bf16[64,128]{1,0:T(8,128)(2,1)S(1)}, bf16[64,128]{1,0:T(8,128)(2,1)S(1)}, u32[]{:S(2)}, u32[]{:S(2)}) collective-permute-start(bf16[64,128]{1,0:T(8,128)(2,1)S(1)} %get-tuple-element.53), channel_id=1, source_target_pairs={{2,0},{3,1},{4,2},{5,3},{6,4},{7,5},{8,6},{9,7},{10,8},{11,9},{12,... | collective-permute-start | bytes 49160 | tf_op jit(solution)/shard_map/ppermute | solution.py:435
  35.3 16.9 %all-to-all-start.2 = ((bf16[16,96,128]{2,1,0:T(8,128)(2,1)}), bf16[16,96,128]{2,1,0:T(8,128)(2,1)S(1)}, u32[]{:S(2)}, u32[]{:S(2)}) async-start(bf16[16,96,128]{2,1,0:T(8,128)(2,1)} %get-tuple-element.54), calls=%async_computation.2 | async-start | bytes 786432 | tf_op jit(solution)/shard_map/all_to_all | solution.py:438
  48.4 5.7 %collective-permute-start.7 = (bf16[2,128,1024]{2,1,0:T(8,128)(2,1)S(1)}, bf16[2,128,1024]{2,1,0:T(8,128)(2,1)S(1)}, u32[]{:S(2)}, u32[]{:S(2)}) collective-permute-start(bf16[2,128,1024]{2,1,0:T(8,128)(2,1)S(1)} %get-tuple-element.63), channel_id=1, source_target_pairs={{0,1},{1,0},{2,3},{3,2},{4,5},{5,4},{6,7},{7,6},{8,9},{9,8},{10,11... | collective-permute-start | bytes 1572872 | tf_op jit(solution)/shard_map/ppermute | solution.py:431
  52.6 2.6 %collective-permute-start.5 = (bf16[128,1024]{1,0:T(8,128)(2,1)S(1)}, bf16[128,1024]{1,0:T(8,128)(2,1)S(1)}, u32[]{:S(2)}, u32[]{:S(2)}) collective-permute-start(bf16[128,1024]{1,0:T(8,128)(2,1)S(1)} %get-tuple-element.61), channel_id=1, source_target_pairs={{0,1},{1,0},{2,3},{3,2},{4,5},{5,4},{6,7},{7,6},{8,9},{9,8},{10,11... | collective-permute-start | bytes 786440 | tf_op jit(solution)/shard_map/ppermute | solution.py:431
  54.0 1.2 %collective-permute-start.6 = (f32[32,128]{1,0:T(8,128)S(1)}, f32[32,128]{1,0:T(8,128)S(1)}, u32[]{:S(2)}, u32[]{:S(2)}) collective-permute-start(f32[32,128]{1,0:T(8,128)S(1)} %get-tuple-element.62.taps_ref), channel_id=1, source_target_pairs={{0,1},{1,0},{2,3},{3,2},{4,5},{5,4},{6,7},{7,6},{8,9},{9,8},{10,11... | collective-permute-start | bytes 49160 | tf_op jit(solution)/shard_map/ppermute | solution.py:431
